TPU v7x, 256 devices: a whole 4x4x8 slice. The times are simulated.
256 devices in a mesh: dp: 32 (over x, y, core), tensor: 8 (over z).
Axes of the slice: x: 4, y: 4, z: 8, core: 2. Of those that a mesh axis runs over, the one named last changes fastest.
Arguments:
- rotated_queries: bfloat16 [4096, 8192], P('dp', 'tensor'), may hold values from -5 to 5
- rotated_keys: bfloat16 [4096, 1024], P('dp', 'tensor'), may hold values from -5 to 5
- value_heads_packed: bfloat16 [4096, 1024], P('dp', 'tensor'), may hold values from -6 to 6
- out_weight: bfloat16 [8192, 4096], P('tensor'), may hold values from -0.0625 to 0.0625
- out_cotangent: bfloat16 [4096, 4096], P('dp', 'tensor'), may hold values from -6 to 6
- doc_ids: int32 [4096], P('dp'), may hold values from 0 to 15, never falling along the last dimension, each value on 1 to 2048 neighbouring positions
Outputs:
- projected: bfloat16 [4096, 4096], P('dp', 'tensor')
- query_grad: bfloat16 [4096, 8192], P('dp', 'tensor')
- key_state_gradient: bfloat16 [4096, 1024], P('dp', 'tensor')
- value_state_gradient: bfloat16 [4096, 1024], P('dp', 'tensor')
Inputs may be any that keep to these rules, and one draw needn't show every extreme that they name: doc_ids never falls along the tokens; each number names one run of 1 to 2048 tokens, and one run has exactly 2048.
All inputs are finite; a program needn't handle non-finite values.
Results may differ from a plain program's by a relative error of at most 0.034.
Values may be sent and summed in bfloat16 or wider, within the bound.
No kernel may reach another device: no remote copies, remote signals or barrier semaphores. Data moves between devices by JAX's collectives and lax.ppermute only.
A program may use at most 128 MiB of HBM per device.

v0:
```python
import math

import jax
import jax.numpy as jnp
from jax import lax
from jax.sharding import PartitionSpec as P

QUERY_HEAD_COUNT = 64
KEY_VALUE_HEADS = 8
HEAD_SIZE = 128
SPAN_MAX = 16


masked_score = -1e30


def from_behind(x, axis, by):
    size = lax.axis_size(axis)
    pairs = [(i, i + by) for i in range(size) if 0 <= i + by < size]
    return lax.ppermute(x, axis, pairs)


def block_scores(query_heads, key_blk, allowed, live_flag):
    score_scale = 1.0 / math.sqrt(key_blk.shape[-1])

    def block_compute(query_heads, key_blk, allowed):
        raw_scores = jnp.einsum(
            "cgtd,scd->cgts", query_heads, key_blk, preferred_element_type=jnp.float32
        )
        return jnp.where(allowed, raw_scores * score_scale, masked_score)

    def block_skipped(query_heads, key_blk, allowed):
        return jnp.full(query_heads.shape[:3] + (key_blk.shape[0],), masked_score, jnp.float32)

    return lax.cond(live_flag, block_compute, block_skipped, query_heads, key_blk, allowed)


def per_device(
    rotated_queries, rotated_keys, value_heads_packed, out_weight, out_cotangent, doc_ids
):
    row_count = rotated_queries.shape[0]
    kv_heads = rotated_keys.shape[1] // HEAD_SIZE
    kv_width = kv_heads * HEAD_SIZE
    query_group_width = QUERY_HEAD_COUNT // KEY_VALUE_HEADS
    spread = lax.axis_size("dp")
    reach_devs = min(SPAN_MAX, spread // 2)
    my_index = lax.axis_index("dp")
    score_scale = 1.0 / math.sqrt(HEAD_SIZE)
    query_heads = rotated_queries.reshape(
        row_count, kv_heads, query_group_width, HEAD_SIZE
    ).transpose(1, 2, 0, 3)
    key_rows = rotated_keys.reshape(row_count, kv_heads, HEAD_SIZE)
    value_rows = value_heads_packed.reshape(row_count, kv_heads, HEAD_SIZE)

    def relay_step(holding, unused):
        arrived = from_behind((holding[0], holding[1], holding[2]), "dp", 1)
        return (arrived, arrived)

    unused, trail = lax.scan(relay_step, (key_rows, value_rows, doc_ids), None, length=reach_devs)
    key_blocks = jnp.concatenate([key_rows[None], trail[0]], 0)
    value_blocks = jnp.concatenate([value_rows[None], trail[1]], 0)
    id_blocks = jnp.concatenate([doc_ids[None], trail[2]], 0)
    sources = my_index - jnp.arange(reach_devs + 1, dtype=jnp.int32)
    offsets = jnp.arange(row_count, dtype=jnp.int32)
    query_pos = my_index * row_count + offsets
    key_pos = sources[:, None] * row_count + offsets[None, :]
    allowed = (
        (doc_ids[None, :, None] == id_blocks[:, None, :])
        & (key_pos[:, None, :] <= query_pos[None, :, None])
        & (sources >= 0)[:, None, None]
    )
    live_flags = jnp.any(allowed, axis=(1, 2))

    def score_one(element):
        return block_scores(query_heads, element[0], element[1], element[2])

    scores = lax.map(score_one, (key_blocks, allowed, live_flags))
    row_peak = jnp.max(scores, axis=(0, 4))

    def accumulate(running, element):
        score_blk, value_blk, live_flag = element

        def accumulate_compute(running, score_blk, value_blk):
            weight = jnp.exp(score_blk - row_peak[..., None])
            mixed = jnp.einsum(
                "cgts,scd->cgtd",
                weight.astype(jnp.bfloat16),
                value_blk,
                preferred_element_type=jnp.float32,
            )
            return (running[0] + jnp.sum(weight, axis=-1), running[1] + mixed)

        def accumulate_skipped(running, score_blk, value_blk):
            return running

        return (
            lax.cond(
                live_flag, accumulate_compute, accumulate_skipped, running, score_blk, value_blk
            ),
            None,
        )

    zero_heads = jnp.zeros(query_heads.shape, jnp.float32)
    totals, unused = lax.scan(
        accumulate,
        (jnp.zeros(query_heads.shape[:3], jnp.float32), zero_heads),
        (scores, value_blocks, live_flags),
    )
    row_total, weighted = totals
    attended = (weighted / row_total[..., None]).astype(jnp.bfloat16)
    log_total = row_peak + jnp.log(row_total)
    attended_rows = attended.transpose(2, 0, 1, 3).reshape(row_count, -1)
    partial_out = jnp.dot(attended_rows, out_weight, preferred_element_type=jnp.float32)
    projected = lax.psum_scatter(
        partial_out.astype(jnp.bfloat16), "tensor", scatter_dimension=1, tiled=True
    )
    cotangent_all = lax.all_gather(out_cotangent, "tensor", axis=1, tiled=True)
    attended_gradient = lax.dot_general(
        cotangent_all, out_weight, (((1,), (1,)), ((), ())), preferred_element_type=jnp.float32
    ).astype(jnp.bfloat16)
    grad_heads = attended_gradient.reshape(
        row_count, kv_heads, query_group_width, HEAD_SIZE
    ).transpose(1, 2, 0, 3)
    row_delta = jnp.einsum(
        "cgtd,cgtd->cgt", grad_heads, attended, preferred_element_type=jnp.float32
    )

    def backward_step(query_sum, element):
        score_blk, key_blk, value_blk, live_flag = element

        def backward_compute(score_blk, key_blk, value_blk):
            probability = jnp.exp(score_blk - log_total[..., None])
            value_term = jnp.einsum(
                "cgts,cgtd->scd",
                probability.astype(jnp.bfloat16),
                grad_heads,
                preferred_element_type=jnp.float32,
            )
            grad_prob = jnp.einsum(
                "cgtd,scd->cgts", grad_heads, value_blk, preferred_element_type=jnp.float32
            )
            grad_score = (probability * (grad_prob - row_delta[..., None]) * score_scale).astype(
                jnp.bfloat16
            )
            query_term = jnp.einsum(
                "cgts,scd->cgtd", grad_score, key_blk, preferred_element_type=jnp.float32
            )
            key_term = jnp.einsum(
                "cgts,cgtd->scd", grad_score, query_heads, preferred_element_type=jnp.float32
            )
            return (query_term, key_term, value_term)

        def backward_skipped(score_blk, key_blk, value_blk):
            zero_rows = jnp.zeros(key_blk.shape, jnp.float32)
            return (jnp.zeros(query_heads.shape, jnp.float32), zero_rows, zero_rows)

        query_term, key_term, value_term = lax.cond(
            live_flag, backward_compute, backward_skipped, score_blk, key_blk, value_blk
        )
        return (query_sum + query_term, (key_term, value_term))

    query_sum, block_terms = lax.scan(
        backward_step, zero_heads, (scores, key_blocks, value_blocks, live_flags)
    )
    query_grad = query_sum.transpose(2, 0, 1, 3).reshape(row_count, -1).astype(jnp.bfloat16)
    key_terms = block_terms[0].reshape(reach_devs + 1, row_count, kv_width)
    value_terms = block_terms[1].reshape(reach_devs + 1, row_count, kv_width)

    def return_step(holding, element):
        arrived = (
            from_behind(holding[0].astype(jnp.bfloat16), "dp", -1).astype(jnp.float32),
            from_behind(holding[1].astype(jnp.bfloat16), "dp", -1).astype(jnp.float32),
        )
        return ((arrived[0] + element[0], arrived[1] + element[1]), None)

    holding, unused = lax.scan(
        return_step,
        (key_terms[reach_devs], value_terms[reach_devs]),
        (key_terms[:reach_devs][::-1], value_terms[:reach_devs][::-1]),
    )
    key_sum, value_sum = (holding[0], holding[1])
    key_state_gradient = key_sum.astype(jnp.bfloat16)
    value_state_gradient = value_sum.astype(jnp.bfloat16)
    return (projected, query_grad, key_state_gradient, value_state_gradient)


def solution(mesh):
    return jax.shard_map(
        per_device,
        mesh=mesh,
        in_specs=(
            P("dp", "tensor"),
            P("dp", "tensor"),
            P("dp", "tensor"),
            P("tensor", None),
            P("dp", "tensor"),
            P("dp"),
        ),
        out_specs=(P("dp", "tensor"), P("dp", "tensor"), P("dp", "tensor"), P("dp", "tensor")),
        check_vma=False,
    )
```

profile of v0, /device:TPU:155, one launch (start us, length us, event | category | flops | bytes accessed | tf_op | source)
XLA Modules:
  0.0 593.6 jit_solution(3970372579189418808)
XLA Ops:
  11.6 178.5 %while.70 = (s32[]{:T(128)}, bf16[128,1,128]{2,0,1:T(8,128)(2,1)S(1)}, bf16[128,1,128]{2,0,1:T(8,128)(2,1)S(1)}, s32[128]{0:T(128)S(1)}, bf16[16,128,1,128]{3,1,...) while((s32[]{:T(128)}, ...), condition=%wide.region_1.2_spmd, body=%wide.region_0.1_spmd.sunk | while | flops 2 | bytes 528617 | solution.py:59
  21.5 6.3 %collective-permute-start = (bf16[128,1,128]{2,0,1:T(8,128)(2,1)S(1)}, bf16[128,1,128]{2,0,1:T(8,128)(2,1)S(1)}, u32[]{:S(2)}, u32[]{:S(2)}) collective-permute-start(bf16[128,1,128]{2,0,1:T(8,128)(2,1)S(1)} %get-tuple-element.922), channel_id=1, source_target_pairs={{0,8},{8,16},{16,24},{24,32},{32,40},{40,48},{48,56},{56,64},{64,7... | collective-permute-start | bytes 98312 | tf_op jit(solution)/shard_map/while/body/eval_jaxpr/ppermute | solution.py:20
  32.9 6.2 %collective-permute-start = (bf16[128,1,128]{2,0,1:T(8,128)(2,1)S(1)}, bf16[128,1,128]{2,0,1:T(8,128)(2,1)S(1)}, u32[]{:S(2)}, u32[]{:S(2)}) collective-permute-start(bf16[128,1,128]{2,0,1:T(8,128)(2,1)S(1)} %get-tuple-element.922), channel_id=1, source_target_pairs={{0,8},{8,16},{16,24},{24,32},{32,40},{40,48},{48,56},{56,64},{64,7... | collective-permute-start | bytes 98312 | tf_op jit(solution)/shard_map/while/body/eval_jaxpr/ppermute | solution.py:20
  44.1 6.2 %collective-permute-start = (bf16[128,1,128]{2,0,1:T(8,128)(2,1)S(1)}, bf16[128,1,128]{2,0,1:T(8,128)(2,1)S(1)}, u32[]{:S(2)}, u32[]{:S(2)}) collective-permute-start(bf16[128,1,128]{2,0,1:T(8,128)(2,1)S(1)} %get-tuple-element.922), channel_id=1, source_target_pairs={{0,8},{8,16},{16,24},{24,32},{32,40},{40,48},{48,56},{56,64},{64,7... | collective-permute-start | bytes 98312 | tf_op jit(solution)/shard_map/while/body/eval_jaxpr/ppermute | solution.py:20
  55.3 6.2 %collective-permute-start = (bf16[128,1,128]{2,0,1:T(8,128)(2,1)S(1)}, bf16[128,1,128]{2,0,1:T(8,128)(2,1)S(1)}, u32[]{:S(2)}, u32[]{:S(2)}) collective-permute-start(bf16[128,1,128]{2,0,1:T(8,128)(2,1)S(1)} %get-tuple-element.922), channel_id=1, source_target_pairs={{0,8},{8,16},{16,24},{24,32},{32,40},{40,48},{48,56},{56,64},{64,7... | collective-permute-start | bytes 98312 | tf_op jit(solution)/shard_map/while/body/eval_jaxpr/ppermute | solution.py:20
  66.6 6.2 %collective-permute-start = (bf16[128,1,128]{2,0,1:T(8,128)(2,1)S(1)}, bf16[128,1,128]{2,0,1:T(8,128)(2,1)S(1)}, u32[]{:S(2)}, u32[]{:S(2)}) collective-permute-start(bf16[128,1,128]{2,0,1:T(8,128)(2,1)S(1)} %get-tuple-element.922), channel_id=1, source_target_pairs={{0,8},{8,16},{16,24},{24,32},{32,40},{40,48},{48,56},{56,64},{64,7... | collective-permute-start | bytes 98312 | tf_op jit(solution)/shard_map/while/body/eval_jaxpr/ppermute | solution.py:20
  77.8 6.2 %collective-permute-start = (bf16[128,1,128]{2,0,1:T(8,128)(2,1)S(1)}, bf16[128,1,128]{2,0,1:T(8,128)(2,1)S(1)}, u32[]{:S(2)}, u32[]{:S(2)}) collective-permute-start(bf16[128,1,128]{2,0,1:T(8,128)(2,1)S(1)} %get-tuple-element.922), channel_id=1, source_target_pairs={{0,8},{8,16},{16,24},{24,32},{32,40},{40,48},{48,56},{56,64},{64,7... | collective-permute-start | bytes 98312 | tf_op jit(solution)/shard_map/while/body/eval_jaxpr/ppermute | solution.py:20
  89.0 6.2 %collective-permute-start = (bf16[128,1,128]{2,0,1:T(8,128)(2,1)S(1)}, bf16[128,1,128]{2,0,1:T(8,128)(2,1)S(1)}, u32[]{:S(2)}, u32[]{:S(2)}) collective-permute-start(bf16[128,1,128]{2,0,1:T(8,128)(2,1)S(1)} %get-tuple-element.922), channel_id=1, source_target_pairs={{0,8},{8,16},{16,24},{24,32},{32,40},{40,48},{48,56},{56,64},{64,7... | collective-permute-start | bytes 98312 | tf_op jit(solution)/shard_map/while/body/eval_jaxpr/ppermute | solution.py:20
  100.3 6.2 %collective-permute-start = (bf16[128,1,128]{2,0,1:T(8,128)(2,1)S(1)}, bf16[128,1,128]{2,0,1:T(8,128)(2,1)S(1)}, u32[]{:S(2)}, u32[]{:S(2)}) collective-permute-start(bf16[128,1,128]{2,0,1:T(8,128)(2,1)S(1)} %get-tuple-element.922), channel_id=1, source_target_pairs={{0,8},{8,16},{16,24},{24,32},{32,40},{40,48},{48,56},{56,64},{64,7... | collective-permute-start | bytes 98312 | tf_op jit(solution)/shard_map/while/body/eval_jaxpr/ppermute | solution.py:20
  111.5 6.2 %collective-permute-start = (bf16[128,1,128]{2,0,1:T(8,128)(2,1)S(1)}, bf16[128,1,128]{2,0,1:T(8,128)(2,1)S(1)}, u32[]{:S(2)}, u32[]{:S(2)}) collective-permute-start(bf16[128,1,128]{2,0,1:T(8,128)(2,1)S(1)} %get-tuple-element.922), channel_id=1, source_target_pairs={{0,8},{8,16},{16,24},{24,32},{32,40},{40,48},{48,56},{56,64},{64,7... | collective-permute-start | bytes 98312 | tf_op jit(solution)/shard_map/while/body/eval_jaxpr/ppermute | solution.py:20
  122.7 6.2 %collective-permute-start = (bf16[128,1,128]{2,0,1:T(8,128)(2,1)S(1)}, bf16[128,1,128]{2,0,1:T(8,128)(2,1)S(1)}, u32[]{:S(2)}, u32[]{:S(2)}) collective-permute-start(bf16[128,1,128]{2,0,1:T(8,128)(2,1)S(1)} %get-tuple-element.922), channel_id=1, source_target_pairs={{0,8},{8,16},{16,24},{24,32},{32,40},{40,48},{48,56},{56,64},{64,7... | collective-permute-start | bytes 98312 | tf_op jit(solution)/shard_map/while/body/eval_jaxpr/ppermute | solution.py:20
  133.9 6.2 %collective-permute-start = (bf16[128,1,128]{2,0,1:T(8,128)(2,1)S(1)}, bf16[128,1,128]{2,0,1:T(8,128)(2,1)S(1)}, u32[]{:S(2)}, u32[]{:S(2)}) collective-permute-start(bf16[128,1,128]{2,0,1:T(8,128)(2,1)S(1)} %get-tuple-element.922), channel_id=1, source_target_pairs={{0,8},{8,16},{16,24},{24,32},{32,40},{40,48},{48,56},{56,64},{64,7... | collective-permute-start | bytes 98312 | tf_op jit(solution)/shard_map/while/body/eval_jaxpr/ppermute | solution.py:20
  145.2 6.2 %collective-permute-start = (bf16[128,1,128]{2,0,1:T(8,128)(2,1)S(1)}, bf16[128,1,128]{2,0,1:T(8,128)(2,1)S(1)}, u32[]{:S(2)}, u32[]{:S(2)}) collective-permute-start(bf16[128,1,128]{2,0,1:T(8,128)(2,1)S(1)} %get-tuple-element.922), channel_id=1, source_target_pairs={{0,8},{8,16},{16,24},{24,32},{32,40},{40,48},{48,56},{56,64},{64,7... | collective-permute-start | bytes 98312 | tf_op jit(solution)/shard_map/while/body/eval_jaxpr/ppermute | solution.py:20
  156.4 6.2 %collective-permute-start = (bf16[128,1,128]{2,0,1:T(8,128)(2,1)S(1)}, bf16[128,1,128]{2,0,1:T(8,128)(2,1)S(1)}, u32[]{:S(2)}, u32[]{:S(2)}) collective-permute-start(bf16[128,1,128]{2,0,1:T(8,128)(2,1)S(1)} %get-tuple-element.922), channel_id=1, source_target_pairs={{0,8},{8,16},{16,24},{24,32},{32,40},{40,48},{48,56},{56,64},{64,7... | collective-permute-start | bytes 98312 | tf_op jit(solution)/shard_map/while/body/eval_jaxpr/ppermute | solution.py:20
  167.6 6.2 %collective-permute-start = (bf16[128,1,128]{2,0,1:T(8,128)(2,1)S(1)}, bf16[128,1,128]{2,0,1:T(8,128)(2,1)S(1)}, u32[]{:S(2)}, u32[]{:S(2)}) collective-permute-start(bf16[128,1,128]{2,0,1:T(8,128)(2,1)S(1)} %get-tuple-element.922), channel_id=1, source_target_pairs={{0,8},{8,16},{16,24},{24,32},{32,40},{40,48},{48,56},{56,64},{64,7... | collective-permute-start | bytes 98312 | tf_op jit(solution)/shard_map/while/body/eval_jaxpr/ppermute | solution.py:20
  178.8 6.2 %collective-permute-start = (bf16[128,1,128]{2,0,1:T(8,128)(2,1)S(1)}, bf16[128,1,128]{2,0,1:T(8,128)(2,1)S(1)}, u32[]{:S(2)}, u32[]{:S(2)}) collective-permute-start(bf16[128,1,128]{2,0,1:T(8,128)(2,1)S(1)} %get-tuple-element.922), channel_id=1, source_target_pairs={{0,8},{8,16},{16,24},{24,32},{32,40},{40,48},{48,56},{56,64},{64,7... | collective-permute-start | bytes 98312 | tf_op jit(solution)/shard_map/while/body/eval_jaxpr/ppermute | solution.py:20
  191.9 61.6 %while.73 = (s32[]{:T(128)}, f32[17,1,8,128,128]{3,4,2,1,0:T(8,128)}, pred[17]{0:T(512)(128)(4,1)S(1)}, bf16[17,128,1,128]{3,1,2,0:T(8,128)(2,1)S(1)}, bf16[1,8,...) while((s32[]{:T(128)}, ...), condition=%wide.region_6.7_spmd.clone, body=%wide.region_3.6_spmd.clone.sunk | while | flops 33882112 | bytes 1905359 | solution.py:77
  253.4 9.4 %copy.25 = f32[17,1,8,128,128]{4,3,2,1,0:T(8,128)} copy(f32[17,1,8,128,128]{3,4,2,1,0:T(8,128)} %get-tuple-element.1001) | data formatting | bytes 17825792 | tf_op jit(solution)/shard_map/while | solution.py:104
  262.8 4.3 reduce_max.11
  267.1 67.3 %while.71 = (s32[]{:T(128)}, f32[1,8,128]{2,1,0:T(8,128)S(1)}, f32[1,8,128,128]{3,2,1,0:T(8,128)S(1)}, pred[17]{0:T(512)(128)(4,1)S(1)}, f32[17,1,8,128,128]{4,3...) while((s32[]{:T(128)}, f32[1,8,128]{2,1,0:T(8,128)S(1)}, ...), condition=%wide.region_12.13_spmd, body=%wide.region_8.12_spmd.sunk | while | flops 34209792 | bytes 2155708 | solution.py:104
  334.7 6.6 %fusion.38 = bf16[16,8,8,128]{3,1,2,0:T(8,128)(2,1)S(1)} fusion(bf16[128,4096]{1,0:T(8,128)(2,1)} %all-gather.2.cloned.1.call-done, bf16[1024,4096]{1,0:T(8,128)(2,1)} %param.25), kind=kOutput, calls=%fused_computation.59 | convolution fusion | flops 1073872896 | bytes 9699328 | tf_op jit(solution)/shard_map/dot_general | solution.py:118
  341.8 85.3 %while.74 = (s32[]{:T(128)}, f32[1,8,128,128]{3,2,1,0:T(8,128)S(1)}, f32[17,128,1,128]{3,1,2,0:T(8,128)}, f32[17,128,1,128]{3,1,2,0:T(8,128)}, pred[17]{0:T(512)...) while((s32[]{:T(128)}, ...), condition=%wide.region_17.18_spmd.clone, body=%wide.region_14.17_spmd.clone.sunk | while | flops 135397376 | bytes 5191926 | solution.py:162
  431.6 5.7 convolution_convert_fusion
  437.3 148.8 %while.72 = (s32[]{:T(128)}, bf16[128,128]{1,0:T(8,128)(2,1)S(1)}, bf16[128,128]{1,0:T(8,128)(2,1)S(1)}, f32[16,128,128]{2,1,0:T(8,128)}, f32[16,128,128]{2,1,0:T(8,128)S(1)}, /*index=5*/s32[]{:T(128)}) while((s32[]{:T(128)}, bf16[128,128]{1,0:T(8,128)(2,1)S(1)}, bf16[128,128]{1,0:T(8,128)(2,1)S(1)}, f32[16,128,128]{2,1,0:T(8,128)}, ...), condition=%wide.region_19.20_spmd, body=%wide.region_18.19_spmd.sunk | while | flops 98306 | bytes 524453 | solution.py:176
  (659 shorter events, 544.1 us)
Async XLA Ops:
  7.2 327.5 %all-gather.2.cloned.1.call-start = ((), (), s32[]{:S(2)}) async-start(), calls=%async_computation.2 | async-start | bytes 1179648 | tf_op jit(solution)/shard_map/all_gather | solution.py:117
  7.9 578.2 %reduce-scatter.2.cloned.1.call-start = ((), (), s32[]{:S(2)}) async-start(), calls=%async_computation.1 | async-start | bytes 1179648 | tf_op jit(solution)/shard_map/reduce_scatter | solution.py:114
  11.6 8.9 %collective-permute-start = (bf16[128,1,128]{2,0,1:T(8,128)(2,1)S(1)}, bf16[128,1,128]{2,0,1:T(8,128)(2,1)S(1)}, u32[]{:S(2)}, u32[]{:S(2)}) collective-permute-start(bf16[128,1,128]{2,0,1:T(8,128)(2,1)S(1)} %get-tuple-element.922), channel_id=1, source_target_pairs={{0,8},{8,16},{16,24},{24,32},{32,40},{40,48},{48,56},{56,64},{64,7... | collective-permute-start | bytes 98312 | tf_op jit(solution)/shard_map/while/body/eval_jaxpr/ppermute | solution.py:20
  21.5 10.3 %collective-permute-start = (bf16[128,1,128]{2,0,1:T(8,128)(2,1)S(1)}, bf16[128,1,128]{2,0,1:T(8,128)(2,1)S(1)}, u32[]{:S(2)}, u32[]{:S(2)}) collective-permute-start(bf16[128,1,128]{2,0,1:T(8,128)(2,1)S(1)} %get-tuple-element.922), channel_id=1, source_target_pairs={{0,8},{8,16},{16,24},{24,32},{32,40},{40,48},{48,56},{56,64},{64,7... | collective-permute-start | bytes 98312 | tf_op jit(solution)/shard_map/while/body/eval_jaxpr/ppermute | solution.py:20
  32.9 10.1 %collective-permute-start = (bf16[128,1,128]{2,0,1:T(8,128)(2,1)S(1)}, bf16[128,1,128]{2,0,1:T(8,128)(2,1)S(1)}, u32[]{:S(2)}, u32[]{:S(2)}) collective-permute-start(bf16[128,1,128]{2,0,1:T(8,128)(2,1)S(1)} %get-tuple-element.922), channel_id=1, source_target_pairs={{0,8},{8,16},{16,24},{24,32},{32,40},{40,48},{48,56},{56,64},{64,7... | collective-permute-start | bytes 98312 | tf_op jit(solution)/shard_map/while/body/eval_jaxpr/ppermute | solution.py:20
  44.1 10.1 %collective-permute-start = (bf16[128,1,128]{2,0,1:T(8,128)(2,1)S(1)}, bf16[128,1,128]{2,0,1:T(8,128)(2,1)S(1)}, u32[]{:S(2)}, u32[]{:S(2)}) collective-permute-start(bf16[128,1,128]{2,0,1:T(8,128)(2,1)S(1)} %get-tuple-element.922), channel_id=1, source_target_pairs={{0,8},{8,16},{16,24},{24,32},{32,40},{40,48},{48,56},{56,64},{64,7... | collective-permute-start | bytes 98312 | tf_op jit(solution)/shard_map/while/body/eval_jaxpr/ppermute | solution.py:20
  55.3 10.1 %collective-permute-start = (bf16[128,1,128]{2,0,1:T(8,128)(2,1)S(1)}, bf16[128,1,128]{2,0,1:T(8,128)(2,1)S(1)}, u32[]{:S(2)}, u32[]{:S(2)}) collective-permute-start(bf16[128,1,128]{2,0,1:T(8,128)(2,1)S(1)} %get-tuple-element.922), channel_id=1, source_target_pairs={{0,8},{8,16},{16,24},{24,32},{32,40},{40,48},{48,56},{56,64},{64,7... | collective-permute-start | bytes 98312 | tf_op jit(solution)/shard_map/while/body/eval_jaxpr/ppermute | solution.py:20
  66.6 10.1 %collective-permute-start = (bf16[128,1,128]{2,0,1:T(8,128)(2,1)S(1)}, bf16[128,1,128]{2,0,1:T(8,128)(2,1)S(1)}, u32[]{:S(2)}, u32[]{:S(2)}) collective-permute-start(bf16[128,1,128]{2,0,1:T(8,128)(2,1)S(1)} %get-tuple-element.922), channel_id=1, source_target_pairs={{0,8},{8,16},{16,24},{24,32},{32,40},{40,48},{48,56},{56,64},{64,7... | collective-permute-start | bytes 98312 | tf_op jit(solution)/shard_map/while/body/eval_jaxpr/ppermute | solution.py:20
  77.8 10.1 %collective-permute-start = (bf16[128,1,128]{2,0,1:T(8,128)(2,1)S(1)}, bf16[128,1,128]{2,0,1:T(8,128)(2,1)S(1)}, u32[]{:S(2)}, u32[]{:S(2)}) collective-permute-start(bf16[128,1,128]{2,0,1:T(8,128)(2,1)S(1)} %get-tuple-element.922), channel_id=1, source_target_pairs={{0,8},{8,16},{16,24},{24,32},{32,40},{40,48},{48,56},{56,64},{64,7... | collective-permute-start | bytes 98312 | tf_op jit(solution)/shard_map/while/body/eval_jaxpr/ppermute | solution.py:20
  89.0 10.1 %collective-permute-start = (bf16[128,1,128]{2,0,1:T(8,128)(2,1)S(1)}, bf16[128,1,128]{2,0,1:T(8,128)(2,1)S(1)}, u32[]{:S(2)}, u32[]{:S(2)}) collective-permute-start(bf16[128,1,128]{2,0,1:T(8,128)(2,1)S(1)} %get-tuple-element.922), channel_id=1, source_target_pairs={{0,8},{8,16},{16,24},{24,32},{32,40},{40,48},{48,56},{56,64},{64,7... | collective-permute-start | bytes 98312 | tf_op jit(solution)/shard_map/while/body/eval_jaxpr/ppermute | solution.py:20
  100.3 10.1 %collective-permute-start = (bf16[128,1,128]{2,0,1:T(8,128)(2,1)S(1)}, bf16[128,1,128]{2,0,1:T(8,128)(2,1)S(1)}, u32[]{:S(2)}, u32[]{:S(2)}) collective-permute-start(bf16[128,1,128]{2,0,1:T(8,128)(2,1)S(1)} %get-tuple-element.922), channel_id=1, source_target_pairs={{0,8},{8,16},{16,24},{24,32},{32,40},{40,48},{48,56},{56,64},{64,7... | collective-permute-start | bytes 98312 | tf_op jit(solution)/shard_map/while/body/eval_jaxpr/ppermute | solution.py:20
  111.5 10.1 %collective-permute-start = (bf16[128,1,128]{2,0,1:T(8,128)(2,1)S(1)}, bf16[128,1,128]{2,0,1:T(8,128)(2,1)S(1)}, u32[]{:S(2)}, u32[]{:S(2)}) collective-permute-start(bf16[128,1,128]{2,0,1:T(8,128)(2,1)S(1)} %get-tuple-element.922), channel_id=1, source_target_pairs={{0,8},{8,16},{16,24},{24,32},{32,40},{40,48},{48,56},{56,64},{64,7... | collective-permute-start | bytes 98312 | tf_op jit(solution)/shard_map/while/body/eval_jaxpr/ppermute | solution.py:20
  122.7 10.1 %collective-permute-start = (bf16[128,1,128]{2,0,1:T(8,128)(2,1)S(1)}, bf16[128,1,128]{2,0,1:T(8,128)(2,1)S(1)}, u32[]{:S(2)}, u32[]{:S(2)}) collective-permute-start(bf16[128,1,128]{2,0,1:T(8,128)(2,1)S(1)} %get-tuple-element.922), channel_id=1, source_target_pairs={{0,8},{8,16},{16,24},{24,32},{32,40},{40,48},{48,56},{56,64},{64,7... | collective-permute-start | bytes 98312 | tf_op jit(solution)/shard_map/while/body/eval_jaxpr/ppermute | solution.py:20
  133.9 10.1 %collective-permute-start = (bf16[128,1,128]{2,0,1:T(8,128)(2,1)S(1)}, bf16[128,1,128]{2,0,1:T(8,128)(2,1)S(1)}, u32[]{:S(2)}, u32[]{:S(2)}) collective-permute-start(bf16[128,1,128]{2,0,1:T(8,128)(2,1)S(1)} %get-tuple-element.922), channel_id=1, source_target_pairs={{0,8},{8,16},{16,24},{24,32},{32,40},{40,48},{48,56},{56,64},{64,7... | collective-permute-start | bytes 98312 | tf_op jit(solution)/shard_map/while/body/eval_jaxpr/ppermute | solution.py:20
  145.2 10.1 %collective-permute-start = (bf16[128,1,128]{2,0,1:T(8,128)(2,1)S(1)}, bf16[128,1,128]{2,0,1:T(8,128)(2,1)S(1)}, u32[]{:S(2)}, u32[]{:S(2)}) collective-permute-start(bf16[128,1,128]{2,0,1:T(8,128)(2,1)S(1)} %get-tuple-element.922), channel_id=1, source_target_pairs={{0,8},{8,16},{16,24},{24,32},{32,40},{40,48},{48,56},{56,64},{64,7... | collective-permute-start | bytes 98312 | tf_op jit(solution)/shard_map/while/body/eval_jaxpr/ppermute | solution.py:20
  156.4 10.1 %collective-permute-start = (bf16[128,1,128]{2,0,1:T(8,128)(2,1)S(1)}, bf16[128,1,128]{2,0,1:T(8,128)(2,1)S(1)}, u32[]{:S(2)}, u32[]{:S(2)}) collective-permute-start(bf16[128,1,128]{2,0,1:T(8,128)(2,1)S(1)} %get-tuple-element.922), channel_id=1, source_target_pairs={{0,8},{8,16},{16,24},{24,32},{32,40},{40,48},{48,56},{56,64},{64,7... | collective-permute-start | bytes 98312 | tf_op jit(solution)/shard_map/while/body/eval_jaxpr/ppermute | solution.py:20
  167.6 10.1 %collective-permute-start = (bf16[128,1,128]{2,0,1:T(8,128)(2,1)S(1)}, bf16[128,1,128]{2,0,1:T(8,128)(2,1)S(1)}, u32[]{:S(2)}, u32[]{:S(2)}) collective-permute-start(bf16[128,1,128]{2,0,1:T(8,128)(2,1)S(1)} %get-tuple-element.922), channel_id=1, source_target_pairs={{0,8},{8,16},{16,24},{24,32},{32,40},{40,48},{48,56},{56,64},{64,7... | collective-permute-start | bytes 98312 | tf_op jit(solution)/shard_map/while/body/eval_jaxpr/ppermute | solution.py:20
  178.8 10.1 %collective-permute-start = (bf16[128,1,128]{2,0,1:T(8,128)(2,1)S(1)}, bf16[128,1,128]{2,0,1:T(8,128)(2,1)S(1)}, u32[]{:S(2)}, u32[]{:S(2)}) collective-permute-start(bf16[128,1,128]{2,0,1:T(8,128)(2,1)S(1)} %get-tuple-element.922), channel_id=1, source_target_pairs={{0,8},{8,16},{16,24},{24,32},{32,40},{40,48},{48,56},{56,64},{64,7... | collective-permute-start | bytes 98312 | tf_op jit(solution)/shard_map/while/body/eval_jaxpr/ppermute | solution.py:20
  437.3 7.3 %collective-permute-start.3 = (bf16[128,128]{1,0:T(8,128)(2,1)S(1)}, bf16[128,128]{1,0:T(8,128)(2,1)S(1)}, u32[]{:S(2)}, u32[]{:S(2)}) collective-permute-start(bf16[128,128]{1,0:T(8,128)(2,1)S(1)} %get-tuple-element.1045), channel_id=1, source_target_pairs={{8,0},{16,8},{24,16},{32,24},{40,32},{48,40},{56,48},{64,56},{72,6... | collective-permute-start | bytes 98312 | tf_op jit(solution)/shard_map/while/body/eval_jaxpr/ppermute | solution.py:20
  439.2 7.3 %collective-permute-start.4 = (bf16[128,128]{1,0:T(8,128)(2,1)S(1)}, bf16[128,128]{1,0:T(8,128)(2,1)S(1)}, u32[]{:S(2)}, u32[]{:S(2)}) collective-permute-start(bf16[128,128]{1,0:T(8,128)(2,1)S(1)} %get-tuple-element.1046), channel_id=1, source_target_pairs={{8,0},{16,8},{24,16},{32,24},{40,32},{48,40},{56,48},{64,56},{72,6... | collective-permute-start | bytes 98312 | tf_op jit(solution)/shard_map/while/body/eval_jaxpr/ppermute | solution.py:20
  446.6 7.3 %collective-permute-start.3 = (bf16[128,128]{1,0:T(8,128)(2,1)S(1)}, bf16[128,128]{1,0:T(8,128)(2,1)S(1)}, u32[]{:S(2)}, u32[]{:S(2)}) collective-permute-start(bf16[128,128]{1,0:T(8,128)(2,1)S(1)} %get-tuple-element.1045), channel_id=1, source_target_pairs={{8,0},{16,8},{24,16},{32,24},{40,32},{48,40},{56,48},{64,56},{72,6... | collective-permute-start | bytes 98312 | tf_op jit(solution)/shard_map/while/body/eval_jaxpr/ppermute | solution.py:20
  448.5 7.3 %collective-permute-start.4 = (bf16[128,128]{1,0:T(8,128)(2,1)S(1)}, bf16[128,128]{1,0:T(8,128)(2,1)S(1)}, u32[]{:S(2)}, u32[]{:S(2)}) collective-permute-start(bf16[128,128]{1,0:T(8,128)(2,1)S(1)} %get-tuple-element.1046), channel_id=1, source_target_pairs={{8,0},{16,8},{24,16},{32,24},{40,32},{48,40},{56,48},{64,56},{72,6... | collective-permute-start | bytes 98312 | tf_op jit(solution)/shard_map/while/body/eval_jaxpr/ppermute | solution.py:20
  455.9 7.3 %collective-permute-start.3 = (bf16[128,128]{1,0:T(8,128)(2,1)S(1)}, bf16[128,128]{1,0:T(8,128)(2,1)S(1)}, u32[]{:S(2)}, u32[]{:S(2)}) collective-permute-start(bf16[128,128]{1,0:T(8,128)(2,1)S(1)} %get-tuple-element.1045), channel_id=1, source_target_pairs={{8,0},{16,8},{24,16},{32,24},{40,32},{48,40},{56,48},{64,56},{72,6... | collective-permute-start | bytes 98312 | tf_op jit(solution)/shard_map/while/body/eval_jaxpr/ppermute | solution.py:20
  457.8 7.3 %collective-permute-start.4 = (bf16[128,128]{1,0:T(8,128)(2,1)S(1)}, bf16[128,128]{1,0:T(8,128)(2,1)S(1)}, u32[]{:S(2)}, u32[]{:S(2)}) collective-permute-start(bf16[128,128]{1,0:T(8,128)(2,1)S(1)} %get-tuple-element.1046), channel_id=1, source_target_pairs={{8,0},{16,8},{24,16},{32,24},{40,32},{48,40},{56,48},{64,56},{72,6... | collective-permute-start | bytes 98312 | tf_op jit(solution)/shard_map/while/body/eval_jaxpr/ppermute | solution.py:20
  (64 other events, 859.3 us)
Sparse Core Ops, SparseCore 0:
  9.8 32.7 all-gather.1
  437.4 30.8 reduce-scatter.1
where the time goes:
time: 601 us; the launch traced here: 594 us
  starting transfers between devices  221 us (37%)
  waiting for transfers between devices  90.8 us (15%)
  matrix products  87.3 us (15%)
  local copies, waits for them, and re-layouts  85 us (14%)
  other arithmetic  57.5 us (10%)
  loops' own time  37.9 us (6%)
  between operations  14.4 us (2%)
    ppermute x80, starting transfers between devices, from_behind(): return lax.ppermute(x, axis, pairs)  221 us
    ppermute x80, waiting for transfers between devices, from_behind(): return lax.ppermute(x, axis, pairs)  90.1 us
    dynamic_slice x83, local copies, waits for them, and re-layouts, per_device(): scores = lax.map(score_one, (key_blocks, allowed, live_flags))  39.7 us
    reduce_sum x16, other arithmetic, accumulate_compute(): return (running[0] + jnp.sum(weight, axis=-1), running[1] + mixed)  22.8 us
    dot_general x16, matrix products, accumulate_compute(): jnp.einsum('cgts,scd->cgtd', weight.astype(jnp.bfloat16), value_blk, pref...  22.3 us
    dot_general x16, matrix products, backward_compute(): jnp.einsum('cgtd,scd->cgts', grad_heads, value_blk, preferred_element_typ...  20.9 us
    dot_general x16, matrix products, backward_compute(): jnp.einsum('cgts,cgtd->scd', probability.astype(jnp.bfloat16), grad_heads...  20.3 us
    dynamic_update_slice x17, local copies, waits for them, and re-layouts, per_device(): scores = lax.map(score_one, (key_blocks, allowed, live_flags))  14.5 us
  transfers between devices with their start and end apart: 82, of which 48 were waited for; matrix products, arithmetic and copies ran while one was open for 23% of the time, Pallas kernels for 0%

commit v1 on v0

v1 whole, which is shorter than its diff:
```python
import math

import jax
import jax.numpy as jnp
from jax import lax
from jax.experimental import pallas as pl
from jax.experimental.pallas import tpu as pltpu
from jax.sharding import PartitionSpec as P

HEADS = 8
HEAD_SIZE = 128
TOK = 128
PAIR = 2 * TOK
DOCS = 16
ROWS = TOK + DOCS
SLOTS = 9
KEYS = SLOTS * PAIR
STEP = 2 * PAIR
CHUNK = 256
QROWS = HEADS * TOK
FEATURES = 512
MASKED = -1e30
SCALE = 1.0 / math.sqrt(HEAD_SIZE)
SCALE_LOG2 = SCALE * math.log2(math.e)

VMEM = pl.BlockSpec(memory_space=pltpu.VMEM)
SMEM = pl.BlockSpec(memory_space=pltpu.SMEM)
NT = (((1,), (1,)), ((), ()))

PLACE = {0: (0, 0), 4: (0, 1), 8: (1, 0), 1: (2, 0), 5: (2, 1), 2: (3, 0), 6: (3, 1), 3: (4, 0), 7: (4, 1)}
HELD = (2, 1, 2, 2, 2)


def dot_nt(a, b):
    return lax.dot_general(a, b, NT, preferred_element_type=jnp.float32)


def dot(a, b):
    return jnp.dot(a, b, preferred_element_type=jnp.float32)


def params(mib):
    return pltpu.CompilerParams(vmem_limit_bytes=mib * 1024 * 1024)


def cost(flops, nbytes, trans=0):
    return pl.CostEstimate(flops=flops, bytes_accessed=nbytes, transcendentals=trans)


def shaped(*shape, dtype=jnp.bfloat16):
    return jax.ShapeDtypeStruct(shape, dtype)


def pack_kernel(key_ref, value_ref, id_ref, out_ref):
    out_ref[0, 0:TOK, 0:HEAD_SIZE] = key_ref[...]
    out_ref[0, 0:TOK, HEAD_SIZE : 2 * HEAD_SIZE] = value_ref[...]
    number = lax.broadcasted_iota(jnp.int32, (DOCS, TOK), 0)
    below = jnp.where(id_ref[...] < number, 1.0, 0.0)
    count = jnp.sum(below, axis=1, keepdims=True)
    out_ref[0, TOK:ROWS, :] = jnp.broadcast_to(count, (DOCS, 2 * HEAD_SIZE)).astype(jnp.bfloat16)


def bias_of(base, rows, core, query_pair, first_row):
    row = lax.broadcasted_iota(jnp.int32, (rows, TOK), 0)
    column = lax.broadcasted_iota(jnp.int32, (rows, TOK), 1)
    key_pos = base + jnp.where(row < PAIR, row, row - 2 * PAIR)
    query_pos = query_pair * PAIR + core * TOK + column
    allowed = (key_pos >= first_row) & (key_pos <= query_pos)
    bias = jnp.where(allowed, 0.0, MASKED)
    return jnp.concatenate([bias] * (CHUNK // TOK), 1)


def eights(value):
    return value.reshape(value.shape[0] // 8, 8, value.shape[1])


def forward_kernel(info_ref, q_ref, id_ref, *refs):
    own, sib, refs = refs[:5], refs[5:10], refs[10:]
    att_ref, att_t_ref, log_ref, first_ref, rows_ref, key_ref, value_ref = refs[:7]
    score_ref, acc_ref, max_ref, sum_ref = refs[7:]
    query_pair, core = info_ref[0], info_ref[1]
    at_own = pl.multiple_of(core * TOK, TOK)
    at_sib = pl.multiple_of((1 - core) * TOK, TOK)
    below = jnp.zeros((DOCS, TOK), jnp.float32)
    for j in range(SLOTS):
        array, place = PLACE[j]
        valid = jnp.where(query_pair >= j, 1.0, 0.0)
        for held, at in ((own, at_own), (sib, at_sib)):
            ref = held[array]
            key_ref[pl.ds(j * PAIR + at, TOK), :] = ref[place, 0:TOK, 0:HEAD_SIZE]
            value_ref[pl.ds(j * PAIR + at, TOK), :] = ref[place, 0:TOK, HEAD_SIZE : 2 * HEAD_SIZE]
            below = below + valid * ref[place, TOK:ROWS, 0:TOK].astype(jnp.float32)
    for h in range(HEADS):
        rows_ref[h * TOK : (h + 1) * TOK, :] = q_ref[:, h * HEAD_SIZE : (h + 1) * HEAD_SIZE]
    number = lax.broadcasted_iota(jnp.int32, (DOCS, TOK), 0)
    before = jnp.sum(jnp.where(id_ref[...] == number, below, 0.0), axis=0, keepdims=True)
    first_row = before.astype(jnp.int32) + PAIR * jnp.maximum(query_pair - (SLOTS - 1), 0)
    first_ref[...] = first_row
    live = query_pair - jnp.min(first_row) // PAIR + 1
    max_ref[...] = jnp.full(max_ref.shape, MASKED, jnp.float32)
    sum_ref[...] = jnp.zeros(sum_ref.shape, jnp.float32)
    acc_ref[...] = jnp.zeros(acc_ref.shape, jnp.float32)

    def score_rows(start, count, base):
        rows = pl.ds(start, count)
        key = key_ref[rows, :]
        bias = bias_of(base, count, core, query_pair, first_row)
        for n in range(QROWS // CHUNK):
            cols = slice(n * CHUNK, (n + 1) * CHUNK)
            score = dot_nt(key, rows_ref[cols, :]) * SCALE_LOG2 + bias
            score_ref[rows, cols] = score
            max_ref[:, cols] = jnp.maximum(max_ref[:, cols], jnp.max(eights(score), axis=0))

    def mix_rows(start, count):
        rows = pl.ds(start, count)
        value_t = value_ref[rows, :].T
        for n in range(QROWS // CHUNK):
            cols = slice(n * CHUNK, (n + 1) * CHUNK)
            weight = jnp.exp2(score_ref[rows, cols] - log_ref[:, cols])
            sum_ref[:, cols] = sum_ref[:, cols] + jnp.sum(eights(weight), axis=0)
            acc_ref[:, cols] = acc_ref[:, cols] + dot(value_t, weight.astype(jnp.bfloat16))

    def score_step(s, unused):
        score_rows(pl.multiple_of(PAIR + s * STEP, PAIR), STEP, (query_pair - 1 - 2 * s) * PAIR)
        return unused

    def mix_step(s, unused):
        mix_rows(pl.multiple_of(PAIR + s * STEP, PAIR), STEP)
        return unused

    score_rows(0, PAIR, query_pair * PAIR)
    lax.fori_loop(0, live // 2, score_step, 0)
    log_ref[...] = jnp.max(max_ref[...], axis=0, keepdims=True)
    mix_rows(0, PAIR)
    lax.fori_loop(0, live // 2, mix_step, 0)
    total = jnp.sum(sum_ref[...], axis=0, keepdims=True)
    log_ref[...] = log_ref[...] + jnp.log2(total)
    inverse = 1.0 / total
    for h in range(HEADS):
        cols = slice(h * TOK, (h + 1) * TOK)
        mixed = acc_ref[:, cols] * inverse[:, cols]
        att_t_ref[:, cols] = mixed.astype(jnp.bfloat16)
        att_ref[:, h * HEAD_SIZE : (h + 1) * HEAD_SIZE] = mixed.T.astype(jnp.bfloat16)


def backward_kernel(info_ref, rows_ref, key_ref, value_ref, att_t_ref, grad_ref, log_ref, first_ref, *refs):
    dq_ref, own, sib, refs = refs[0], refs[1:6], refs[6:11], refs[11:]
    grad_t_ref, grows_ref, acc_ref, delta_ref, out_ref = refs
    query_pair, core = info_ref[0], info_ref[1]
    at_own = pl.multiple_of(core * TOK, TOK)
    at_sib = pl.multiple_of((1 - core) * TOK, TOK)
    first_row = first_ref[...]
    live = query_pair - jnp.min(first_row) // PAIR + 1
    for h in range(HEADS):
        part = slice(h * TOK, (h + 1) * TOK)
        grad_t = grad_ref[part, :]
        grad_t_ref[:, part] = grad_t
        grows_ref[part, :] = grad_t.T
        product = grad_t.astype(jnp.float32) * att_t_ref[:, part].astype(jnp.float32)
        delta_ref[:, part] = jnp.sum(product, axis=0, keepdims=True)
    acc_ref[...] = jnp.zeros(acc_ref.shape, jnp.float32)
    out_ref[...] = jnp.zeros(out_ref.shape, jnp.bfloat16)

    def grad_rows(start, count, base):
        rows = pl.ds(start, count)
        key = key_ref[rows, :]
        value = value_ref[rows, :]
        key_t = key.T
        bias = bias_of(base, count, core, query_pair, first_row)
        dkey = jnp.zeros((count, HEAD_SIZE), jnp.float32)
        dvalue = jnp.zeros((count, HEAD_SIZE), jnp.float32)
        for n in range(QROWS // CHUNK):
            cols = slice(n * CHUNK, (n + 1) * CHUNK)
            score = dot_nt(key, rows_ref[cols, :]) * SCALE_LOG2 + bias
            prob = jnp.exp2(score - log_ref[:, cols])
            gprob = dot(value, grad_t_ref[:, cols])
            gscore = (prob * (gprob - delta_ref[:, cols])).astype(jnp.bfloat16)
            dvalue = dvalue + dot(prob.astype(jnp.bfloat16), grows_ref[cols, :])
            dkey = dkey + dot(gscore, rows_ref[cols, :])
            acc_ref[:, cols] = acc_ref[:, cols] + dot(key_t, gscore)
        out_ref[rows, 0:HEAD_SIZE] = (dkey * SCALE).astype(jnp.bfloat16)
        out_ref[rows, HEAD_SIZE : 2 * HEAD_SIZE] = dvalue.astype(jnp.bfloat16)

    def grad_step(s, unused):
        grad_rows(pl.multiple_of(PAIR + s * STEP, PAIR), STEP, (query_pair - 1 - 2 * s) * PAIR)
        return unused

    grad_rows(0, PAIR, query_pair * PAIR)
    lax.fori_loop(0, live // 2, grad_step, 0)
    for j in range(SLOTS):
        array, place = PLACE[j]
        own[array][place] = out_ref[pl.ds(j * PAIR + at_own, TOK), :]
        sib[array][place] = out_ref[pl.ds(j * PAIR + at_sib, TOK), :]
    for h in range(HEADS):
        mixed = acc_ref[:, h * TOK : (h + 1) * TOK] * SCALE
        dq_ref[:, h * HEAD_SIZE : (h + 1) * HEAD_SIZE] = mixed.T.astype(jnp.bfloat16)


def columns_of(info_ref, w_ref, ahead):
    at = lax.rem(info_ref[2] + ahead, 8) * FEATURES
    return w_ref[:, pl.ds(pl.multiple_of(at, FEATURES), FEATURES)]


def project_kernel(aheads, info_ref, att_ref, w_ref, *out_refs):
    attended = att_ref[...]
    for n, ahead in enumerate(aheads):
        ref = out_refs[n * len(out_refs) // len(aheads)]
        ref[n % ref.shape[0]] = dot(attended, columns_of(info_ref, w_ref, ahead)).astype(ref.dtype)


def project(aheads, info, attended, out_weight, outs):
    def kernel(*refs):
        project_kernel(aheads, *refs)

    return pl.pallas_call(
        kernel,
        in_specs=[SMEM, VMEM, VMEM],
        out_specs=[VMEM] * len(outs),
        out_shape=outs,
        compiler_params=params(14),
        cost_estimate=cost(2 * len(aheads) * TOK * QROWS * FEATURES, len(aheads) * QROWS * FEATURES * 2),
    )(info, attended, out_weight)


def cotangent(aheads, info, pieces, start, out_weight, dtype):
    def kernel(info_ref, *refs):
        w_ref, out_ref = refs[-2], refs[-1]
        total = None if start is None else refs[len(pieces)][...]
        n = 0
        for ref in refs[: len(pieces)]:
            for j in range(ref.shape[0] // TOK):
                part = dot_nt(columns_of(info_ref, w_ref, aheads[n]), ref[j * TOK : (j + 1) * TOK, :])
                total = part if total is None else total + part
                n = n + 1
        out_ref[...] = total.astype(out_ref.dtype)

    operands = list(pieces) + ([] if start is None else [start]) + [out_weight]
    return pl.pallas_call(
        kernel,
        in_specs=[SMEM] + [VMEM] * len(operands),
        out_specs=VMEM,
        out_shape=shaped(QROWS, TOK, dtype=dtype),
        compiler_params=params(14),
        cost_estimate=cost(2 * len(aheads) * TOK * QROWS * FEATURES, len(aheads) * QROWS * FEATURES * 2),
    )(info, *operands)


def chips_on(value, by):
    return lax.ppermute(value, "dp", [(i, (i + 2 * by) % 32) for i in range(32)])


def across(value):
    return lax.ppermute(value, "dp", [(i, i ^ 1) for i in range(32)])


def along_z(value, by):
    return lax.ppermute(value, "tensor", [(i, (i + by) % 8) for i in range(8)])


def wide(value):
    return value.astype(jnp.float32)


def low(value):
    return value.astype(jnp.bfloat16)


def forward(info, queries, ids, own, sib):
    return pl.pallas_call(
        forward_kernel,
        in_specs=[SMEM] + [VMEM] * 12,
        out_specs=[VMEM] * 7,
        out_shape=[
            shaped(TOK, QROWS),
            shaped(HEAD_SIZE, QROWS),
            shaped(1, QROWS, dtype=jnp.float32),
            shaped(1, TOK, dtype=jnp.int32),
            shaped(QROWS, HEAD_SIZE),
            shaped(KEYS, HEAD_SIZE),
            shaped(KEYS, HEAD_SIZE),
        ],
        scratch_shapes=[
            pltpu.VMEM((KEYS, QROWS), jnp.float32),
            pltpu.VMEM((HEAD_SIZE, QROWS), jnp.float32),
            pltpu.VMEM((8, QROWS), jnp.float32),
            pltpu.VMEM((8, QROWS), jnp.float32),
        ],
        compiler_params=params(24),
        cost_estimate=cost(4 * KEYS * QROWS * HEAD_SIZE, 4 << 20, KEYS * QROWS),
    )(info, queries, ids, *own, *sib)


def backward(info, rows, key, value, att_t, grad, log_total, first_row):
    pieces = [shaped(n, TOK, 2 * HEAD_SIZE) for n in HELD]
    outs = pl.pallas_call(
        backward_kernel,
        in_specs=[SMEM] + [VMEM] * 7,
        out_specs=[VMEM] * 11,
        out_shape=[shaped(TOK, QROWS)] + pieces + pieces,
        scratch_shapes=[
            pltpu.VMEM((HEAD_SIZE, QROWS), jnp.bfloat16),
            pltpu.VMEM((QROWS, HEAD_SIZE), jnp.bfloat16),
            pltpu.VMEM((HEAD_SIZE, QROWS), jnp.float32),
            pltpu.VMEM((1, QROWS), jnp.float32),
            pltpu.VMEM((KEYS, 2 * HEAD_SIZE), jnp.bfloat16),
        ],
        compiler_params=params(20),
        cost_estimate=cost(10 * KEYS * QROWS * HEAD_SIZE, 4 << 20, KEYS * QROWS),
    )(info, rows, key, value, att_t, grad, log_total, first_row)
    return outs[0], outs[1:6], outs[6:11]


def per_device(rotated_queries, rotated_keys, value_heads_packed, out_weight, out_cotangent, doc_ids):
    me = lax.axis_index("dp").astype(jnp.int32)
    z = lax.axis_index("tensor").astype(jnp.int32)
    info = jnp.stack([me // 2, me % 2, z])
    ids = doc_ids.reshape(1, TOK)

    block = pl.pallas_call(
        pack_kernel,
        in_specs=[VMEM] * 3,
        out_specs=VMEM,
        out_shape=shaped(1, ROWS, 2 * HEAD_SIZE),
        compiler_params=params(2),
    )(rotated_keys, value_heads_packed, ids)
    block_4 = chips_on(block, 4)
    block_8 = chips_on(block, 8)
    z_up, z_down, z_four = along_z(out_cotangent, -1), along_z(out_cotangent, 1), along_z(out_cotangent, 4)
    near = jnp.concatenate([block, block_4], 0)
    own = [near, block_8] + [chips_on(near, by) for by in (1, 2, 3)]
    sib = [across(piece) for piece in own]
    z_far_up = along_z(jnp.concatenate([z_up, z_four], 0), -1)
    z_far_down = along_z(jnp.concatenate([z_down, z_four], 0), 1)

    grad_near = cotangent((0, 1, 7, 4), info, [out_cotangent, z_up, z_down, z_four], None, out_weight, jnp.float32)
    grad_t = cotangent((2, 5, 6, 3), info, [z_far_up, z_far_down], grad_near, out_weight, jnp.bfloat16)

    attended, att_t, log_total, first_row, rows, key, value = forward(info, rotated_queries, ids, own, sib)
    to_up, to_down = project((2, 5, 6, 3), info, attended, out_weight, [shaped(2, TOK, FEATURES)] * 2)
    near_up, near_four, near_down, kept = project(
        (1, 4, 7, 0), info, attended, out_weight, [shaped(1, TOK, FEATURES, dtype=jnp.float32)] * 4
    )
    att_t, to_up, to_down, near_up, near_four, near_down, kept = lax.optimization_barrier(
        (att_t, to_up, to_down, near_up, near_four, near_down, kept)
    )
    got_up = along_z(to_up, 1)
    got_down = along_z(to_down, -1)

    query_grad, grad_own, grad_sib = backward(info, rows, key, value, att_t, grad_t, log_total, first_row)

    sum_up = along_z(low(near_up[0] + wide(got_up[0])), 1)
    sum_four = along_z(low(near_four[0] + wide(got_up[1]) + wide(got_down[1])), 4)
    sum_down = along_z(low(near_down[0] + wide(got_down[0])), -1)
    projected = low(kept[0] + wide(sum_up) + wide(sum_four) + wide(sum_down))

    both = [wide(mine) + wide(across(theirs)) for mine, theirs in zip(grad_own, grad_sib)]
    back = [wide(chips_on(low(both[2 + n]), -(n + 1))) for n in range(3)]
    back_8 = wide(chips_on(low(both[1]), -8))
    near_sum = both[0] + back[0] + back[1] + back[2]
    total = near_sum[0] + back_8[0] + wide(chips_on(low(near_sum[1]), -4))
    total = low(total)
    return projected, query_grad, total[:, :HEAD_SIZE], total[:, HEAD_SIZE:]


def solution(mesh):
    return jax.shard_map(
        per_device,
        mesh=mesh,
        in_specs=(
            P("dp", "tensor"),
            P("dp", "tensor"),
            P("dp", "tensor"),
            P("tensor", None),
            P("dp", "tensor"),
            P("dp"),
        ),
        out_specs=(P("dp", "tensor"), P("dp", "tensor"), P("dp", "tensor"), P("dp", "tensor")),
        check_vma=False,
    )
```

time: 601 us -> 89.6 us (0.15)
  the two profiles are of different devices: /device:TPU:155 before, /device:TPU:8 now
where the time goes in v1:
time: 89.6 us; the launch traced here: 88.2 us
  starting transfers between devices  48.9 us (55%)
  waiting for transfers between devices  17 us (19%)
  Pallas kernels  13.1 us (15%)
  local copies, waits for them, and re-layouts  7.1 us (8%)
  other arithmetic  1.23 us (1%)
    ppermute x10, starting transfers between devices, along_z(): return lax.ppermute(value, 'tensor', [(i, (i + by) % 8) for i in range(8)])  24.9 us
    ppermute x10, starting transfers between devices, chips_on(): lax.ppermute(value, 'dp', [(i, (i + 2 * by) % 32) for i in range(32)])  22 us
    ppermute x10, waiting for transfers between devices, along_z(): return lax.ppermute(value, 'tensor', [(i, (i + by) % 8) for i in range(8)])  13.4 us
    unnamed x16, local copies, waits for them, and re-layouts  6.46 us
    pallas_call x1, Pallas kernels, backward(): pl.pallas_call(backward_kernel, in_specs=[SMEM] + [VMEM] * 7, out_specs=[...  4.15 us
    pallas_call x2, Pallas kernels, cotangent(): pl.pallas_call(kernel, in_specs=[SMEM] + [VMEM] * len(operands), out_spec...  3.56 us
    ppermute x10, waiting for transfers between devices, chips_on(): lax.ppermute(value, 'dp', [(i, (i + 2 * by) % 32) for i in range(32)])  3.3 us
    pallas_call x1, Pallas kernels, forward(): pl.pallas_call(forward_kernel, in_specs=[SMEM] + [VMEM] * 12, out_specs=[...  2.75 us
  transfers between devices with their start and end apart: 30, of which 10 were waited for; matrix products, arithmetic and copies ran while one was open for 1% of the time, Pallas kernels for 8%

profile of v1, /device:TPU:8, one launch (start us, length us, event | category | flops | bytes accessed | tf_op | source)
XLA Modules:
  0.0 88.2 jit_solution(10965869183703712354)
XLA Ops:
  2.9 1.5 %collective-permute-start = (bf16[1,144,256]{2,1,0:T(8,128)(2,1)S(1)}, bf16[1,144,256]{2,1,0:T(8,128)(2,1)S(1)}, u32[]{:S(2)}, u32[]{:S(2)}) collective-permute-start(bf16[1,144,256]{2,1,0:T(8,128)(2,1)S(1)} %shard_map.93), channel_id=1, source_target_pairs={{0,64},{8,72},{16,80},{24,88},{32,96},{40,104},{48,112},{56,120},{... | collective-permute-start | bytes 221192 | tf_op jit(solution)/shard_map/ppermute | solution.py:249
  4.4 2.7 %collective-permute-start.1 = (bf16[1,144,256]{2,1,0:T(8,128)(2,1)S(1)}, bf16[1,144,256]{2,1,0:T(8,128)(2,1)S(1)}, u32[]{:S(2)}, u32[]{:S(2)}) collective-permute-start(bf16[1,144,256]{2,1,0:T(8,128)(2,1)S(1)} %shard_map.93), channel_id=1, source_target_pairs={{0,128},{8,136},{16,144},{24,152},{32,160},{40,168},{48,176},{56,1... | collective-permute-start | bytes 221192 | tf_op jit(solution)/shard_map/ppermute | solution.py:249
  7.1 7.2 %collective-permute-start.16 = (bf16[128,512]{1,0:T(8,128)(2,1)}, bf16[128,512]{1,0:T(8,128)(2,1)S(1)}, u32[]{:S(2)}, u32[]{:S(2)}) collective-permute-start(bf16[128,512]{1,0:T(8,128)(2,1)} %refs_0_.1), channel_id=1, source_target_pairs={{0,4},{1,5},{2,6},{3,7},{4,0},{5,1},{6,2},{7,3},{8,12},{9,13},{10,... | collective-permute-start | bytes 393224 | tf_op jit(solution)/shard_map/ppermute | solution.py:257
  15.4 1.7 %collective-permute-start.2 = (bf16[2,144,256]{2,1,0:T(8,128)(2,1)S(1)}, bf16[2,144,256]{2,1,0:T(8,128)(2,1)S(1)}, u32[]{:S(2)}, u32[]{:S(2)}) collective-permute-start(bf16[2,144,256]{2,1,0:T(8,128)(2,1)S(1)} %pad_maximum_fusion.2.refs_0_), channel_id=1, source_target_pairs={{0,16},{8,24},{16,32},{24,40},{32,48},{40,56},{48,64},{56,72},{64,... | collective-permute-start | bytes 442376 | tf_op jit(solution)/shard_map/ppermute | solution.py:249
  17.8 1.9 %collective-permute-start.4 = (bf16[2,144,256]{2,1,0:T(8,128)(2,1)S(1)}, bf16[2,144,256]{2,1,0:T(8,128)(2,1)S(1)}, u32[]{:S(2)}, u32[]{:S(2)}) collective-permute-start(bf16[2,144,256]{2,1,0:T(8,128)(2,1)S(1)} %pad_maximum_fusion.2.refs_0_), channel_id=1, source_target_pairs={{0,48},{8,56},{16,64},{24,72},{32,80},{40,88},{48,96},{56,104},{64... | collective-permute-start | bytes 442376 | tf_op jit(solution)/shard_map/ppermute | solution.py:249
  20.3 2.7 %collective-permute-start.15 = (bf16[128,512]{1,0:T(8,128)(2,1)}, bf16[128,512]{1,0:T(8,128)(2,1)S(1)}, u32[]{:S(2)}, u32[]{:S(2)}) collective-permute-start(bf16[128,512]{1,0:T(8,128)(2,1)} %refs_0_.1), channel_id=1, source_target_pairs={{0,7},{1,0},{2,1},{3,2},{4,3},{5,4},{6,5},{7,6},{8,15},{9,8},{10,9... | collective-permute-start | bytes 393224 | tf_op jit(solution)/shard_map/ppermute | solution.py:257
  23.1 2.8 %collective-permute-done.15.refs_1_ = bf16[128,512]{1,0:T(8,128)(2,1)S(1)} collective-permute-done((bf16[128,512]{1,0:T(8,128)(2,1)}, bf16[128,512]{1,0:T(8,128)(2,1)S(1)}, u32[]{:S(2)}, u32[]{:S(2)}) %collective-permute-start.15) | collective-permute-done | bytes 131104 | tf_op jit(solution)/shard_map/ppermute | solution.py:257
  26.4 1.6 %collective-permute-done.3.refs_3_ = bf16[2,144,256]{2,1,0:T(8,128)(2,1)S(1)} collective-permute-done((bf16[2,144,256]{2,1,0:T(8,128)(2,1)S(1)}, bf16[2,144,256]{2,1,0:T(8,128)(2,1)S(1)}, u32[]{:S(2)}, u32[]{:S(2)}) %collective-permute-start.3) | collective-permute-done | bytes 147488 | tf_op jit(solution)/shard_map/ppermute | solution.py:249
  28.5 2.3 %collective-permute-start.17 = (bf16[256,512]{1,0:T(8,128)(2,1)S(1)}, bf16[256,512]{1,0:T(8,128)(2,1)S(1)}, u32[]{:S(2)}, u32[]{:S(2)}) collective-permute-start(bf16[256,512]{1,0:T(8,128)(2,1)S(1)} %get-tuple-element.70), channel_id=1, source_target_pairs={{0,7},{1,0},{2,1},{3,2},{4,3},{5,4},{6,5},{7,6},{8,15},{9,8},{10,9... | collective-permute-start | bytes 786440 | tf_op jit(solution)/shard_map/ppermute | solution.py:257
  30.8 3.4 %copy-done = bf16[1024,4096]{1,0:T(8,128)(2,1)S(1)} copy-done((bf16[1024,4096]{1,0:T(8,128)(2,1)S(1)}, bf16[1024,4096]{1,0:T(8,128)(2,1)}, u32[]{:S(2)}) %copy-start) | copy-done | bytes 8388632
  35.1 1.8 %shard_map.97.refs_2_ = f32[1024,128]{1,0:T(8,128)S(1)} custom-call(s32[3]{0:T(128)S(1)} %pad_add_fusion.info_ref.refs_0_, bf16[128,512]{1,0:T(8,128)(2,1)S(1)} %copy-done.2, bf16[128,512]{1,0:T(8,128)(2,1)S(1)} %collective-permute-done.15.refs_1_, bf16[128,512]{1,0:T(8,128)(2,1)S(1)} %collective-permute-done.18.refs_2_, ...), custom_call_target="tpu_custom_call" | custom-call | flops 536870912 | bytes 4194304 | tf_op jit(solution)/shard_map/pallas_call | solution.py:238
  36.9 2.8 %shard_map.94 = (bf16[128,1024]{1,0:T(8,128)(2,1)S(1)}, bf16[128,1024]{1,0:T(8,128)(2,1)S(1)}, f32[1,1024]{1,0:T(1,128)S(1)}, s32[1,128]{1,0:T(1,128)S(1)}, bf16...) custom-call(s32[3]{0:T(128)S(1)} %pad_add_fusion.info_ref.refs_0_, ...), custom_call_target="tpu_custom_call" | custom-call | flops 1207959552 | bytes 4194304 | tf_op jit(solution)/shard_map/pallas_call | solution.py:269
  39.7 1.3 %shard_map.95 = (bf16[2,128,512]{2,1,0:T(8,128)(2,1)S(1)}, bf16[2,128,512]{2,1,0:T(8,128)(2,1)S(1)}) custom-call(s32[3]{0:T(128)S(1)} %pad_add_fusion.info_ref.refs_0_, bf16[128,1024]{1,0:T(8,128)(2,1)S(1)} %get-tuple-element.36.refs_1_, bf16[1024,4096]{1,0:T(8,128)(2,1)S(1)} %copy-done.1), custom_call_target="tpu_custom_call" | custom-call | flops 536870912 | bytes 4194304 | tf_op jit(solution)/shard_map/pallas_call | solution.py:215
  42.3 1.8 %shard_map.98.grad_ref = bf16[1024,128]{1,0:T(8,128)(2,1)S(1)} custom-call(s32[3]{0:T(128)S(1)} %pad_add_fusion.info_ref.refs_0_, bf16[256,512]{1,0:T(8,128)(2,1)S(1)} %collective-permute-done.17.refs_0_, bf16[256,512]{1,0:T(8,128)(2,1)S(1)} %collective-permute-done.19.refs_1_, f32[1024,128]{1,0:T(8,128)S(1)} %shard_map.97.refs_2_, ...), custom_call_target="tpu_custom_call" | custom-call | flops 536870912 | bytes 4194304 | tf_op jit(solution)/shard_map/pallas_call | solution.py:238
  44.1 4.2 %shard_map.99 = (bf16[128,1024]{1,0:T(8,128)(2,1)}, bf16[2,128,256]{2,1,0:T(8,128)(2,1)S(1)}, bf16[1,128,256]{2,1,0:T(8,128)(2,1)S(1)}, bf16[2,128,256]{2,1,0:T(...) custom-call(s32[3]{0:T(128)S(1)} %pad_add_fusion.info_ref.refs_0_, ...), custom_call_target="tpu_custom_call" | custom-call | flops 3019898880 | bytes 4194304 | tf_op jit(solution)/shard_map/pallas_call | solution.py:295
  50.4 1.8 %collective-permute-start.26 = (bf16[2,128,256]{2,1,0:T(8,128)(2,1)S(1)}, bf16[2,128,256]{2,1,0:T(8,128)(2,1)S(1)}, u32[]{:S(2)}, u32[]{:S(2)}) collective-permute-start(bf16[2,128,256]{2,1,0:T(8,128)(2,1)S(1)} %add_convert_fusion), channel_id=1, source_target_pairs={{0,208},{8,216},{16,224},{24,232},{32,240},{40,248},{48,0},{56,8},... | collective-permute-start | bytes 393224 | tf_op jit(solution)/shard_map/ppermute | solution.py:249
  52.2 10.1 %collective-permute-start.24 = (bf16[2,128,256]{2,1,0:T(8,128)(2,1)S(1)}, bf16[2,128,256]{2,1,0:T(8,128)(2,1)S(1)}, u32[]{:S(2)}, u32[]{:S(2)}) collective-permute-start(bf16[2,128,256]{2,1,0:T(8,128)(2,1)S(1)} %add_convert_fusion.1), channel_id=1, source_target_pairs={{0,224},{8,232},{16,240},{24,248},{32,0},{40,8},{48,16},{56,24},{6... | collective-permute-start | bytes 393224 | tf_op jit(solution)/shard_map/ppermute | solution.py:249
  62.6 3.3 %collective-permute-start.12 = (bf16[2,128,512]{2,1,0:T(8,128)(2,1)S(1)}, bf16[2,128,512]{2,1,0:T(8,128)(2,1)S(1)}, u32[]{:S(2)}, u32[]{:S(2)}) collective-permute-start(bf16[2,128,512]{2,1,0:T(8,128)(2,1)S(1)} %get-tuple-element.47), channel_id=1, source_target_pairs={{0,7},{1,0},{2,1},{3,2},{4,3},{5,4},{6,5},{7,6},{8,15},{9,8},{10,9... | collective-permute-start | bytes 786440 | tf_op jit(solution)/shard_map/ppermute | solution.py:257
  66.1 1.6 %collective-permute-done.22 = bf16[2,128,256]{2,1,0:T(8,128)(2,1)S(1)} collective-permute-done((bf16[2,128,256]{2,1,0:T(8,128)(2,1)S(1)}, bf16[2,128,256]{2,1,0:T(8,128)(2,1)S(1)}, u32[]{:S(2)}, u32[]{:S(2)}) %collective-permute-start.22) | collective-permute-done | bytes 131104 | tf_op jit(solution)/shard_map/ppermute | solution.py:249
  67.7 1.4 %collective-permute-start.29 = (bf16[128,256]{1,0:T(8,128)(2,1)S(1)}, bf16[128,256]{1,0:T(8,128)(2,1)S(1)}, u32[]{:S(2)}, u32[]{:S(2)}) collective-permute-start(bf16[128,256]{1,0:T(8,128)(2,1)S(1)} %fusion.9), channel_id=1, source_target_pairs={{0,192},{8,200},{16,208},{24,216},{32,224},{40,232},{48,240},{56,2... | collective-permute-start | bytes 196616 | tf_op jit(solution)/shard_map/ppermute | solution.py:249
  69.2 2.2 %collective-permute-done.12 = bf16[2,128,512]{2,1,0:T(8,128)(2,1)S(1)} collective-permute-done((bf16[2,128,512]{2,1,0:T(8,128)(2,1)S(1)}, bf16[2,128,512]{2,1,0:T(8,128)(2,1)S(1)}, u32[]{:S(2)}, u32[]{:S(2)}) %collective-permute-start.12) | collective-permute-done | bytes 262176 | tf_op jit(solution)/shard_map/ppermute | solution.py:257
  71.5 3.8 %collective-permute-start.14 = (bf16[128,512]{1,0:T(8,128)(2,1)S(1)}, bf16[128,512]{1,0:T(8,128)(2,1)S(1)}, u32[]{:S(2)}, u32[]{:S(2)}) collective-permute-start(bf16[128,512]{1,0:T(8,128)(2,1)S(1)} %get-tuple-element.68), channel_id=1, source_target_pairs={{0,7},{1,0},{2,1},{3,2},{4,3},{5,4},{6,5},{7,6},{8,15},{9,8},{10,9... | collective-permute-start | bytes 393224 | tf_op jit(solution)/shard_map/ppermute | solution.py:257
  75.3 3.8 %collective-permute-start.13 = (bf16[128,512]{1,0:T(8,128)(2,1)S(1)}, bf16[128,512]{1,0:T(8,128)(2,1)S(1)}, u32[]{:S(2)}, u32[]{:S(2)}) collective-permute-start(bf16[128,512]{1,0:T(8,128)(2,1)S(1)} %get-tuple-element.67), channel_id=1, source_target_pairs={{0,4},{1,5},{2,6},{3,7},{4,0},{5,1},{6,2},{7,3},{8,12},{9,13},{10,... | collective-permute-start | bytes 393224 | tf_op jit(solution)/shard_map/ppermute | solution.py:257
  80.9 5.9 %collective-permute-done.13 = bf16[128,512]{1,0:T(8,128)(2,1)S(1)} collective-permute-done((bf16[128,512]{1,0:T(8,128)(2,1)S(1)}, bf16[128,512]{1,0:T(8,128)(2,1)S(1)}, u32[]{:S(2)}, u32[]{:S(2)}) %collective-permute-start.13) | collective-permute-done | bytes 131104 | tf_op jit(solution)/shard_map/ppermute | solution.py:257
  (72 shorter events, 14.2 us)
Async XLA Ops:
  2.9 12.4 %collective-permute-start = (bf16[1,144,256]{2,1,0:T(8,128)(2,1)S(1)}, bf16[1,144,256]{2,1,0:T(8,128)(2,1)S(1)}, u32[]{:S(2)}, u32[]{:S(2)}) collective-permute-start(bf16[1,144,256]{2,1,0:T(8,128)(2,1)S(1)} %shard_map.93), channel_id=1, source_target_pairs={{0,64},{8,72},{16,80},{24,88},{32,96},{40,104},{48,112},{56,120},{... | collective-permute-start | bytes 221192 | tf_op jit(solution)/shard_map/ppermute | solution.py:249
  4.4 13.4 %collective-permute-start.1 = (bf16[1,144,256]{2,1,0:T(8,128)(2,1)S(1)}, bf16[1,144,256]{2,1,0:T(8,128)(2,1)S(1)}, u32[]{:S(2)}, u32[]{:S(2)}) collective-permute-start(bf16[1,144,256]{2,1,0:T(8,128)(2,1)S(1)} %shard_map.93), channel_id=1, source_target_pairs={{0,128},{8,136},{16,144},{24,152},{32,160},{40,168},{48,176},{56,1... | collective-permute-start | bytes 221192 | tf_op jit(solution)/shard_map/ppermute | solution.py:249
  7.1 13.2 %collective-permute-start.16 = (bf16[128,512]{1,0:T(8,128)(2,1)}, bf16[128,512]{1,0:T(8,128)(2,1)S(1)}, u32[]{:S(2)}, u32[]{:S(2)}) collective-permute-start(bf16[128,512]{1,0:T(8,128)(2,1)} %refs_0_.1), channel_id=1, source_target_pairs={{0,4},{1,5},{2,6},{3,7},{4,0},{5,1},{6,2},{7,3},{8,12},{9,13},{10,... | collective-permute-start | bytes 393224 | tf_op jit(solution)/shard_map/ppermute | solution.py:257
  14.3 8.7 %collective-permute-start.18 = (bf16[128,512]{1,0:T(8,128)(2,1)}, bf16[128,512]{1,0:T(8,128)(2,1)S(1)}, u32[]{:S(2)}, u32[]{:S(2)}) collective-permute-start(bf16[128,512]{1,0:T(8,128)(2,1)} %refs_0_.1), channel_id=1, source_target_pairs={{0,1},{1,2},{2,3},{3,4},{4,5},{5,6},{6,7},{7,0},{8,9},{9,10},{10,1... | collective-permute-start | bytes 393224 | tf_op jit(solution)/shard_map/ppermute | solution.py:257
  15.4 10.5 %collective-permute-start.2 = (bf16[2,144,256]{2,1,0:T(8,128)(2,1)S(1)}, bf16[2,144,256]{2,1,0:T(8,128)(2,1)S(1)}, u32[]{:S(2)}, u32[]{:S(2)}) collective-permute-start(bf16[2,144,256]{2,1,0:T(8,128)(2,1)S(1)} %pad_maximum_fusion.2.refs_0_), channel_id=1, source_target_pairs={{0,16},{8,24},{16,32},{24,40},{32,48},{40,56},{48,64},{56,72},{64,... | collective-permute-start | bytes 442376 | tf_op jit(solution)/shard_map/ppermute | solution.py:249
  17.0 10.9 %collective-permute-start.3 = (bf16[2,144,256]{2,1,0:T(8,128)(2,1)S(1)}, bf16[2,144,256]{2,1,0:T(8,128)(2,1)S(1)}, u32[]{:S(2)}, u32[]{:S(2)}) collective-permute-start(bf16[2,144,256]{2,1,0:T(8,128)(2,1)S(1)} %pad_maximum_fusion.2.refs_0_), channel_id=1, source_target_pairs={{0,32},{8,40},{16,48},{24,56},{32,64},{40,72},{48,80},{56,88},{64,... | collective-permute-start | bytes 442376 | tf_op jit(solution)/shard_map/ppermute | solution.py:249
  17.8 10.1 %collective-permute-start.4 = (bf16[2,144,256]{2,1,0:T(8,128)(2,1)S(1)}, bf16[2,144,256]{2,1,0:T(8,128)(2,1)S(1)}, u32[]{:S(2)}, u32[]{:S(2)}) collective-permute-start(bf16[2,144,256]{2,1,0:T(8,128)(2,1)S(1)} %pad_maximum_fusion.2.refs_0_), channel_id=1, source_target_pairs={{0,48},{8,56},{16,64},{24,72},{32,80},{40,88},{48,96},{56,104},{64... | collective-permute-start | bytes 442376 | tf_op jit(solution)/shard_map/ppermute | solution.py:249
  23.0 7.8 %collective-permute-start.5 = (bf16[2,144,256]{2,1,0:T(8,128)(2,1)S(1)}, bf16[2,144,256]{2,1,0:T(8,128)(2,1)S(1)}, u32[]{:S(2)}, u32[]{:S(2)}) collective-permute-start(bf16[2,144,256]{2,1,0:T(8,128)(2,1)S(1)} %pad_maximum_fusion.2.refs_0_), channel_id=1, source_target_pairs={{0,8},{8,0},{16,24},{24,16},{32,40},{40,32},{48,56},{56,48},{64,72... | collective-permute-start | bytes 442376 | tf_op jit(solution)/shard_map/ppermute | solution.py:253
  25.9 11.0 %collective-permute-start.7 = (bf16[2,144,256]{2,1,0:T(8,128)(2,1)S(1)}, bf16[2,144,256]{2,1,0:T(8,128)(2,1)S(1)}, u32[]{:S(2)}, u32[]{:S(2)}) collective-permute-start(bf16[2,144,256]{2,1,0:T(8,128)(2,1)S(1)} %collective-permute-done.2.refs_2_), channel_id=1, source_target_pairs={{0,8},{8,0},{16,24},{24,16},{32,40},{40,32},{48,56},{56,48},{64,72... | collective-permute-start | bytes 442376 | tf_op jit(solution)/shard_map/ppermute | solution.py:253
  28.0 9.0 %collective-permute-start.8 = (bf16[2,144,256]{2,1,0:T(8,128)(2,1)S(1)}, bf16[2,144,256]{2,1,0:T(8,128)(2,1)S(1)}, u32[]{:S(2)}, u32[]{:S(2)}) collective-permute-start(bf16[2,144,256]{2,1,0:T(8,128)(2,1)S(1)} %collective-permute-done.3.refs_3_), channel_id=1, source_target_pairs={{0,8},{8,0},{16,24},{24,16},{32,40},{40,32},{48,56},{56,48},{64,72... | collective-permute-start | bytes 442376 | tf_op jit(solution)/shard_map/ppermute | solution.py:253
  28.0 9.0 %collective-permute-start.9 = (bf16[2,144,256]{2,1,0:T(8,128)(2,1)S(1)}, bf16[2,144,256]{2,1,0:T(8,128)(2,1)S(1)}, u32[]{:S(2)}, u32[]{:S(2)}) collective-permute-start(bf16[2,144,256]{2,1,0:T(8,128)(2,1)S(1)} %collective-permute-done.4.refs_4_), channel_id=1, source_target_pairs={{0,8},{8,0},{16,24},{24,16},{32,40},{40,32},{48,56},{56,48},{64,72... | collective-permute-start | bytes 442376 | tf_op jit(solution)/shard_map/ppermute | solution.py:253
  28.5 13.8 %collective-permute-start.17 = (bf16[256,512]{1,0:T(8,128)(2,1)S(1)}, bf16[256,512]{1,0:T(8,128)(2,1)S(1)}, u32[]{:S(2)}, u32[]{:S(2)}) collective-permute-start(bf16[256,512]{1,0:T(8,128)(2,1)S(1)} %get-tuple-element.70), channel_id=1, source_target_pairs={{0,7},{1,0},{2,1},{3,2},{4,3},{5,4},{6,5},{7,6},{8,15},{9,8},{10,9... | collective-permute-start | bytes 786440 | tf_op jit(solution)/shard_map/ppermute | solution.py:257
  30.8 11.5 %collective-permute-start.19 = (bf16[256,512]{1,0:T(8,128)(2,1)S(1)}, bf16[256,512]{1,0:T(8,128)(2,1)S(1)}, u32[]{:S(2)}, u32[]{:S(2)}) collective-permute-start(bf16[256,512]{1,0:T(8,128)(2,1)S(1)} %get-tuple-element.69), channel_id=1, source_target_pairs={{0,1},{1,2},{2,3},{3,4},{4,5},{5,6},{6,7},{7,0},{8,9},{9,10},{10,1... | collective-permute-start | bytes 786440 | tf_op jit(solution)/shard_map/ppermute | solution.py:257
  48.2 20.9 %collective-permute-start.10 = (bf16[2,128,512]{2,1,0:T(8,128)(2,1)S(1)}, bf16[2,128,512]{2,1,0:T(8,128)(2,1)S(1)}, u32[]{:S(2)}, u32[]{:S(2)}) collective-permute-start(bf16[2,128,512]{2,1,0:T(8,128)(2,1)S(1)} %get-tuple-element.45), channel_id=1, source_target_pairs={{0,1},{1,2},{2,3},{3,4},{4,5},{5,6},{6,7},{7,0},{8,9},{9,10},{10,1... | collective-permute-start | bytes 786440 | tf_op jit(solution)/shard_map/ppermute | solution.py:257
  49.6 13.0 %collective-permute-start.20 = (bf16[2,128,256]{2,1,0:T(8,128)(2,1)S(1)}, bf16[2,128,256]{2,1,0:T(8,128)(2,1)S(1)}, u32[]{:S(2)}, u32[]{:S(2)}) collective-permute-start(bf16[2,128,256]{2,1,0:T(8,128)(2,1)S(1)} %get-tuple-element.57), channel_id=1, source_target_pairs={{0,8},{8,0},{16,24},{24,16},{32,40},{40,32},{48,56},{56,48},{64,72... | collective-permute-start | bytes 393224 | tf_op jit(solution)/shard_map/ppermute | solution.py:253
  49.8 12.6 %collective-permute-start.27 = (bf16[1,128,256]{2,1,0:T(8,128)(2,1)S(1)}, bf16[1,128,256]{2,1,0:T(8,128)(2,1)S(1)}, u32[]{:S(2)}, u32[]{:S(2)}) collective-permute-start(bf16[1,128,256]{2,1,0:T(8,128)(2,1)S(1)} %get-tuple-element.65), channel_id=1, source_target_pairs={{0,8},{8,0},{16,24},{24,16},{32,40},{40,32},{48,56},{56,48},{64,72... | collective-permute-start | bytes 196616 | tf_op jit(solution)/shard_map/ppermute | solution.py:253
  50.4 15.5 %collective-permute-start.26 = (bf16[2,128,256]{2,1,0:T(8,128)(2,1)S(1)}, bf16[2,128,256]{2,1,0:T(8,128)(2,1)S(1)}, u32[]{:S(2)}, u32[]{:S(2)}) collective-permute-start(bf16[2,128,256]{2,1,0:T(8,128)(2,1)S(1)} %add_convert_fusion), channel_id=1, source_target_pairs={{0,208},{8,216},{16,224},{24,232},{32,240},{40,248},{48,0},{56,8},... | collective-permute-start | bytes 393224 | tf_op jit(solution)/shard_map/ppermute | solution.py:249
  52.2 13.8 %collective-permute-start.24 = (bf16[2,128,256]{2,1,0:T(8,128)(2,1)S(1)}, bf16[2,128,256]{2,1,0:T(8,128)(2,1)S(1)}, u32[]{:S(2)}, u32[]{:S(2)}) collective-permute-start(bf16[2,128,256]{2,1,0:T(8,128)(2,1)S(1)} %add_convert_fusion.1), channel_id=1, source_target_pairs={{0,224},{8,232},{16,240},{24,248},{32,0},{40,8},{48,16},{56,24},{6... | collective-permute-start | bytes 393224 | tf_op jit(solution)/shard_map/ppermute | solution.py:249
  62.6 8.7 %collective-permute-start.12 = (bf16[2,128,512]{2,1,0:T(8,128)(2,1)S(1)}, bf16[2,128,512]{2,1,0:T(8,128)(2,1)S(1)}, u32[]{:S(2)}, u32[]{:S(2)}) collective-permute-start(bf16[2,128,512]{2,1,0:T(8,128)(2,1)S(1)} %get-tuple-element.47), channel_id=1, source_target_pairs={{0,7},{1,0},{2,1},{3,2},{4,3},{5,4},{6,5},{7,6},{8,15},{9,8},{10,9... | collective-permute-start | bytes 786440 | tf_op jit(solution)/shard_map/ppermute | solution.py:257
  65.9 13.1 %collective-permute-start.28 = (bf16[1,128,256]{2,1,0:T(8,128)(2,1)S(1)}, bf16[1,128,256]{2,1,0:T(8,128)(2,1)S(1)}, u32[]{:S(2)}, u32[]{:S(2)}) collective-permute-start(bf16[1,128,256]{2,1,0:T(8,128)(2,1)S(1)} %add_convert_fusion.6), channel_id=1, source_target_pairs={{0,128},{8,136},{16,144},{24,152},{32,160},{40,168},{48,176},{56,1... | collective-permute-start | bytes 196616 | tf_op jit(solution)/shard_map/ppermute | solution.py:249
  67.7 11.3 %collective-permute-start.29 = (bf16[128,256]{1,0:T(8,128)(2,1)S(1)}, bf16[128,256]{1,0:T(8,128)(2,1)S(1)}, u32[]{:S(2)}, u32[]{:S(2)}) collective-permute-start(bf16[128,256]{1,0:T(8,128)(2,1)S(1)} %fusion.9), channel_id=1, source_target_pairs={{0,192},{8,200},{16,208},{24,216},{32,224},{40,232},{48,240},{56,2... | collective-permute-start | bytes 196616 | tf_op jit(solution)/shard_map/ppermute | solution.py:249
  71.5 9.4 %collective-permute-start.14 = (bf16[128,512]{1,0:T(8,128)(2,1)S(1)}, bf16[128,512]{1,0:T(8,128)(2,1)S(1)}, u32[]{:S(2)}, u32[]{:S(2)}) collective-permute-start(bf16[128,512]{1,0:T(8,128)(2,1)S(1)} %get-tuple-element.68), channel_id=1, source_target_pairs={{0,7},{1,0},{2,1},{3,2},{4,3},{5,4},{6,5},{7,6},{8,15},{9,8},{10,9... | collective-permute-start | bytes 393224 | tf_op jit(solution)/shard_map/ppermute | solution.py:257
  75.3 11.6 %collective-permute-start.13 = (bf16[128,512]{1,0:T(8,128)(2,1)S(1)}, bf16[128,512]{1,0:T(8,128)(2,1)S(1)}, u32[]{:S(2)}, u32[]{:S(2)}) collective-permute-start(bf16[128,512]{1,0:T(8,128)(2,1)S(1)} %get-tuple-element.67), channel_id=1, source_target_pairs={{0,4},{1,5},{2,6},{3,7},{4,0},{5,1},{6,2},{7,3},{8,12},{9,13},{10,... | collective-permute-start | bytes 393224 | tf_op jit(solution)/shard_map/ppermute | solution.py:257
  79.0 8.5 %collective-permute-start.11 = (bf16[128,512]{1,0:T(8,128)(2,1)S(1)}, bf16[128,512]{1,0:T(8,128)(2,1)S(1)}, u32[]{:S(2)}, u32[]{:S(2)}) collective-permute-start(bf16[128,512]{1,0:T(8,128)(2,1)S(1)} %get-tuple-element.66), channel_id=1, source_target_pairs={{0,1},{1,2},{2,3},{3,4},{4,5},{5,6},{6,7},{7,0},{8,9},{9,10},{10,1... | collective-permute-start | bytes 393224 | tf_op jit(solution)/shard_map/ppermute | solution.py:257
  (14 other events, 100.8 us)

commit v2 on v1

--- a/solution.py
+++ b/solution.py
@@ -25,10 +25,14 @@
 
 VMEM = pl.BlockSpec(memory_space=pltpu.VMEM)
 SMEM = pl.BlockSpec(memory_space=pltpu.SMEM)
+HBM = pl.BlockSpec(memory_space=pltpu.HBM)
 NT = (((1,), (1,)), ((), ()))
 
 PLACE = {0: (0, 0), 4: (0, 1), 8: (1, 0), 1: (2, 0), 5: (2, 1), 2: (3, 0), 6: (3, 1), 3: (4, 0), 7: (4, 1)}
 HELD = (2, 1, 2, 2, 2)
+PROJECT_ORDER = (2, 5, 6, 3, 1, 4, 7, 0)
+GRADIENT_ORDER = (0, 1, 7, 4, 2, 5, 6, 3)
+WEIGHT_FLOPS = 2 * TOK * QROWS * 8 * FEATURES
 
 
 def dot_nt(a, b):
@@ -51,13 +55,31 @@
     return jax.ShapeDtypeStruct(shape, dtype)
 
 
-def pack_kernel(key_ref, value_ref, id_ref, out_ref):
-    out_ref[0, 0:TOK, 0:HEAD_SIZE] = key_ref[...]
-    out_ref[0, 0:TOK, HEAD_SIZE : 2 * HEAD_SIZE] = value_ref[...]
+def pack_kernel(key_ref, value_ref, id_ref, out_ref, ids_ref, sems):
+    places = (out_ref.at[0, 0:TOK, 0:HEAD_SIZE], out_ref.at[0, 0:TOK, HEAD_SIZE : 2 * HEAD_SIZE], ids_ref)
+    copies = [
+        pltpu.make_async_copy(source, place, sems.at[n])
+        for n, (source, place) in enumerate(zip((key_ref, value_ref, id_ref), places))
+    ]
+    for copy in copies:
+        copy.start()
     number = lax.broadcasted_iota(jnp.int32, (DOCS, TOK), 0)
-    below = jnp.where(id_ref[...] < number, 1.0, 0.0)
+    copies[2].wait()
+    below = jnp.where(ids_ref[...] < number, 1.0, 0.0)
     count = jnp.sum(below, axis=1, keepdims=True)
     out_ref[0, TOK:ROWS, :] = jnp.broadcast_to(count, (DOCS, 2 * HEAD_SIZE)).astype(jnp.bfloat16)
+    copies[0].wait()
+    copies[1].wait()
+
+
+def fetch_weight(aheads, z, w_ref, held_ref, sems):
+    copies = []
+    for n, ahead in enumerate(aheads):
+        at = pl.multiple_of(lax.rem(z + ahead, 8) * FEATURES, FEATURES)
+        copies.append(pltpu.make_async_copy(w_ref.at[:, pl.ds(at, FEATURES)], held_ref.at[n], sems.at[n]))
+    for copy in copies:
+        copy.start()
+    return copies
 
 
 def bias_of(base, rows, core, query_pair, first_row):
@@ -74,11 +96,21 @@
     return value.reshape(value.shape[0] // 8, 8, value.shape[1])
 
 
-def forward_kernel(info_ref, q_ref, id_ref, *refs):
+def forward_kernel(info_ref, q_ref, w_ref, id_ref, *refs):
     own, sib, refs = refs[:5], refs[5:10], refs[10:]
-    att_ref, att_t_ref, log_ref, first_ref, rows_ref, key_ref, value_ref = refs[:7]
-    score_ref, acc_ref, max_ref, sum_ref = refs[7:]
+    att_t_ref, log_ref, first_ref, rows_ref, key_ref, value_ref = refs[:6]
+    sends, keeps, refs = refs[6:8], refs[8:12], refs[12:]
+    score_ref, acc_ref, max_ref, sum_ref, att_ref, held_ref, sems, q_sems = refs
     query_pair, core = info_ref[0], info_ref[1]
+    q_copies = [
+        pltpu.make_async_copy(
+            q_ref.at[:, pl.ds(h * HEAD_SIZE, HEAD_SIZE)], rows_ref.at[pl.ds(h * TOK, TOK)], q_sems.at[h]
+        )
+        for h in range(HEADS)
+    ]
+    for copy in q_copies:
+        copy.start()
+    w_copies = fetch_weight(PROJECT_ORDER, info_ref[2], w_ref, held_ref, sems)
     at_own = pl.multiple_of(core * TOK, TOK)
     at_sib = pl.multiple_of((1 - core) * TOK, TOK)
     below = jnp.zeros((DOCS, TOK), jnp.float32)
@@ -90,8 +122,6 @@
             key_ref[pl.ds(j * PAIR + at, TOK), :] = ref[place, 0:TOK, 0:HEAD_SIZE]
             value_ref[pl.ds(j * PAIR + at, TOK), :] = ref[place, 0:TOK, HEAD_SIZE : 2 * HEAD_SIZE]
             below = below + valid * ref[place, TOK:ROWS, 0:TOK].astype(jnp.float32)
-    for h in range(HEADS):
-        rows_ref[h * TOK : (h + 1) * TOK, :] = q_ref[:, h * HEAD_SIZE : (h + 1) * HEAD_SIZE]
     number = lax.broadcasted_iota(jnp.int32, (DOCS, TOK), 0)
     before = jnp.sum(jnp.where(id_ref[...] == number, below, 0.0), axis=0, keepdims=True)
     first_row = before.astype(jnp.int32) + PAIR * jnp.maximum(query_pair - (SLOTS - 1), 0)
@@ -128,6 +158,8 @@
         mix_rows(pl.multiple_of(PAIR + s * STEP, PAIR), STEP)
         return unused
 
+    for copy in q_copies:
+        copy.wait()
     score_rows(0, PAIR, query_pair * PAIR)
     lax.fori_loop(0, live // 2, score_step, 0)
     log_ref[...] = jnp.max(max_ref[...], axis=0, keepdims=True)
@@ -141,19 +173,39 @@
         mixed = acc_ref[:, cols] * inverse[:, cols]
         att_t_ref[:, cols] = mixed.astype(jnp.bfloat16)
         att_ref[:, h * HEAD_SIZE : (h + 1) * HEAD_SIZE] = mixed.T.astype(jnp.bfloat16)
-
-
-def backward_kernel(info_ref, rows_ref, key_ref, value_ref, att_t_ref, grad_ref, log_ref, first_ref, *refs):
-    dq_ref, own, sib, refs = refs[0], refs[1:6], refs[6:11], refs[11:]
-    grad_t_ref, grows_ref, acc_ref, delta_ref, out_ref = refs
+    for n in range(8):
+        w_copies[n].wait()
+        part = dot(att_ref[...], held_ref[n])
+        if n < 4:
+            sends[n // 2][n % 2] = part.astype(jnp.bfloat16)
+        else:
+            keeps[n - 4][...] = part
+
+
+def backward_kernel(info_ref, cot_ref, w_ref, *refs):
+    pieces, refs = refs[:5], refs[5:]
+    rows_ref, key_ref, value_ref, att_t_ref, log_ref, first_ref = refs[:6]
+    dq_ref, own, sib, refs = refs[6], refs[7:12], refs[12:17], refs[17:]
+    grad_ref, grad_t_ref, grows_ref, acc_ref, delta_ref, out_ref, mine_ref, held_ref, sems, cot_sem = refs
     query_pair, core = info_ref[0], info_ref[1]
+    cot_copy = pltpu.make_async_copy(cot_ref, mine_ref, cot_sem)
+    cot_copy.start()
+    w_copies = fetch_weight(GRADIENT_ORDER, info_ref[2], w_ref, held_ref, sems)
     at_own = pl.multiple_of(core * TOK, TOK)
     at_sib = pl.multiple_of((1 - core) * TOK, TOK)
     first_row = first_ref[...]
     live = query_pair - jnp.min(first_row) // PAIR + 1
+    cot_copy.wait()
+    n = 0
+    for ref in (mine_ref,) + pieces:
+        for j in range(ref.shape[0] // TOK):
+            w_copies[n].wait()
+            part = dot_nt(held_ref[n], ref[j * TOK : (j + 1) * TOK, :])
+            grad_ref[...] = part if n == 0 else grad_ref[...] + part
+            n = n + 1
     for h in range(HEADS):
         part = slice(h * TOK, (h + 1) * TOK)
-        grad_t = grad_ref[part, :]
+        grad_t = grad_ref[part, :].astype(jnp.bfloat16)
         grad_t_ref[:, part] = grad_t
         grows_ref[part, :] = grad_t.T
         product = grad_t.astype(jnp.float32) * att_t_ref[:, part].astype(jnp.float32)
@@ -196,55 +248,6 @@
         dq_ref[:, h * HEAD_SIZE : (h + 1) * HEAD_SIZE] = mixed.T.astype(jnp.bfloat16)
 
 
-def columns_of(info_ref, w_ref, ahead):
-    at = lax.rem(info_ref[2] + ahead, 8) * FEATURES
-    return w_ref[:, pl.ds(pl.multiple_of(at, FEATURES), FEATURES)]
-
-
-def project_kernel(aheads, info_ref, att_ref, w_ref, *out_refs):
-    attended = att_ref[...]
-    for n, ahead in enumerate(aheads):
-        ref = out_refs[n * len(out_refs) // len(aheads)]
-        ref[n % ref.shape[0]] = dot(attended, columns_of(info_ref, w_ref, ahead)).astype(ref.dtype)
-
-
-def project(aheads, info, attended, out_weight, outs):
-    def kernel(*refs):
-        project_kernel(aheads, *refs)
-
-    return pl.pallas_call(
-        kernel,
-        in_specs=[SMEM, VMEM, VMEM],
-        out_specs=[VMEM] * len(outs),
-        out_shape=outs,
-        compiler_params=params(14),
-        cost_estimate=cost(2 * len(aheads) * TOK * QROWS * FEATURES, len(aheads) * QROWS * FEATURES * 2),
-    )(info, attended, out_weight)
-
-
-def cotangent(aheads, info, pieces, start, out_weight, dtype):
-    def kernel(info_ref, *refs):
-        w_ref, out_ref = refs[-2], refs[-1]
-        total = None if start is None else refs[len(pieces)][...]
-        n = 0
-        for ref in refs[: len(pieces)]:
-            for j in range(ref.shape[0] // TOK):
-                part = dot_nt(columns_of(info_ref, w_ref, aheads[n]), ref[j * TOK : (j + 1) * TOK, :])
-                total = part if total is None else total + part
-                n = n + 1
-        out_ref[...] = total.astype(out_ref.dtype)
-
-    operands = list(pieces) + ([] if start is None else [start]) + [out_weight]
-    return pl.pallas_call(
-        kernel,
-        in_specs=[SMEM] + [VMEM] * len(operands),
-        out_specs=VMEM,
-        out_shape=shaped(QROWS, TOK, dtype=dtype),
-        compiler_params=params(14),
-        cost_estimate=cost(2 * len(aheads) * TOK * QROWS * FEATURES, len(aheads) * QROWS * FEATURES * 2),
-    )(info, *operands)
-
-
 def chips_on(value, by):
     return lax.ppermute(value, "dp", [(i, (i + 2 * by) % 32) for i in range(32)])
 
@@ -265,48 +268,60 @@
     return value.astype(jnp.bfloat16)
 
 
-def forward(info, queries, ids, own, sib):
-    return pl.pallas_call(
+def forward(info, queries, weight, ids, own, sib):
+    outs = pl.pallas_call(
         forward_kernel,
-        in_specs=[SMEM] + [VMEM] * 12,
-        out_specs=[VMEM] * 7,
+        in_specs=[SMEM, HBM, HBM] + [VMEM] * 11,
+        out_specs=[VMEM] * 12,
         out_shape=[
-            shaped(TOK, QROWS),
             shaped(HEAD_SIZE, QROWS),
             shaped(1, QROWS, dtype=jnp.float32),
             shaped(1, TOK, dtype=jnp.int32),
             shaped(QROWS, HEAD_SIZE),
             shaped(KEYS, HEAD_SIZE),
             shaped(KEYS, HEAD_SIZE),
-        ],
+        ]
+        + [shaped(2, TOK, FEATURES)] * 2
+        + [shaped(TOK, FEATURES, dtype=jnp.float32)] * 4,
         scratch_shapes=[
             pltpu.VMEM((KEYS, QROWS), jnp.float32),
             pltpu.VMEM((HEAD_SIZE, QROWS), jnp.float32),
             pltpu.VMEM((8, QROWS), jnp.float32),
             pltpu.VMEM((8, QROWS), jnp.float32),
+            pltpu.VMEM((TOK, QROWS), jnp.bfloat16),
+            pltpu.VMEM((8, QROWS, FEATURES), jnp.bfloat16),
+            pltpu.SemaphoreType.DMA((8,)),
+            pltpu.SemaphoreType.DMA((HEADS,)),
         ],
-        compiler_params=params(24),
-        cost_estimate=cost(4 * KEYS * QROWS * HEAD_SIZE, 4 << 20, KEYS * QROWS),
-    )(info, queries, ids, *own, *sib)
-
-
-def backward(info, rows, key, value, att_t, grad, log_total, first_row):
-    pieces = [shaped(n, TOK, 2 * HEAD_SIZE) for n in HELD]
+        compiler_params=params(46),
+        cost_estimate=cost(9_000_000_000, 1 << 20),
+    )(info, queries, weight, ids, *own, *sib)
+    return outs[:6], outs[6:8], outs[8:]
+
+
+def backward(info, cotangent, weight, pieces, saved):
+    att_t, log_total, first_row, rows, key, value = saved
+    blocks = [shaped(n, TOK, 2 * HEAD_SIZE) for n in HELD]
     outs = pl.pallas_call(
         backward_kernel,
-        in_specs=[SMEM] + [VMEM] * 7,
+        in_specs=[SMEM, HBM, HBM] + [VMEM] * 11,
         out_specs=[VMEM] * 11,
-        out_shape=[shaped(TOK, QROWS)] + pieces + pieces,
+        out_shape=[shaped(TOK, QROWS)] + blocks + blocks,
         scratch_shapes=[
+            pltpu.VMEM((QROWS, TOK), jnp.float32),
             pltpu.VMEM((HEAD_SIZE, QROWS), jnp.bfloat16),
             pltpu.VMEM((QROWS, HEAD_SIZE), jnp.bfloat16),
             pltpu.VMEM((HEAD_SIZE, QROWS), jnp.float32),
             pltpu.VMEM((1, QROWS), jnp.float32),
             pltpu.VMEM((KEYS, 2 * HEAD_SIZE), jnp.bfloat16),
+            pltpu.VMEM((TOK, FEATURES), jnp.bfloat16),
+            pltpu.VMEM((8, QROWS, FEATURES), jnp.bfloat16),
+            pltpu.SemaphoreType.DMA((8,)),
+            pltpu.SemaphoreType.DMA,
         ],
-        compiler_params=params(20),
-        cost_estimate=cost(10 * KEYS * QROWS * HEAD_SIZE, 4 << 20, KEYS * QROWS),
-    )(info, rows, key, value, att_t, grad, log_total, first_row)
+        compiler_params=params(46),
+        cost_estimate=cost(14_000_000_000, 1 << 20),
+    )(info, cotangent, weight, *pieces, rows, key, value, att_t, log_total, first_row)
     return outs[0], outs[1:6], outs[6:11]
 
 
@@ -314,44 +329,40 @@
     me = lax.axis_index("dp").astype(jnp.int32)
     z = lax.axis_index("tensor").astype(jnp.int32)
     info = jnp.stack([me // 2, me % 2, z])
-    ids = doc_ids.reshape(1, TOK)
-
-    block = pl.pallas_call(
+
+    block, ids = pl.pallas_call(
         pack_kernel,
-        in_specs=[VMEM] * 3,
-        out_specs=VMEM,
-        out_shape=shaped(1, ROWS, 2 * HEAD_SIZE),
+        in_specs=[HBM] * 3,
+        out_specs=[VMEM] * 2,
+        out_shape=[shaped(1, ROWS, 2 * HEAD_SIZE), shaped(1, TOK, dtype=jnp.int32)],
+        scratch_shapes=[pltpu.SemaphoreType.DMA((3,))],
         compiler_params=params(2),
-    )(rotated_keys, value_heads_packed, ids)
+        cost_estimate=cost(1_000_000_000, 1 << 16),
+    )(rotated_keys, value_heads_packed, doc_ids.reshape(1, TOK))
     block_4 = chips_on(block, 4)
     block_8 = chips_on(block, 8)
     z_up, z_down, z_four = along_z(out_cotangent, -1), along_z(out_cotangent, 1), along_z(out_cotangent, 4)
     near = jnp.concatenate([block, block_4], 0)
     own = [near, block_8] + [chips_on(near, by) for by in (1, 2, 3)]
     sib = [across(piece) for piece in own]
+    own, sib, z_up, z_down, z_four = lax.optimization_barrier((own, sib, z_up, z_down, z_four))
     z_far_up = along_z(jnp.concatenate([z_up, z_four], 0), -1)
     z_far_down = along_z(jnp.concatenate([z_down, z_four], 0), 1)
 
-    grad_near = cotangent((0, 1, 7, 4), info, [out_cotangent, z_up, z_down, z_four], None, out_weight, jnp.float32)
-    grad_t = cotangent((2, 5, 6, 3), info, [z_far_up, z_far_down], grad_near, out_weight, jnp.bfloat16)
-
-    attended, att_t, log_total, first_row, rows, key, value = forward(info, rotated_queries, ids, own, sib)
-    to_up, to_down = project((2, 5, 6, 3), info, attended, out_weight, [shaped(2, TOK, FEATURES)] * 2)
-    near_up, near_four, near_down, kept = project(
-        (1, 4, 7, 0), info, attended, out_weight, [shaped(1, TOK, FEATURES, dtype=jnp.float32)] * 4
-    )
-    att_t, to_up, to_down, near_up, near_four, near_down, kept = lax.optimization_barrier(
-        (att_t, to_up, to_down, near_up, near_four, near_down, kept)
+    saved, (to_up, to_down), (near_up, near_four, near_down, kept) = forward(
+        info, rotated_queries, out_weight, ids, own, sib
     )
     got_up = along_z(to_up, 1)
     got_down = along_z(to_down, -1)
 
-    query_grad, grad_own, grad_sib = backward(info, rows, key, value, att_t, grad_t, log_total, first_row)
-
-    sum_up = along_z(low(near_up[0] + wide(got_up[0])), 1)
-    sum_four = along_z(low(near_four[0] + wide(got_up[1]) + wide(got_down[1])), 4)
-    sum_down = along_z(low(near_down[0] + wide(got_down[0])), -1)
-    projected = low(kept[0] + wide(sum_up) + wide(sum_four) + wide(sum_down))
+    pieces = (z_up, z_down, z_four, z_far_up, z_far_down)
+    query_grad, grad_own, grad_sib = backward(info, out_cotangent, out_weight, pieces, saved)
+
+    grad_sib, got_up, got_down = lax.optimization_barrier((grad_sib, got_up, got_down))
+    sum_up = along_z(low(near_up + wide(got_up[0])), 1)
+    sum_four = along_z(low(near_four + wide(got_up[1]) + wide(got_down[1])), 4)
+    sum_down = along_z(low(near_down + wide(got_down[0])), -1)
+    projected = low(kept + wide(sum_up) + wide(sum_four) + wide(sum_down))
 
     both = [wide(mine) + wide(across(theirs)) for mine, theirs in zip(grad_own, grad_sib)]
     back = [wide(chips_on(low(both[2 + n]), -(n + 1))) for n in range(3)]

time: 89.6 us -> 87.8 us (0.980)
  local copies, waits for them, and re-layouts: 7.1 us -> 3.77 us
  Pallas kernels: 13.1 us -> 16.2 us
  waiting for transfers between devices: 17 us -> 14.6 us
  starting transfers between devices: 48.9 us -> 49.8 us
    ppermute x10, waiting for transfers between devices: 13.4 us -> 7.76 us  [along_z(): return lax.ppermute(value, 'tensor', [(i, (i + by) % 8) for i in range(8)])]
    ppermute x10, starting transfers between devices: 22 us -> 26.1 us  [chips_on(): lax.ppermute(value, 'dp', [(i, (i + 2 * by) % 32) for i in range(32)])]
    ppermute x10, starting transfers between devices: 24.9 us -> 21.1 us  [along_z(): return lax.ppermute(value, 'tensor', [(i, (i + by) % 8) for i in range(8)])]
    unnamed x16 -> x11, local copies, waits for them, and re-layouts: 6.46 us -> 3.12 us
    pallas_call x7 -> x3, Pallas kernels: 13.1 us -> 16.2 us  [the longest x1 10.5 us: backward(): pl.pallas_call(backward_kernel, in_specs=[SMEM, HBM, HBM] + [VMEM] * 11,...]
    ppermute x10, waiting for transfers between devices: 0.31 us -> 2.26 us  [across(): return lax.ppermute(value, 'dp', [(i, i ^ 1) for i in range(32)])]
    ppermute x10, waiting for transfers between devices: 3.3 us -> 4.58 us  [chips_on(): lax.ppermute(value, 'dp', [(i, (i + 2 * by) % 32) for i in range(32)])]
  transfers between devices with their start and end apart: 30 -> 30, of which waited for: 10 -> 9; matrix products, arithmetic and copies ran while one was open for 1% -> 1% of each run, Pallas kernels for 8% -> 19%
where the time goes in v2:
time: 87.8 us; the launch traced here: 86.4 us
  starting transfers between devices  49.8 us (57%)
  Pallas kernels  16.2 us (18%)
  waiting for transfers between devices  14.6 us (17%)
  local copies, waits for them, and re-layouts  3.77 us (4%)
  other arithmetic  1.22 us (1%)
    ppermute x10, starting transfers between devices, chips_on(): lax.ppermute(value, 'dp', [(i, (i + 2 * by) % 32) for i in range(32)])  26.1 us
    ppermute x10, starting transfers between devices, along_z(): return lax.ppermute(value, 'tensor', [(i, (i + by) % 8) for i in range(8)])  21.1 us
    pallas_call x1, Pallas kernels, backward(): pl.pallas_call(backward_kernel, in_specs=[SMEM, HBM, HBM] + [VMEM] * 11,...  10.5 us
    ppermute x10, waiting for transfers between devices, along_z(): return lax.ppermute(value, 'tensor', [(i, (i + by) % 8) for i in range(8)])  7.76 us
    pallas_call x1, Pallas kernels, forward(): pl.pallas_call(forward_kernel, in_specs=[SMEM, HBM, HBM] + [VMEM] * 11, o...  5.53 us
    ppermute x10, waiting for transfers between devices, chips_on(): lax.ppermute(value, 'dp', [(i, (i + 2 * by) % 32) for i in range(32)])  4.58 us
    unnamed x11, local copies, waits for them, and re-layouts  3.12 us
    ppermute x10, starting transfers between devices, across(): return lax.ppermute(value, 'dp', [(i, i ^ 1) for i in range(32)])  2.57 us
  transfers between devices with their start and end apart: 30, of which 9 were waited for; matrix products, arithmetic and copies ran while one was open for 1% of the time, Pallas kernels for 19%

profile of v2, /device:TPU:8, one launch (start us, length us, event | category | flops | bytes accessed | tf_op | source)
XLA Modules:
  0.0 86.4 jit_solution(5328016581586085800)
XLA Ops:
  0.6 0.7 copy-done.2
  1.4 0.8 copy-done.3
  2.2 0.7 copy-done.4
  2.9 3.1 %collective-permute-start.1 = (bf16[1,144,256]{2,1,0:T(8,128)(2,1)S(1)}, bf16[1,144,256]{2,1,0:T(8,128)(2,1)S(1)}, u32[]{:S(2)}, u32[]{:S(2)}) collective-permute-start(bf16[1,144,256]{2,1,0:T(8,128)(2,1)S(1)} %get-tuple-element.50), channel_id=1, source_target_pairs={{0,128},{8,136},{16,144},{24,152},{32,160},{40,168},{48,176},{56,1... | collective-permute-start | bytes 221192 | tf_op jit(solution)/shard_map/ppermute | solution.py:252
  6.6 1.9 %collective-permute-start.11 = (bf16[128,512]{1,0:T(8,128)(2,1)}, bf16[128,512]{1,0:T(8,128)(2,1)S(1)}, u32[]{:S(2)}, u32[]{:S(2)}) collective-permute-start(bf16[128,512]{1,0:T(8,128)(2,1)} %cot_ref.1), channel_id=1, source_target_pairs={{0,1},{1,2},{2,3},{3,4},{4,5},{5,6},{6,7},{7,0},{8,9},{9,10},{10,1... | collective-permute-start | bytes 393224 | tf_op jit(solution)/shard_map/ppermute | solution.py:260
  8.6 3.0 %collective-permute-done = bf16[1,144,256]{2,1,0:T(8,128)(2,1)S(1)} collective-permute-done((bf16[1,144,256]{2,1,0:T(8,128)(2,1)S(1)}, bf16[1,144,256]{2,1,0:T(8,128)(2,1)S(1)}, u32[]{:S(2)}, u32[]{:S(2)}) %collective-permute-start) | collective-permute-done | bytes 73760 | tf_op jit(solution)/shard_map/ppermute | solution.py:252
  11.6 2.5 %collective-permute-start.3 = (bf16[2,144,256]{2,1,0:T(8,128)(2,1)S(1)}, bf16[2,144,256]{2,1,0:T(8,128)(2,1)S(1)}, u32[]{:S(2)}, u32[]{:S(2)}) collective-permute-start(bf16[2,144,256]{2,1,0:T(8,128)(2,1)S(1)} %constant_dynamic-update-slice_fusion.refs_0_), channel_id=1, source_target_pairs={{0,32},{8,40},{16,48},{24,56},{32,64},{40,72},{48,80},{56,88},{64,... | collective-permute-start | bytes 442376 | tf_op jit(solution)/shard_map/ppermute | solution.py:252
  14.1 1.9 %collective-permute-start.2 = (bf16[2,144,256]{2,1,0:T(8,128)(2,1)S(1)}, bf16[2,144,256]{2,1,0:T(8,128)(2,1)S(1)}, u32[]{:S(2)}, u32[]{:S(2)}) collective-permute-start(bf16[2,144,256]{2,1,0:T(8,128)(2,1)S(1)} %constant_dynamic-update-slice_fusion.refs_0_), channel_id=1, source_target_pairs={{0,16},{8,24},{16,32},{24,40},{32,48},{40,56},{48,64},{56,72},{64,... | collective-permute-start | bytes 442376 | tf_op jit(solution)/shard_map/ppermute | solution.py:252
  16.0 5.9 %collective-permute-start.10 = (bf16[128,512]{1,0:T(8,128)(2,1)}, bf16[128,512]{1,0:T(8,128)(2,1)S(1)}, u32[]{:S(2)}, u32[]{:S(2)}) collective-permute-start(bf16[128,512]{1,0:T(8,128)(2,1)} %cot_ref.1), channel_id=1, source_target_pairs={{0,7},{1,0},{2,1},{3,2},{4,3},{5,4},{6,5},{7,6},{8,15},{9,8},{10,9... | collective-permute-start | bytes 393224 | tf_op jit(solution)/shard_map/ppermute | solution.py:260
  21.9 1.4 %collective-permute-start.12 = (bf16[128,512]{1,0:T(8,128)(2,1)}, bf16[128,512]{1,0:T(8,128)(2,1)S(1)}, u32[]{:S(2)}, u32[]{:S(2)}) collective-permute-start(bf16[128,512]{1,0:T(8,128)(2,1)} %cot_ref.1), channel_id=1, source_target_pairs={{0,4},{1,5},{2,6},{3,7},{4,0},{5,1},{6,2},{7,3},{8,12},{9,13},{10,... | collective-permute-start | bytes 393224 | tf_op jit(solution)/shard_map/ppermute | solution.py:260
  23.3 6.6 %collective-permute-done.10.refs_0_ = bf16[128,512]{1,0:T(8,128)(2,1)S(1)} collective-permute-done((bf16[128,512]{1,0:T(8,128)(2,1)}, bf16[128,512]{1,0:T(8,128)(2,1)S(1)}, u32[]{:S(2)}, u32[]{:S(2)}) %collective-permute-start.10) | collective-permute-done | bytes 131104 | tf_op jit(solution)/shard_map/ppermute | solution.py:260
  30.9 1.2 %collective-permute-done.12.refs_2_ = bf16[128,512]{1,0:T(8,128)(2,1)S(1)} collective-permute-done((bf16[128,512]{1,0:T(8,128)(2,1)}, bf16[128,512]{1,0:T(8,128)(2,1)S(1)}, u32[]{:S(2)}, u32[]{:S(2)}) %collective-permute-start.12) | collective-permute-done | bytes 131104 | tf_op jit(solution)/shard_map/ppermute | solution.py:260
  32.2 1.2 %collective-permute-done.6.refs_6_ = bf16[1,144,256]{2,1,0:T(8,128)(2,1)S(1)} collective-permute-done((bf16[1,144,256]{2,1,0:T(8,128)(2,1)S(1)}, bf16[1,144,256]{2,1,0:T(8,128)(2,1)S(1)}, u32[]{:S(2)}, u32[]{:S(2)}) %collective-permute-start.6) | collective-permute-done | bytes 73760 | tf_op jit(solution)/shard_map/ppermute | solution.py:256
  33.9 2.9 %collective-permute-start.13 = (bf16[256,512]{1,0:T(8,128)(2,1)S(1)}, bf16[256,512]{1,0:T(8,128)(2,1)S(1)}, u32[]{:S(2)}, u32[]{:S(2)}) collective-permute-start(bf16[256,512]{1,0:T(8,128)(2,1)S(1)} %get-tuple-element.98), channel_id=1, source_target_pairs={{0,7},{1,0},{2,1},{3,2},{4,3},{5,4},{6,5},{7,6},{8,15},{9,8},{10,9... | collective-permute-start | bytes 786440 | tf_op jit(solution)/shard_map/ppermute | solution.py:260
  36.7 0.9 %copy-done = bf16[128,1024]{1,0:T(8,128)(2,1)S(1)} copy-done((bf16[128,1024]{1,0:T(8,128)(2,1)S(1)}, bf16[128,1024]{1,0:T(8,128)(2,1)}, u32[]{:S(2)}) %copy-start) | copy-done | bytes 262168
  37.7 5.5 %shard_map.94 = (bf16[128,1024]{1,0:T(8,128)(2,1)S(1)}, f32[1,1024]{1,0:T(1,128)S(1)}, s32[1,128]{1,0:T(1,128)S(1)}, bf16[1024,128]{1,0:T(8,128)(2,1)S(1)}, bf16...) custom-call(s32[3]{0:T(128)S(1)} %pad_add_fusion.info_ref, ...), custom_call_target="tpu_custom_call" | custom-call | flops 8999999488 | bytes 1048576 | tf_op jit(solution)/shard_map/pallas_call | solution.py:272
  43.3 3.2 %collective-permute-start.16 = (bf16[2,128,512]{2,1,0:T(8,128)(2,1)S(1)}, bf16[2,128,512]{2,1,0:T(8,128)(2,1)S(1)}, u32[]{:S(2)}, u32[]{:S(2)}) collective-permute-start(bf16[2,128,512]{2,1,0:T(8,128)(2,1)S(1)} %get-tuple-element.78), channel_id=1, source_target_pairs={{0,7},{1,0},{2,1},{3,2},{4,3},{5,4},{6,5},{7,6},{8,15},{9,8},{10,9... | collective-permute-start | bytes 786440 | tf_op jit(solution)/shard_map/ppermute | solution.py:260
  46.6 10.5 %shard_map.95 = (bf16[128,1024]{1,0:T(8,128)(2,1)}, bf16[2,128,256]{2,1,0:T(8,128)(2,1)S(1)}, bf16[1,128,256]{2,1,0:T(8,128)(2,1)S(1)}, bf16[2,128,256]{2,1,0:T(...) custom-call(s32[3]{0:T(128)S(1)} %pad_add_fusion.info_ref, ...), custom_call_target="tpu_custom_call" | custom-call | flops 14000000000 | bytes 1048576 | tf_op jit(solution)/shard_map/pallas_call | solution.py:305
  60.0 11.1 %collective-permute-start.24 = (bf16[2,128,256]{2,1,0:T(8,128)(2,1)S(1)}, bf16[2,128,256]{2,1,0:T(8,128)(2,1)S(1)}, u32[]{:S(2)}, u32[]{:S(2)}) collective-permute-start(bf16[2,128,256]{2,1,0:T(8,128)(2,1)S(1)} %add_convert_fusion.1), channel_id=1, source_target_pairs={{0,224},{8,232},{16,240},{24,248},{32,0},{40,8},{48,16},{56,24},{6... | collective-permute-start | bytes 393224 | tf_op jit(solution)/shard_map/ppermute | solution.py:252
  71.7 2.1 %collective-permute-start.18 = (bf16[128,512]{1,0:T(8,128)(2,1)S(1)}, bf16[128,512]{1,0:T(8,128)(2,1)S(1)}, u32[]{:S(2)}, u32[]{:S(2)}) collective-permute-start(bf16[128,512]{1,0:T(8,128)(2,1)S(1)} %get-tuple-element.95), channel_id=1, source_target_pairs={{0,4},{1,5},{2,6},{3,7},{4,0},{5,1},{6,2},{7,3},{8,12},{9,13},{10,... | collective-permute-start | bytes 393224 | tf_op jit(solution)/shard_map/ppermute | solution.py:260
  73.8 3.1 %collective-permute-start.19 = (bf16[128,512]{1,0:T(8,128)(2,1)S(1)}, bf16[128,512]{1,0:T(8,128)(2,1)S(1)}, u32[]{:S(2)}, u32[]{:S(2)}) collective-permute-start(bf16[128,512]{1,0:T(8,128)(2,1)S(1)} %get-tuple-element.96), channel_id=1, source_target_pairs={{0,7},{1,0},{2,1},{3,2},{4,3},{5,4},{6,5},{7,6},{8,15},{9,8},{10,9... | collective-permute-start | bytes 393224 | tf_op jit(solution)/shard_map/ppermute | solution.py:260
  77.4 6.4 %collective-permute-start.29 = (bf16[128,256]{1,0:T(8,128)(2,1)S(1)}, bf16[128,256]{1,0:T(8,128)(2,1)S(1)}, u32[]{:S(2)}, u32[]{:S(2)}) collective-permute-start(bf16[128,256]{1,0:T(8,128)(2,1)S(1)} %fusion.6), channel_id=1, source_target_pairs={{0,192},{8,200},{16,208},{24,216},{32,224},{40,232},{48,240},{56,2... | collective-permute-start | bytes 196616 | tf_op jit(solution)/shard_map/ppermute | solution.py:252
  83.8 0.7 add_convert_fusion.3
  84.6 1.2 %collective-permute-done.29 = bf16[128,256]{1,0:T(8,128)(2,1)S(1)} collective-permute-done((bf16[128,256]{1,0:T(8,128)(2,1)S(1)}, bf16[128,256]{1,0:T(8,128)(2,1)S(1)}, u32[]{:S(2)}, u32[]{:S(2)}) %collective-permute-start.29) | collective-permute-done | bytes 65568 | tf_op jit(solution)/shard_map/ppermute | solution.py:252
  (63 shorter events, 7.0 us)
Async XLA Ops:
  2.9 13.1 %collective-permute-start.1 = (bf16[1,144,256]{2,1,0:T(8,128)(2,1)S(1)}, bf16[1,144,256]{2,1,0:T(8,128)(2,1)S(1)}, u32[]{:S(2)}, u32[]{:S(2)}) collective-permute-start(bf16[1,144,256]{2,1,0:T(8,128)(2,1)S(1)} %get-tuple-element.50), channel_id=1, source_target_pairs={{0,128},{8,136},{16,144},{24,152},{32,160},{40,168},{48,176},{56,1... | collective-permute-start | bytes 221192 | tf_op jit(solution)/shard_map/ppermute | solution.py:252
  6.1 5.6 %collective-permute-start = (bf16[1,144,256]{2,1,0:T(8,128)(2,1)S(1)}, bf16[1,144,256]{2,1,0:T(8,128)(2,1)S(1)}, u32[]{:S(2)}, u32[]{:S(2)}) collective-permute-start(bf16[1,144,256]{2,1,0:T(8,128)(2,1)S(1)} %get-tuple-element.50), channel_id=1, source_target_pairs={{0,64},{8,72},{16,80},{24,88},{32,96},{40,104},{48,112},{56,120},{... | collective-permute-start | bytes 221192 | tf_op jit(solution)/shard_map/ppermute | solution.py:252
  6.6 15.2 %collective-permute-start.11 = (bf16[128,512]{1,0:T(8,128)(2,1)}, bf16[128,512]{1,0:T(8,128)(2,1)S(1)}, u32[]{:S(2)}, u32[]{:S(2)}) collective-permute-start(bf16[128,512]{1,0:T(8,128)(2,1)} %cot_ref.1), channel_id=1, source_target_pairs={{0,1},{1,2},{2,3},{3,4},{4,5},{5,6},{6,7},{7,0},{8,9},{9,10},{10,1... | collective-permute-start | bytes 393224 | tf_op jit(solution)/shard_map/ppermute | solution.py:260
  11.6 18.3 %collective-permute-start.4 = (bf16[2,144,256]{2,1,0:T(8,128)(2,1)S(1)}, bf16[2,144,256]{2,1,0:T(8,128)(2,1)S(1)}, u32[]{:S(2)}, u32[]{:S(2)}) collective-permute-start(bf16[2,144,256]{2,1,0:T(8,128)(2,1)S(1)} %constant_dynamic-update-slice_fusion.refs_0_), channel_id=1, source_target_pairs={{0,48},{8,56},{16,64},{24,72},{32,80},{40,88},{48,96},{56,104},{64... | collective-permute-start | bytes 442376 | tf_op jit(solution)/shard_map/ppermute | solution.py:252
  11.6 18.8 %collective-permute-start.3 = (bf16[2,144,256]{2,1,0:T(8,128)(2,1)S(1)}, bf16[2,144,256]{2,1,0:T(8,128)(2,1)S(1)}, u32[]{:S(2)}, u32[]{:S(2)}) collective-permute-start(bf16[2,144,256]{2,1,0:T(8,128)(2,1)S(1)} %constant_dynamic-update-slice_fusion.refs_0_), channel_id=1, source_target_pairs={{0,32},{8,40},{16,48},{24,56},{32,64},{40,72},{48,80},{56,88},{64,... | collective-permute-start | bytes 442376 | tf_op jit(solution)/shard_map/ppermute | solution.py:252
  14.1 16.4 %collective-permute-start.2 = (bf16[2,144,256]{2,1,0:T(8,128)(2,1)S(1)}, bf16[2,144,256]{2,1,0:T(8,128)(2,1)S(1)}, u32[]{:S(2)}, u32[]{:S(2)}) collective-permute-start(bf16[2,144,256]{2,1,0:T(8,128)(2,1)S(1)} %constant_dynamic-update-slice_fusion.refs_0_), channel_id=1, source_target_pairs={{0,16},{8,24},{16,32},{24,40},{32,48},{40,56},{48,64},{56,72},{64,... | collective-permute-start | bytes 442376 | tf_op jit(solution)/shard_map/ppermute | solution.py:252
  16.0 13.9 %collective-permute-start.10 = (bf16[128,512]{1,0:T(8,128)(2,1)}, bf16[128,512]{1,0:T(8,128)(2,1)S(1)}, u32[]{:S(2)}, u32[]{:S(2)}) collective-permute-start(bf16[128,512]{1,0:T(8,128)(2,1)} %cot_ref.1), channel_id=1, source_target_pairs={{0,7},{1,0},{2,1},{3,2},{4,3},{5,4},{6,5},{7,6},{8,15},{9,8},{10,9... | collective-permute-start | bytes 393224 | tf_op jit(solution)/shard_map/ppermute | solution.py:260
  21.9 10.2 %collective-permute-start.12 = (bf16[128,512]{1,0:T(8,128)(2,1)}, bf16[128,512]{1,0:T(8,128)(2,1)S(1)}, u32[]{:S(2)}, u32[]{:S(2)}) collective-permute-start(bf16[128,512]{1,0:T(8,128)(2,1)} %cot_ref.1), channel_id=1, source_target_pairs={{0,4},{1,5},{2,6},{3,7},{4,0},{5,1},{6,2},{7,3},{8,12},{9,13},{10,... | collective-permute-start | bytes 393224 | tf_op jit(solution)/shard_map/ppermute | solution.py:260
  29.9 3.5 %collective-permute-start.5 = (bf16[2,144,256]{2,1,0:T(8,128)(2,1)S(1)}, bf16[2,144,256]{2,1,0:T(8,128)(2,1)S(1)}, u32[]{:S(2)}, u32[]{:S(2)}) collective-permute-start(bf16[2,144,256]{2,1,0:T(8,128)(2,1)S(1)} %constant_dynamic-update-slice_fusion.refs_0_), channel_id=1, source_target_pairs={{0,8},{8,0},{16,24},{24,16},{32,40},{40,32},{48,56},{56,48},{64,72... | collective-permute-start | bytes 442376 | tf_op jit(solution)/shard_map/ppermute | solution.py:256
  29.9 3.5 %collective-permute-start.9 = (bf16[2,144,256]{2,1,0:T(8,128)(2,1)S(1)}, bf16[2,144,256]{2,1,0:T(8,128)(2,1)S(1)}, u32[]{:S(2)}, u32[]{:S(2)}) collective-permute-start(bf16[2,144,256]{2,1,0:T(8,128)(2,1)S(1)} %collective-permute-done.4.refs_4_), channel_id=1, source_target_pairs={{0,8},{8,0},{16,24},{24,16},{32,40},{40,32},{48,56},{56,48},{64,72... | collective-permute-start | bytes 442376 | tf_op jit(solution)/shard_map/ppermute | solution.py:256
  33.4 13.1 %collective-permute-start.14 = (bf16[256,512]{1,0:T(8,128)(2,1)S(1)}, bf16[256,512]{1,0:T(8,128)(2,1)S(1)}, u32[]{:S(2)}, u32[]{:S(2)}) collective-permute-start(bf16[256,512]{1,0:T(8,128)(2,1)S(1)} %get-tuple-element.97), channel_id=1, source_target_pairs={{0,1},{1,2},{2,3},{3,4},{4,5},{5,6},{6,7},{7,0},{8,9},{9,10},{10,1... | collective-permute-start | bytes 786440 | tf_op jit(solution)/shard_map/ppermute | solution.py:260
  33.9 12.7 %collective-permute-start.13 = (bf16[256,512]{1,0:T(8,128)(2,1)S(1)}, bf16[256,512]{1,0:T(8,128)(2,1)S(1)}, u32[]{:S(2)}, u32[]{:S(2)}) collective-permute-start(bf16[256,512]{1,0:T(8,128)(2,1)S(1)} %get-tuple-element.98), channel_id=1, source_target_pairs={{0,7},{1,0},{2,1},{3,2},{4,3},{5,4},{6,5},{7,6},{8,15},{9,8},{10,9... | collective-permute-start | bytes 786440 | tf_op jit(solution)/shard_map/ppermute | solution.py:260
  43.2 13.8 %collective-permute-start.15 = (bf16[2,128,512]{2,1,0:T(8,128)(2,1)S(1)}, bf16[2,128,512]{2,1,0:T(8,128)(2,1)S(1)}, u32[]{:S(2)}, u32[]{:S(2)}) collective-permute-start(bf16[2,128,512]{2,1,0:T(8,128)(2,1)S(1)} %get-tuple-element.77), channel_id=1, source_target_pairs={{0,1},{1,2},{2,3},{3,4},{4,5},{5,6},{6,7},{7,0},{8,9},{9,10},{10,1... | collective-permute-start | bytes 786440 | tf_op jit(solution)/shard_map/ppermute | solution.py:260
  43.3 13.8 %collective-permute-start.16 = (bf16[2,128,512]{2,1,0:T(8,128)(2,1)S(1)}, bf16[2,128,512]{2,1,0:T(8,128)(2,1)S(1)}, u32[]{:S(2)}, u32[]{:S(2)}) collective-permute-start(bf16[2,128,512]{2,1,0:T(8,128)(2,1)S(1)} %get-tuple-element.78), channel_id=1, source_target_pairs={{0,7},{1,0},{2,1},{3,2},{4,3},{5,4},{6,5},{7,6},{8,15},{9,8},{10,9... | collective-permute-start | bytes 786440 | tf_op jit(solution)/shard_map/ppermute | solution.py:260
  57.1 14.1 %collective-permute-start.27 = (bf16[1,128,256]{2,1,0:T(8,128)(2,1)S(1)}, bf16[1,128,256]{2,1,0:T(8,128)(2,1)S(1)}, u32[]{:S(2)}, u32[]{:S(2)}) collective-permute-start(bf16[1,128,256]{2,1,0:T(8,128)(2,1)S(1)} %get-tuple-element.93), channel_id=1, source_target_pairs={{0,8},{8,0},{16,24},{24,16},{32,40},{40,32},{48,56},{56,48},{64,72... | collective-permute-start | bytes 196616 | tf_op jit(solution)/shard_map/ppermute | solution.py:256
  57.8 26.0 %collective-permute-start.17 = (bf16[128,512]{1,0:T(8,128)(2,1)S(1)}, bf16[128,512]{1,0:T(8,128)(2,1)S(1)}, u32[]{:S(2)}, u32[]{:S(2)}) collective-permute-start(bf16[128,512]{1,0:T(8,128)(2,1)S(1)} %get-tuple-element.94), channel_id=1, source_target_pairs={{0,1},{1,2},{2,3},{3,4},{4,5},{5,6},{6,7},{7,0},{8,9},{9,10},{10,1... | collective-permute-start | bytes 393224 | tf_op jit(solution)/shard_map/ppermute | solution.py:260
  57.9 13.8 %collective-permute-start.20 = (bf16[2,128,256]{2,1,0:T(8,128)(2,1)S(1)}, bf16[2,128,256]{2,1,0:T(8,128)(2,1)S(1)}, u32[]{:S(2)}, u32[]{:S(2)}) collective-permute-start(bf16[2,128,256]{2,1,0:T(8,128)(2,1)S(1)} %get-tuple-element.85), channel_id=1, source_target_pairs={{0,8},{8,0},{16,24},{24,16},{32,40},{40,32},{48,56},{56,48},{64,72... | collective-permute-start | bytes 393224 | tf_op jit(solution)/shard_map/ppermute | solution.py:256
  59.6 14.3 %collective-permute-start.22 = (bf16[2,128,256]{2,1,0:T(8,128)(2,1)S(1)}, bf16[2,128,256]{2,1,0:T(8,128)(2,1)S(1)}, u32[]{:S(2)}, u32[]{:S(2)}) collective-permute-start(bf16[2,128,256]{2,1,0:T(8,128)(2,1)S(1)} %add_convert_fusion.2), channel_id=1, source_target_pairs={{0,240},{8,248},{16,0},{24,8},{32,16},{40,24},{48,32},{56,40},{64,... | collective-permute-start | bytes 393224 | tf_op jit(solution)/shard_map/ppermute | solution.py:252
  60.0 16.9 %collective-permute-start.24 = (bf16[2,128,256]{2,1,0:T(8,128)(2,1)S(1)}, bf16[2,128,256]{2,1,0:T(8,128)(2,1)S(1)}, u32[]{:S(2)}, u32[]{:S(2)}) collective-permute-start(bf16[2,128,256]{2,1,0:T(8,128)(2,1)S(1)} %add_convert_fusion.1), channel_id=1, source_target_pairs={{0,224},{8,232},{16,240},{24,248},{32,0},{40,8},{48,16},{56,24},{6... | collective-permute-start | bytes 393224 | tf_op jit(solution)/shard_map/ppermute | solution.py:252
  71.2 6.1 %collective-permute-start.26 = (bf16[2,128,256]{2,1,0:T(8,128)(2,1)S(1)}, bf16[2,128,256]{2,1,0:T(8,128)(2,1)S(1)}, u32[]{:S(2)}, u32[]{:S(2)}) collective-permute-start(bf16[2,128,256]{2,1,0:T(8,128)(2,1)S(1)} %add_convert_fusion), channel_id=1, source_target_pairs={{0,208},{8,216},{16,224},{24,232},{32,240},{40,248},{48,0},{56,8},... | collective-permute-start | bytes 393224 | tf_op jit(solution)/shard_map/ppermute | solution.py:252
  71.7 12.1 %collective-permute-start.18 = (bf16[128,512]{1,0:T(8,128)(2,1)S(1)}, bf16[128,512]{1,0:T(8,128)(2,1)S(1)}, u32[]{:S(2)}, u32[]{:S(2)}) collective-permute-start(bf16[128,512]{1,0:T(8,128)(2,1)S(1)} %get-tuple-element.95), channel_id=1, source_target_pairs={{0,4},{1,5},{2,6},{3,7},{4,0},{5,1},{6,2},{7,3},{8,12},{9,13},{10,... | collective-permute-start | bytes 393224 | tf_op jit(solution)/shard_map/ppermute | solution.py:260
  73.8 10.0 %collective-permute-start.19 = (bf16[128,512]{1,0:T(8,128)(2,1)S(1)}, bf16[128,512]{1,0:T(8,128)(2,1)S(1)}, u32[]{:S(2)}, u32[]{:S(2)}) collective-permute-start(bf16[128,512]{1,0:T(8,128)(2,1)S(1)} %get-tuple-element.96), channel_id=1, source_target_pairs={{0,7},{1,0},{2,1},{3,2},{4,3},{5,4},{6,5},{7,6},{8,15},{9,8},{10,9... | collective-permute-start | bytes 393224 | tf_op jit(solution)/shard_map/ppermute | solution.py:260
  77.0 7.6 %collective-permute-start.28 = (bf16[1,128,256]{2,1,0:T(8,128)(2,1)S(1)}, bf16[1,128,256]{2,1,0:T(8,128)(2,1)S(1)}, u32[]{:S(2)}, u32[]{:S(2)}) collective-permute-start(bf16[1,128,256]{2,1,0:T(8,128)(2,1)S(1)} %add_convert_fusion.4), channel_id=1, source_target_pairs={{0,128},{8,136},{16,144},{24,152},{32,160},{40,168},{48,176},{56,1... | collective-permute-start | bytes 196616 | tf_op jit(solution)/shard_map/ppermute | solution.py:252
  77.4 8.3 %collective-permute-start.29 = (bf16[128,256]{1,0:T(8,128)(2,1)S(1)}, bf16[128,256]{1,0:T(8,128)(2,1)S(1)}, u32[]{:S(2)}, u32[]{:S(2)}) collective-permute-start(bf16[128,256]{1,0:T(8,128)(2,1)S(1)} %fusion.6), channel_id=1, source_target_pairs={{0,192},{8,200},{16,208},{24,216},{32,224},{40,232},{48,240},{56,2... | collective-permute-start | bytes 196616 | tf_op jit(solution)/shard_map/ppermute | solution.py:252
  (11 other events, 23.4 us)

commit v3 on v2

--- a/solution.py
+++ b/solution.py
@@ -30,9 +30,9 @@
 
 PLACE = {0: (0, 0), 4: (0, 1), 8: (1, 0), 1: (2, 0), 5: (2, 1), 2: (3, 0), 6: (3, 1), 3: (4, 0), 7: (4, 1)}
 HELD = (2, 1, 2, 2, 2)
-PROJECT_ORDER = (2, 5, 6, 3, 1, 4, 7, 0)
-GRADIENT_ORDER = (0, 1, 7, 4, 2, 5, 6, 3)
-WEIGHT_FLOPS = 2 * TOK * QROWS * 8 * FEATURES
+PART_ORDER = (2, 5, 6, 3, 1, 4, 7, 0)
+FORWARD_MIB = 40
+BACKWARD_MIB = 36
 
 
 def dot_nt(a, b):
@@ -55,28 +55,19 @@
     return jax.ShapeDtypeStruct(shape, dtype)
 
 
-def pack_kernel(key_ref, value_ref, id_ref, out_ref, ids_ref, sems):
-    places = (out_ref.at[0, 0:TOK, 0:HEAD_SIZE], out_ref.at[0, 0:TOK, HEAD_SIZE : 2 * HEAD_SIZE], ids_ref)
-    copies = [
-        pltpu.make_async_copy(source, place, sems.at[n])
-        for n, (source, place) in enumerate(zip((key_ref, value_ref, id_ref), places))
-    ]
-    for copy in copies:
-        copy.start()
-    number = lax.broadcasted_iota(jnp.int32, (DOCS, TOK), 0)
-    copies[2].wait()
-    below = jnp.where(ids_ref[...] < number, 1.0, 0.0)
-    count = jnp.sum(below, axis=1, keepdims=True)
-    out_ref[0, TOK:ROWS, :] = jnp.broadcast_to(count, (DOCS, 2 * HEAD_SIZE)).astype(jnp.bfloat16)
-    copies[0].wait()
-    copies[1].wait()
+def packed(keys, values, ids):
+    count = jnp.sum(ids[None, :] < jnp.arange(DOCS, dtype=jnp.int32)[:, None], axis=1).astype(jnp.bfloat16)
+    counts = jnp.broadcast_to(count[:, None], (DOCS, TOK))
+    numbers = jnp.broadcast_to(ids.astype(jnp.bfloat16)[None, :], (DOCS, TOK))
+    rows = jnp.concatenate([keys, values], 1)
+    return jnp.concatenate([rows, jnp.concatenate([counts, numbers], 1)], 0)[None]
 
 
 def fetch_weight(aheads, z, w_ref, held_ref, sems):
     copies = []
     for n, ahead in enumerate(aheads):
         at = pl.multiple_of(lax.rem(z + ahead, 8) * FEATURES, FEATURES)
-        copies.append(pltpu.make_async_copy(w_ref.at[:, pl.ds(at, FEATURES)], held_ref.at[n], sems.at[n]))
+        copies.append(pltpu.make_async_copy(w_ref.at[:, pl.ds(at, FEATURES)], held_ref.at[:, pl.ds(n * FEATURES, FEATURES)], sems.at[n]))
     for copy in copies:
         copy.start()
     return copies
@@ -96,21 +87,13 @@
     return value.reshape(value.shape[0] // 8, 8, value.shape[1])
 
 
-def forward_kernel(info_ref, q_ref, w_ref, id_ref, *refs):
+def forward_kernel(info_ref, w_ref, rows_ref, *refs):
     own, sib, refs = refs[:5], refs[5:10], refs[10:]
-    att_t_ref, log_ref, first_ref, rows_ref, key_ref, value_ref = refs[:6]
+    att_t_ref, log_ref, first_ref, key_ref, value_ref, held_ref = refs[:6]
     sends, keeps, refs = refs[6:8], refs[8:12], refs[12:]
-    score_ref, acc_ref, max_ref, sum_ref, att_ref, held_ref, sems, q_sems = refs
+    score_ref, acc_ref, max_ref, sum_ref, att_ref, sems = refs
     query_pair, core = info_ref[0], info_ref[1]
-    q_copies = [
-        pltpu.make_async_copy(
-            q_ref.at[:, pl.ds(h * HEAD_SIZE, HEAD_SIZE)], rows_ref.at[pl.ds(h * TOK, TOK)], q_sems.at[h]
-        )
-        for h in range(HEADS)
-    ]
-    for copy in q_copies:
-        copy.start()
-    w_copies = fetch_weight(PROJECT_ORDER, info_ref[2], w_ref, held_ref, sems)
+    w_copies = fetch_weight(PART_ORDER, info_ref[2], w_ref, held_ref, sems)
     at_own = pl.multiple_of(core * TOK, TOK)
     at_sib = pl.multiple_of((1 - core) * TOK, TOK)
     below = jnp.zeros((DOCS, TOK), jnp.float32)
@@ -123,7 +106,8 @@
             value_ref[pl.ds(j * PAIR + at, TOK), :] = ref[place, 0:TOK, HEAD_SIZE : 2 * HEAD_SIZE]
             below = below + valid * ref[place, TOK:ROWS, 0:TOK].astype(jnp.float32)
     number = lax.broadcasted_iota(jnp.int32, (DOCS, TOK), 0)
-    before = jnp.sum(jnp.where(id_ref[...] == number, below, 0.0), axis=0, keepdims=True)
+    numbers = own[0][0, TOK:ROWS, TOK : 2 * TOK].astype(jnp.float32).astype(jnp.int32)
+    before = jnp.sum(jnp.where(numbers == number, below, 0.0), axis=0, keepdims=True)
     first_row = before.astype(jnp.int32) + PAIR * jnp.maximum(query_pair - (SLOTS - 1), 0)
     first_ref[...] = first_row
     live = query_pair - jnp.min(first_row) // PAIR + 1
@@ -158,8 +142,6 @@
         mix_rows(pl.multiple_of(PAIR + s * STEP, PAIR), STEP)
         return unused
 
-    for copy in q_copies:
-        copy.wait()
     score_rows(0, PAIR, query_pair * PAIR)
     lax.fori_loop(0, live // 2, score_step, 0)
     log_ref[...] = jnp.max(max_ref[...], axis=0, keepdims=True)
@@ -173,36 +155,32 @@
         mixed = acc_ref[:, cols] * inverse[:, cols]
         att_t_ref[:, cols] = mixed.astype(jnp.bfloat16)
         att_ref[:, h * HEAD_SIZE : (h + 1) * HEAD_SIZE] = mixed.T.astype(jnp.bfloat16)
+    for copy in w_copies:
+        copy.wait()
     for n in range(8):
-        w_copies[n].wait()
-        part = dot(att_ref[...], held_ref[n])
+        part = dot(att_ref[...], held_ref[:, n * FEATURES : (n + 1) * FEATURES])
         if n < 4:
             sends[n // 2][n % 2] = part.astype(jnp.bfloat16)
         else:
             keeps[n - 4][...] = part
 
 
-def backward_kernel(info_ref, cot_ref, w_ref, *refs):
-    pieces, refs = refs[:5], refs[5:]
+def backward_kernel(info_ref, held_ref, *refs):
+    pieces, refs = refs[:6], refs[6:]
     rows_ref, key_ref, value_ref, att_t_ref, log_ref, first_ref = refs[:6]
     dq_ref, own, sib, refs = refs[6], refs[7:12], refs[12:17], refs[17:]
-    grad_ref, grad_t_ref, grows_ref, acc_ref, delta_ref, out_ref, mine_ref, held_ref, sems, cot_sem = refs
+    cot_ref, grad_ref, grad_t_ref, grows_ref, acc_ref, delta_ref, out_ref = refs
     query_pair, core = info_ref[0], info_ref[1]
-    cot_copy = pltpu.make_async_copy(cot_ref, mine_ref, cot_sem)
-    cot_copy.start()
-    w_copies = fetch_weight(GRADIENT_ORDER, info_ref[2], w_ref, held_ref, sems)
     at_own = pl.multiple_of(core * TOK, TOK)
     at_sib = pl.multiple_of((1 - core) * TOK, TOK)
     first_row = first_ref[...]
     live = query_pair - jnp.min(first_row) // PAIR + 1
-    cot_copy.wait()
     n = 0
-    for ref in (mine_ref,) + pieces:
+    for ref in pieces:
         for j in range(ref.shape[0] // TOK):
-            w_copies[n].wait()
-            part = dot_nt(held_ref[n], ref[j * TOK : (j + 1) * TOK, :])
-            grad_ref[...] = part if n == 0 else grad_ref[...] + part
+            cot_ref[:, n * FEATURES : (n + 1) * FEATURES] = ref[j * TOK : (j + 1) * TOK, :]
             n = n + 1
+    grad_ref[...] = dot_nt(held_ref[...], cot_ref[...])
     for h in range(HEADS):
         part = slice(h * TOK, (h + 1) * TOK)
         grad_t = grad_ref[part, :].astype(jnp.bfloat16)
@@ -268,18 +246,18 @@
     return value.astype(jnp.bfloat16)
 
 
-def forward(info, queries, weight, ids, own, sib):
+def forward(info, weight, rows, own, sib):
     outs = pl.pallas_call(
         forward_kernel,
-        in_specs=[SMEM, HBM, HBM] + [VMEM] * 11,
+        in_specs=[SMEM, HBM] + [VMEM] * 11,
         out_specs=[VMEM] * 12,
         out_shape=[
             shaped(HEAD_SIZE, QROWS),
             shaped(1, QROWS, dtype=jnp.float32),
             shaped(1, TOK, dtype=jnp.int32),
-            shaped(QROWS, HEAD_SIZE),
             shaped(KEYS, HEAD_SIZE),
             shaped(KEYS, HEAD_SIZE),
+            shaped(QROWS, 8 * FEATURES),
         ]
         + [shaped(2, TOK, FEATURES)] * 2
         + [shaped(TOK, FEATURES, dtype=jnp.float32)] * 4,
@@ -289,39 +267,34 @@
             pltpu.VMEM((8, QROWS), jnp.float32),
             pltpu.VMEM((8, QROWS), jnp.float32),
             pltpu.VMEM((TOK, QROWS), jnp.bfloat16),
-            pltpu.VMEM((8, QROWS, FEATURES), jnp.bfloat16),
             pltpu.SemaphoreType.DMA((8,)),
-            pltpu.SemaphoreType.DMA((HEADS,)),
         ],
-        compiler_params=params(46),
+        compiler_params=params(FORWARD_MIB),
         cost_estimate=cost(9_000_000_000, 1 << 20),
-    )(info, queries, weight, ids, *own, *sib)
+    )(info, weight, rows, *own, *sib)
     return outs[:6], outs[6:8], outs[8:]
 
 
-def backward(info, cotangent, weight, pieces, saved):
-    att_t, log_total, first_row, rows, key, value = saved
+def backward(info, pieces, rows, saved):
+    att_t, log_total, first_row, key, value, held = saved
     blocks = [shaped(n, TOK, 2 * HEAD_SIZE) for n in HELD]
     outs = pl.pallas_call(
         backward_kernel,
-        in_specs=[SMEM, HBM, HBM] + [VMEM] * 11,
+        in_specs=[SMEM] + [VMEM] * 13,
         out_specs=[VMEM] * 11,
         out_shape=[shaped(TOK, QROWS)] + blocks + blocks,
         scratch_shapes=[
+            pltpu.VMEM((TOK, 8 * FEATURES), jnp.bfloat16),
             pltpu.VMEM((QROWS, TOK), jnp.float32),
             pltpu.VMEM((HEAD_SIZE, QROWS), jnp.bfloat16),
             pltpu.VMEM((QROWS, HEAD_SIZE), jnp.bfloat16),
             pltpu.VMEM((HEAD_SIZE, QROWS), jnp.float32),
             pltpu.VMEM((1, QROWS), jnp.float32),
             pltpu.VMEM((KEYS, 2 * HEAD_SIZE), jnp.bfloat16),
-            pltpu.VMEM((TOK, FEATURES), jnp.bfloat16),
-            pltpu.VMEM((8, QROWS, FEATURES), jnp.bfloat16),
-            pltpu.SemaphoreType.DMA((8,)),
-            pltpu.SemaphoreType.DMA,
         ],
-        compiler_params=params(46),
+        compiler_params=params(BACKWARD_MIB),
         cost_estimate=cost(14_000_000_000, 1 << 20),
-    )(info, cotangent, weight, *pieces, rows, key, value, att_t, log_total, first_row)
+    )(info, held, *pieces, rows, key, value, att_t, log_total, first_row)
     return outs[0], outs[1:6], outs[6:11]
 
 
@@ -330,33 +303,26 @@
     z = lax.axis_index("tensor").astype(jnp.int32)
     info = jnp.stack([me // 2, me % 2, z])
 
-    block, ids = pl.pallas_call(
-        pack_kernel,
-        in_specs=[HBM] * 3,
-        out_specs=[VMEM] * 2,
-        out_shape=[shaped(1, ROWS, 2 * HEAD_SIZE), shaped(1, TOK, dtype=jnp.int32)],
-        scratch_shapes=[pltpu.SemaphoreType.DMA((3,))],
-        compiler_params=params(2),
-        cost_estimate=cost(1_000_000_000, 1 << 16),
-    )(rotated_keys, value_heads_packed, doc_ids.reshape(1, TOK))
+    block = packed(rotated_keys, value_heads_packed, doc_ids)
+    rows = rotated_queries.reshape(TOK, HEADS, HEAD_SIZE).transpose(1, 0, 2).reshape(QROWS, HEAD_SIZE)
     block_4 = chips_on(block, 4)
     block_8 = chips_on(block, 8)
     z_up, z_down, z_four = along_z(out_cotangent, -1), along_z(out_cotangent, 1), along_z(out_cotangent, 4)
     near = jnp.concatenate([block, block_4], 0)
+    near, rows, z_up, z_down, z_four = lax.optimization_barrier((near, rows, z_up, z_down, z_four))
     own = [near, block_8] + [chips_on(near, by) for by in (1, 2, 3)]
     sib = [across(piece) for piece in own]
-    own, sib, z_up, z_down, z_four = lax.optimization_barrier((own, sib, z_up, z_down, z_four))
     z_far_up = along_z(jnp.concatenate([z_up, z_four], 0), -1)
     z_far_down = along_z(jnp.concatenate([z_down, z_four], 0), 1)
 
     saved, (to_up, to_down), (near_up, near_four, near_down, kept) = forward(
-        info, rotated_queries, out_weight, ids, own, sib
+        info, out_weight, rows, own, sib
     )
     got_up = along_z(to_up, 1)
     got_down = along_z(to_down, -1)
 
-    pieces = (z_up, z_down, z_four, z_far_up, z_far_down)
-    query_grad, grad_own, grad_sib = backward(info, out_cotangent, out_weight, pieces, saved)
+    pieces = (z_far_up, z_far_down, z_up, z_four, z_down, out_cotangent)
+    query_grad, grad_own, grad_sib = backward(info, pieces, rows, saved)
 
     grad_sib, got_up, got_down = lax.optimization_barrier((grad_sib, got_up, got_down))
     sum_up = along_z(low(near_up + wide(got_up[0])), 1)

time: 87.8 us -> 87.6 us (level)
  local copies, waits for them, and re-layouts: 3.77 us -> 7.43 us
  Pallas kernels: 16.2 us -> 12.9 us
  starting transfers between devices: 49.8 us -> 46.7 us
  other arithmetic: 1.22 us -> 3.44 us
  waiting for transfers between devices: 14.6 us -> 15.5 us
    ppermute x10, starting transfers between devices: 26.1 us -> 20.6 us  [chips_on(): lax.ppermute(value, 'dp', [(i, (i + 2 * by) % 32) for i in range(32)])]
    ppermute x10, waiting for transfers between devices: 4.58 us -> 8.95 us  [chips_on(): lax.ppermute(value, 'dp', [(i, (i + 2 * by) % 32) for i in range(32)])]
    unnamed x11 -> x8, local copies, waits for them, and re-layouts: 3.12 us -> 6.66 us
    pallas_call x3 -> x2, Pallas kernels: 16.2 us -> 12.9 us  [the longest x1 7.15 us: backward(): pl.pallas_call(backward_kernel, in_specs=[SMEM] + [VMEM] * 13, out_specs=...]
    ppermute x10, waiting for transfers between devices: 7.76 us -> 4.66 us  [along_z(): return lax.ppermute(value, 'tensor', [(i, (i + by) % 8) for i in range(8)])]
    ppermute x10, starting transfers between devices: 21.1 us -> 24 us  [along_z(): return lax.ppermute(value, 'tensor', [(i, (i + by) % 8) for i in range(8)])]
  transfers between devices with their start and end apart: 30 -> 30, of which waited for: 9 -> 9; matrix products, arithmetic and copies ran while one was open for 1% -> 4% of each run, Pallas kernels for 19% -> 15%
where the time goes in v3:
time: 87.6 us; the launch traced here: 86.8 us
  starting transfers between devices  46.7 us (53%)
  waiting for transfers between devices  15.5 us (18%)
  Pallas kernels  12.9 us (15%)
  local copies, waits for them, and re-layouts  7.43 us (8%)
  other arithmetic  3.44 us (4%)
    ppermute x10, starting transfers between devices, along_z(): return lax.ppermute(value, 'tensor', [(i, (i + by) % 8) for i in range(8)])  24 us
    ppermute x10, starting transfers between devices, chips_on(): lax.ppermute(value, 'dp', [(i, (i + 2 * by) % 32) for i in range(32)])  20.6 us
    ppermute x10, waiting for transfers between devices, chips_on(): lax.ppermute(value, 'dp', [(i, (i + 2 * by) % 32) for i in range(32)])  8.95 us
    pallas_call x1, Pallas kernels, backward(): pl.pallas_call(backward_kernel, in_specs=[SMEM] + [VMEM] * 13, out_specs=...  7.15 us
    unnamed x8, local copies, waits for them, and re-layouts  6.66 us
    pallas_call x1, Pallas kernels, forward(): pl.pallas_call(forward_kernel, in_specs=[SMEM, HBM] + [VMEM] * 11, out_sp...  5.77 us
    ppermute x10, waiting for transfers between devices, along_z(): return lax.ppermute(value, 'tensor', [(i, (i + by) % 8) for i in range(8)])  4.66 us
    ppermute x10, starting transfers between devices, across(): return lax.ppermute(value, 'dp', [(i, i ^ 1) for i in range(32)])  2.02 us
  transfers between devices with their start and end apart: 30, of which 9 were waited for; matrix products, arithmetic and copies ran while one was open for 4% of the time, Pallas kernels for 15%

profile of v3, /device:TPU:8, one launch (start us, length us, event | category | flops | bytes accessed | tf_op | source)
XLA Modules:
  0.0 86.8 jit_solution(12410822610451088779)
XLA Ops:
  0.6 2.0 %collective-permute-start.2 = (bf16[128,512]{1,0:T(8,128)(2,1)}, bf16[128,512]{1,0:T(8,128)(2,1)S(1)}, u32[]{:S(2)}, u32[]{:S(2)}) collective-permute-start(bf16[128,512]{1,0:T(8,128)(2,1)} %refs_5_.1), channel_id=1, source_target_pairs={{0,1},{1,2},{2,3},{3,4},{4,5},{5,6},{6,7},{7,0},{8,9},{9,10},{10,1... | collective-permute-start | bytes 393224 | tf_op jit(solution)/shard_map/ppermute | solution.py:238
  2.6 4.0 %collective-permute-start.1 = (bf16[128,512]{1,0:T(8,128)(2,1)}, bf16[128,512]{1,0:T(8,128)(2,1)S(1)}, u32[]{:S(2)}, u32[]{:S(2)}) collective-permute-start(bf16[128,512]{1,0:T(8,128)(2,1)} %refs_5_.1), channel_id=1, source_target_pairs={{0,7},{1,0},{2,1},{3,2},{4,3},{5,4},{6,5},{7,6},{8,15},{9,8},{10,9... | collective-permute-start | bytes 393224 | tf_op jit(solution)/shard_map/ppermute | solution.py:238
  6.7 4.5 %collective-permute-start.3 = (bf16[128,512]{1,0:T(8,128)(2,1)}, bf16[128,512]{1,0:T(8,128)(2,1)S(1)}, u32[]{:S(2)}, u32[]{:S(2)}) collective-permute-start(bf16[128,512]{1,0:T(8,128)(2,1)} %refs_5_.1), channel_id=1, source_target_pairs={{0,4},{1,5},{2,6},{3,7},{4,0},{5,1},{6,2},{7,3},{8,12},{9,13},{10,... | collective-permute-start | bytes 393224 | tf_op jit(solution)/shard_map/ppermute | solution.py:238
  11.8 0.8 convert_reduce_fusion
  12.7 0.8 maximum_bitcast_fusion
  13.5 1.6 %collective-permute-start = (bf16[1,144,256]{2,1,0:T(8,128)(2,1)S(1)}, bf16[1,144,256]{2,1,0:T(8,128)(2,1)S(1)}, u32[]{:S(2)}, u32[]{:S(2)}) collective-permute-start(bf16[1,144,256]{2,1,0:T(8,128)(2,1)S(1)} %maximum_bitcast_fusion), channel_id=1, source_target_pairs={{0,64},{8,72},{16,80},{24,88},{32,96},{40,104},{48,112},{56,120},{... | collective-permute-start | bytes 221192 | tf_op jit(solution)/shard_map/ppermute | solution.py:230
  15.1 4.0 %collective-permute-done = bf16[1,144,256]{2,1,0:T(8,128)(2,1)S(1)} collective-permute-done((bf16[1,144,256]{2,1,0:T(8,128)(2,1)S(1)}, bf16[1,144,256]{2,1,0:T(8,128)(2,1)S(1)}, u32[]{:S(2)}, u32[]{:S(2)}) %collective-permute-start) | collective-permute-done | bytes 73760 | tf_op jit(solution)/shard_map/ppermute | solution.py:230
  19.8 2.6 %collective-permute-start.6 = (bf16[2,144,256]{2,1,0:T(8,128)(2,1)S(1)}, bf16[2,144,256]{2,1,0:T(8,128)(2,1)S(1)}, u32[]{:S(2)}, u32[]{:S(2)}) collective-permute-start(bf16[2,144,256]{2,1,0:T(8,128)(2,1)S(1)} %pad_maximum_fusion.2.refs_0_), channel_id=1, source_target_pairs={{0,32},{8,40},{16,48},{24,56},{32,64},{40,72},{48,80},{56,88},{64,... | collective-permute-start | bytes 442376 | tf_op jit(solution)/shard_map/ppermute | solution.py:230
  22.4 1.9 %collective-permute-start.5 = (bf16[2,144,256]{2,1,0:T(8,128)(2,1)S(1)}, bf16[2,144,256]{2,1,0:T(8,128)(2,1)S(1)}, u32[]{:S(2)}, u32[]{:S(2)}) collective-permute-start(bf16[2,144,256]{2,1,0:T(8,128)(2,1)S(1)} %pad_maximum_fusion.2.refs_0_), channel_id=1, source_target_pairs={{0,16},{8,24},{16,32},{24,40},{32,48},{40,56},{48,64},{56,72},{64,... | collective-permute-start | bytes 442376 | tf_op jit(solution)/shard_map/ppermute | solution.py:230
  24.3 2.7 %collective-permute-start.4 = (bf16[1,144,256]{2,1,0:T(8,128)(2,1)S(1)}, bf16[1,144,256]{2,1,0:T(8,128)(2,1)S(1)}, u32[]{:S(2)}, u32[]{:S(2)}) collective-permute-start(bf16[1,144,256]{2,1,0:T(8,128)(2,1)S(1)} %maximum_bitcast_fusion), channel_id=1, source_target_pairs={{0,128},{8,136},{16,144},{24,152},{32,160},{40,168},{48,176},{56,1... | collective-permute-start | bytes 221192 | tf_op jit(solution)/shard_map/ppermute | solution.py:230
  27.0 1.6 %collective-permute-done.7.refs_4_ = bf16[2,144,256]{2,1,0:T(8,128)(2,1)S(1)} collective-permute-done((bf16[2,144,256]{2,1,0:T(8,128)(2,1)S(1)}, bf16[2,144,256]{2,1,0:T(8,128)(2,1)S(1)}, u32[]{:S(2)}, u32[]{:S(2)}) %collective-permute-start.7) | collective-permute-done | bytes 147488 | tf_op jit(solution)/shard_map/ppermute | solution.py:230
  28.6 3.1 %collective-permute-done.6.refs_3_ = bf16[2,144,256]{2,1,0:T(8,128)(2,1)S(1)} collective-permute-done((bf16[2,144,256]{2,1,0:T(8,128)(2,1)S(1)}, bf16[2,144,256]{2,1,0:T(8,128)(2,1)S(1)}, u32[]{:S(2)}, u32[]{:S(2)}) %collective-permute-start.6) | collective-permute-done | bytes 147488 | tf_op jit(solution)/shard_map/ppermute | solution.py:230
  32.5 1.2 %collective-permute-done.9.refs_6_ = bf16[1,144,256]{2,1,0:T(8,128)(2,1)S(1)} collective-permute-done((bf16[1,144,256]{2,1,0:T(8,128)(2,1)S(1)}, bf16[1,144,256]{2,1,0:T(8,128)(2,1)S(1)}, u32[]{:S(2)}, u32[]{:S(2)}) %collective-permute-start.9) | collective-permute-done | bytes 73760 | tf_op jit(solution)/shard_map/ppermute | solution.py:234
  33.7 3.2 %collective-permute-start.13 = (bf16[256,512]{1,0:T(8,128)(2,1)S(1)}, bf16[256,512]{1,0:T(8,128)(2,1)S(1)}, u32[]{:S(2)}, u32[]{:S(2)}) collective-permute-start(bf16[256,512]{1,0:T(8,128)(2,1)S(1)} %get-tuple-element.78), channel_id=1, source_target_pairs={{0,7},{1,0},{2,1},{3,2},{4,3},{5,4},{6,5},{7,6},{8,15},{9,8},{10,9... | collective-permute-start | bytes 786440 | tf_op jit(solution)/shard_map/ppermute | solution.py:238
  36.9 5.8 %shard_map.93 = (bf16[128,1024]{1,0:T(8,128)(2,1)S(1)}, f32[1,1024]{1,0:T(1,128)S(1)}, s32[1,128]{1,0:T(1,128)S(1)}, bf16[2304,128]{1,0:T(8,128)(2,1)S(1)}, bf16...) custom-call(s32[3]{0:T(128)S(1)} %pad_add_fusion.info_ref, ...), custom_call_target="tpu_custom_call" | custom-call | flops 8999999488 | bytes 1048576 | tf_op jit(solution)/shard_map/pallas_call | solution.py:250
  42.7 3.3 %copy-done.2 = bf16[1024,4096]{1,0:T(8,128)(2,1)} copy-done((bf16[1024,4096]{1,0:T(8,128)(2,1)}, bf16[1024,4096]{1,0:T(8,128)(2,1)S(1)}, u32[]{:S(2)}) %copy-start.2) | copy-done | bytes 8388632
  46.0 3.2 %collective-permute-start.16 = (bf16[2,128,512]{2,1,0:T(8,128)(2,1)S(1)}, bf16[2,128,512]{2,1,0:T(8,128)(2,1)S(1)}, u32[]{:S(2)}, u32[]{:S(2)}) collective-permute-start(bf16[2,128,512]{2,1,0:T(8,128)(2,1)S(1)} %get-tuple-element.58), channel_id=1, source_target_pairs={{0,7},{1,0},{2,1},{3,2},{4,3},{5,4},{6,5},{7,6},{8,15},{9,8},{10,9... | collective-permute-start | bytes 786440 | tf_op jit(solution)/shard_map/ppermute | solution.py:238
  49.2 3.4 %copy-done.3 = bf16[1024,4096]{1,0:T(8,128)(2,1)S(1)} copy-done((bf16[1024,4096]{1,0:T(8,128)(2,1)S(1)}, bf16[1024,4096]{1,0:T(8,128)(2,1)}, u32[]{:S(2)}) %copy-start.3) | copy-done | bytes 8388632
  52.6 7.2 %shard_map.94 = (bf16[128,1024]{1,0:T(8,128)(2,1)}, bf16[2,128,256]{2,1,0:T(8,128)(2,1)S(1)}, bf16[1,128,256]{2,1,0:T(8,128)(2,1)S(1)}, bf16[2,128,256]{2,1,0:T(...) custom-call(s32[3]{0:T(128)S(1)} %pad_add_fusion.info_ref, ...), custom_call_target="tpu_custom_call" | custom-call | flops 14000000000 | bytes 1048576 | tf_op jit(solution)/shard_map/pallas_call | solution.py:281
  62.1 1.0 %collective-permute-start.22 = (bf16[2,128,256]{2,1,0:T(8,128)(2,1)S(1)}, bf16[2,128,256]{2,1,0:T(8,128)(2,1)S(1)}, u32[]{:S(2)}, u32[]{:S(2)}) collective-permute-start(bf16[2,128,256]{2,1,0:T(8,128)(2,1)S(1)} %add_convert_fusion.2), channel_id=1, source_target_pairs={{0,240},{8,248},{16,0},{24,8},{32,16},{40,24},{48,32},{56,40},{64,... | collective-permute-start | bytes 393224 | tf_op jit(solution)/shard_map/ppermute | solution.py:230
  63.8 9.5 %collective-permute-start.26 = (bf16[2,128,256]{2,1,0:T(8,128)(2,1)S(1)}, bf16[2,128,256]{2,1,0:T(8,128)(2,1)S(1)}, u32[]{:S(2)}, u32[]{:S(2)}) collective-permute-start(bf16[2,128,256]{2,1,0:T(8,128)(2,1)S(1)} %add_convert_fusion), channel_id=1, source_target_pairs={{0,208},{8,216},{16,224},{24,232},{32,240},{40,248},{48,0},{56,8},... | collective-permute-start | bytes 393224 | tf_op jit(solution)/shard_map/ppermute | solution.py:230
  73.4 3.8 %collective-permute-start.18 = (bf16[128,512]{1,0:T(8,128)(2,1)S(1)}, bf16[128,512]{1,0:T(8,128)(2,1)S(1)}, u32[]{:S(2)}, u32[]{:S(2)}) collective-permute-start(bf16[128,512]{1,0:T(8,128)(2,1)S(1)} %get-tuple-element.75), channel_id=1, source_target_pairs={{0,4},{1,5},{2,6},{3,7},{4,0},{5,1},{6,2},{7,3},{8,12},{9,13},{10,... | collective-permute-start | bytes 393224 | tf_op jit(solution)/shard_map/ppermute | solution.py:238
  77.2 3.1 %collective-permute-start.19 = (bf16[128,512]{1,0:T(8,128)(2,1)S(1)}, bf16[128,512]{1,0:T(8,128)(2,1)S(1)}, u32[]{:S(2)}, u32[]{:S(2)}) collective-permute-start(bf16[128,512]{1,0:T(8,128)(2,1)S(1)} %get-tuple-element.76), channel_id=1, source_target_pairs={{0,7},{1,0},{2,1},{3,2},{4,3},{5,4},{6,5},{7,6},{8,15},{9,8},{10,9... | collective-permute-start | bytes 393224 | tf_op jit(solution)/shard_map/ppermute | solution.py:238
  80.6 4.5 %collective-permute-done.18 = bf16[128,512]{1,0:T(8,128)(2,1)S(1)} collective-permute-done((bf16[128,512]{1,0:T(8,128)(2,1)S(1)}, bf16[128,512]{1,0:T(8,128)(2,1)S(1)}, u32[]{:S(2)}, u32[]{:S(2)}) %collective-permute-start.18) | collective-permute-done | bytes 131104 | tf_op jit(solution)/shard_map/ppermute | solution.py:238
  (66 shorter events, 7.2 us)
Async XLA Ops:
  0.6 18.5 %collective-permute-start.2 = (bf16[128,512]{1,0:T(8,128)(2,1)}, bf16[128,512]{1,0:T(8,128)(2,1)S(1)}, u32[]{:S(2)}, u32[]{:S(2)}) collective-permute-start(bf16[128,512]{1,0:T(8,128)(2,1)} %refs_5_.1), channel_id=1, source_target_pairs={{0,1},{1,2},{2,3},{3,4},{4,5},{5,6},{6,7},{7,0},{8,9},{9,10},{10,1... | collective-permute-start | bytes 393224 | tf_op jit(solution)/shard_map/ppermute | solution.py:238
  2.6 16.5 %collective-permute-start.1 = (bf16[128,512]{1,0:T(8,128)(2,1)}, bf16[128,512]{1,0:T(8,128)(2,1)S(1)}, u32[]{:S(2)}, u32[]{:S(2)}) collective-permute-start(bf16[128,512]{1,0:T(8,128)(2,1)} %refs_5_.1), channel_id=1, source_target_pairs={{0,7},{1,0},{2,1},{3,2},{4,3},{5,4},{6,5},{7,6},{8,15},{9,8},{10,9... | collective-permute-start | bytes 393224 | tf_op jit(solution)/shard_map/ppermute | solution.py:238
  6.7 12.5 %collective-permute-start.3 = (bf16[128,512]{1,0:T(8,128)(2,1)}, bf16[128,512]{1,0:T(8,128)(2,1)S(1)}, u32[]{:S(2)}, u32[]{:S(2)}) collective-permute-start(bf16[128,512]{1,0:T(8,128)(2,1)} %refs_5_.1), channel_id=1, source_target_pairs={{0,4},{1,5},{2,6},{3,7},{4,0},{5,1},{6,2},{7,3},{8,12},{9,13},{10,... | collective-permute-start | bytes 393224 | tf_op jit(solution)/shard_map/ppermute | solution.py:238
  13.5 5.6 %collective-permute-start = (bf16[1,144,256]{2,1,0:T(8,128)(2,1)S(1)}, bf16[1,144,256]{2,1,0:T(8,128)(2,1)S(1)}, u32[]{:S(2)}, u32[]{:S(2)}) collective-permute-start(bf16[1,144,256]{2,1,0:T(8,128)(2,1)S(1)} %maximum_bitcast_fusion), channel_id=1, source_target_pairs={{0,64},{8,72},{16,80},{24,88},{32,96},{40,104},{48,112},{56,120},{... | collective-permute-start | bytes 221192 | tf_op jit(solution)/shard_map/ppermute | solution.py:230
  19.1 9.5 %collective-permute-start.7 = (bf16[2,144,256]{2,1,0:T(8,128)(2,1)S(1)}, bf16[2,144,256]{2,1,0:T(8,128)(2,1)S(1)}, u32[]{:S(2)}, u32[]{:S(2)}) collective-permute-start(bf16[2,144,256]{2,1,0:T(8,128)(2,1)S(1)} %pad_maximum_fusion.2.refs_0_), channel_id=1, source_target_pairs={{0,48},{8,56},{16,64},{24,72},{32,80},{40,88},{48,96},{56,104},{64... | collective-permute-start | bytes 442376 | tf_op jit(solution)/shard_map/ppermute | solution.py:230
  19.8 11.9 %collective-permute-start.6 = (bf16[2,144,256]{2,1,0:T(8,128)(2,1)S(1)}, bf16[2,144,256]{2,1,0:T(8,128)(2,1)S(1)}, u32[]{:S(2)}, u32[]{:S(2)}) collective-permute-start(bf16[2,144,256]{2,1,0:T(8,128)(2,1)S(1)} %pad_maximum_fusion.2.refs_0_), channel_id=1, source_target_pairs={{0,32},{8,40},{16,48},{24,56},{32,64},{40,72},{48,80},{56,88},{64,... | collective-permute-start | bytes 442376 | tf_op jit(solution)/shard_map/ppermute | solution.py:230
  22.4 9.4 %collective-permute-start.5 = (bf16[2,144,256]{2,1,0:T(8,128)(2,1)S(1)}, bf16[2,144,256]{2,1,0:T(8,128)(2,1)S(1)}, u32[]{:S(2)}, u32[]{:S(2)}) collective-permute-start(bf16[2,144,256]{2,1,0:T(8,128)(2,1)S(1)} %pad_maximum_fusion.2.refs_0_), channel_id=1, source_target_pairs={{0,16},{8,24},{16,32},{24,40},{32,48},{40,56},{48,64},{56,72},{64,... | collective-permute-start | bytes 442376 | tf_op jit(solution)/shard_map/ppermute | solution.py:230
  24.3 8.1 %collective-permute-start.4 = (bf16[1,144,256]{2,1,0:T(8,128)(2,1)S(1)}, bf16[1,144,256]{2,1,0:T(8,128)(2,1)S(1)}, u32[]{:S(2)}, u32[]{:S(2)}) collective-permute-start(bf16[1,144,256]{2,1,0:T(8,128)(2,1)S(1)} %maximum_bitcast_fusion), channel_id=1, source_target_pairs={{0,128},{8,136},{16,144},{24,152},{32,160},{40,168},{48,176},{56,1... | collective-permute-start | bytes 221192 | tf_op jit(solution)/shard_map/ppermute | solution.py:230
  27.0 6.6 %collective-permute-start.8 = (bf16[2,144,256]{2,1,0:T(8,128)(2,1)S(1)}, bf16[2,144,256]{2,1,0:T(8,128)(2,1)S(1)}, u32[]{:S(2)}, u32[]{:S(2)}) collective-permute-start(bf16[2,144,256]{2,1,0:T(8,128)(2,1)S(1)} %pad_maximum_fusion.2.refs_0_), channel_id=1, source_target_pairs={{0,8},{8,0},{16,24},{24,16},{32,40},{40,32},{48,56},{56,48},{64,72... | collective-permute-start | bytes 442376 | tf_op jit(solution)/shard_map/ppermute | solution.py:234
  28.6 8.3 %collective-permute-start.12 = (bf16[2,144,256]{2,1,0:T(8,128)(2,1)S(1)}, bf16[2,144,256]{2,1,0:T(8,128)(2,1)S(1)}, u32[]{:S(2)}, u32[]{:S(2)}) collective-permute-start(bf16[2,144,256]{2,1,0:T(8,128)(2,1)S(1)} %collective-permute-done.7.refs_4_), channel_id=1, source_target_pairs={{0,8},{8,0},{16,24},{24,16},{32,40},{40,32},{48,56},{56,48},{64,72... | collective-permute-start | bytes 442376 | tf_op jit(solution)/shard_map/ppermute | solution.py:234
  31.8 5.1 %collective-permute-start.11 = (bf16[2,144,256]{2,1,0:T(8,128)(2,1)S(1)}, bf16[2,144,256]{2,1,0:T(8,128)(2,1)S(1)}, u32[]{:S(2)}, u32[]{:S(2)}) collective-permute-start(bf16[2,144,256]{2,1,0:T(8,128)(2,1)S(1)} %collective-permute-done.6.refs_3_), channel_id=1, source_target_pairs={{0,8},{8,0},{16,24},{24,16},{32,40},{40,32},{48,56},{56,48},{64,72... | collective-permute-start | bytes 442376 | tf_op jit(solution)/shard_map/ppermute | solution.py:234
  33.7 15.6 %collective-permute-start.14 = (bf16[256,512]{1,0:T(8,128)(2,1)S(1)}, bf16[256,512]{1,0:T(8,128)(2,1)S(1)}, u32[]{:S(2)}, u32[]{:S(2)}) collective-permute-start(bf16[256,512]{1,0:T(8,128)(2,1)S(1)} %get-tuple-element.77), channel_id=1, source_target_pairs={{0,1},{1,2},{2,3},{3,4},{4,5},{5,6},{6,7},{7,0},{8,9},{9,10},{10,1... | collective-permute-start | bytes 786440 | tf_op jit(solution)/shard_map/ppermute | solution.py:238
  33.7 15.5 %collective-permute-start.13 = (bf16[256,512]{1,0:T(8,128)(2,1)S(1)}, bf16[256,512]{1,0:T(8,128)(2,1)S(1)}, u32[]{:S(2)}, u32[]{:S(2)}) collective-permute-start(bf16[256,512]{1,0:T(8,128)(2,1)S(1)} %get-tuple-element.78), channel_id=1, source_target_pairs={{0,7},{1,0},{2,1},{3,2},{4,3},{5,4},{6,5},{7,6},{8,15},{9,8},{10,9... | collective-permute-start | bytes 786440 | tf_op jit(solution)/shard_map/ppermute | solution.py:238
  46.0 13.8 %collective-permute-start.15 = (bf16[2,128,512]{2,1,0:T(8,128)(2,1)S(1)}, bf16[2,128,512]{2,1,0:T(8,128)(2,1)S(1)}, u32[]{:S(2)}, u32[]{:S(2)}) collective-permute-start(bf16[2,128,512]{2,1,0:T(8,128)(2,1)S(1)} %get-tuple-element.57), channel_id=1, source_target_pairs={{0,1},{1,2},{2,3},{3,4},{4,5},{5,6},{6,7},{7,0},{8,9},{9,10},{10,1... | collective-permute-start | bytes 786440 | tf_op jit(solution)/shard_map/ppermute | solution.py:238
  46.0 13.8 %collective-permute-start.16 = (bf16[2,128,512]{2,1,0:T(8,128)(2,1)S(1)}, bf16[2,128,512]{2,1,0:T(8,128)(2,1)S(1)}, u32[]{:S(2)}, u32[]{:S(2)}) collective-permute-start(bf16[2,128,512]{2,1,0:T(8,128)(2,1)S(1)} %get-tuple-element.58), channel_id=1, source_target_pairs={{0,7},{1,0},{2,1},{3,2},{4,3},{5,4},{6,5},{7,6},{8,15},{9,8},{10,9... | collective-permute-start | bytes 786440 | tf_op jit(solution)/shard_map/ppermute | solution.py:238
  60.4 20.1 %collective-permute-start.17 = (bf16[128,512]{1,0:T(8,128)(2,1)S(1)}, bf16[128,512]{1,0:T(8,128)(2,1)S(1)}, u32[]{:S(2)}, u32[]{:S(2)}) collective-permute-start(bf16[128,512]{1,0:T(8,128)(2,1)S(1)} %get-tuple-element.74), channel_id=1, source_target_pairs={{0,1},{1,2},{2,3},{3,4},{4,5},{5,6},{6,7},{7,0},{8,9},{9,10},{10,1... | collective-permute-start | bytes 393224 | tf_op jit(solution)/shard_map/ppermute | solution.py:238
  60.5 12.8 %collective-permute-start.20 = (bf16[2,128,256]{2,1,0:T(8,128)(2,1)S(1)}, bf16[2,128,256]{2,1,0:T(8,128)(2,1)S(1)}, u32[]{:S(2)}, u32[]{:S(2)}) collective-permute-start(bf16[2,128,256]{2,1,0:T(8,128)(2,1)S(1)} %get-tuple-element.65), channel_id=1, source_target_pairs={{0,8},{8,0},{16,24},{24,16},{32,40},{40,32},{48,56},{56,48},{64,72... | collective-permute-start | bytes 393224 | tf_op jit(solution)/shard_map/ppermute | solution.py:234
  62.1 15.1 %collective-permute-start.22 = (bf16[2,128,256]{2,1,0:T(8,128)(2,1)S(1)}, bf16[2,128,256]{2,1,0:T(8,128)(2,1)S(1)}, u32[]{:S(2)}, u32[]{:S(2)}) collective-permute-start(bf16[2,128,256]{2,1,0:T(8,128)(2,1)S(1)} %add_convert_fusion.2), channel_id=1, source_target_pairs={{0,240},{8,248},{16,0},{24,8},{32,16},{40,24},{48,32},{56,40},{64,... | collective-permute-start | bytes 393224 | tf_op jit(solution)/shard_map/ppermute | solution.py:230
  63.1 17.2 %collective-permute-start.24 = (bf16[2,128,256]{2,1,0:T(8,128)(2,1)S(1)}, bf16[2,128,256]{2,1,0:T(8,128)(2,1)S(1)}, u32[]{:S(2)}, u32[]{:S(2)}) collective-permute-start(bf16[2,128,256]{2,1,0:T(8,128)(2,1)S(1)} %add_convert_fusion.1), channel_id=1, source_target_pairs={{0,224},{8,232},{16,240},{24,248},{32,0},{40,8},{48,16},{56,24},{6... | collective-permute-start | bytes 393224 | tf_op jit(solution)/shard_map/ppermute | solution.py:230
  63.8 16.5 %collective-permute-start.26 = (bf16[2,128,256]{2,1,0:T(8,128)(2,1)S(1)}, bf16[2,128,256]{2,1,0:T(8,128)(2,1)S(1)}, u32[]{:S(2)}, u32[]{:S(2)}) collective-permute-start(bf16[2,128,256]{2,1,0:T(8,128)(2,1)S(1)} %add_convert_fusion), channel_id=1, source_target_pairs={{0,208},{8,216},{16,224},{24,232},{32,240},{40,248},{48,0},{56,8},... | collective-permute-start | bytes 393224 | tf_op jit(solution)/shard_map/ppermute | solution.py:230
  73.4 11.7 %collective-permute-start.18 = (bf16[128,512]{1,0:T(8,128)(2,1)S(1)}, bf16[128,512]{1,0:T(8,128)(2,1)S(1)}, u32[]{:S(2)}, u32[]{:S(2)}) collective-permute-start(bf16[128,512]{1,0:T(8,128)(2,1)S(1)} %get-tuple-element.75), channel_id=1, source_target_pairs={{0,4},{1,5},{2,6},{3,7},{4,0},{5,1},{6,2},{7,3},{8,12},{9,13},{10,... | collective-permute-start | bytes 393224 | tf_op jit(solution)/shard_map/ppermute | solution.py:238
  77.2 8.0 %collective-permute-start.19 = (bf16[128,512]{1,0:T(8,128)(2,1)S(1)}, bf16[128,512]{1,0:T(8,128)(2,1)S(1)}, u32[]{:S(2)}, u32[]{:S(2)}) collective-permute-start(bf16[128,512]{1,0:T(8,128)(2,1)S(1)} %get-tuple-element.76), channel_id=1, source_target_pairs={{0,7},{1,0},{2,1},{3,2},{4,3},{5,4},{6,5},{7,6},{8,15},{9,8},{10,9... | collective-permute-start | bytes 393224 | tf_op jit(solution)/shard_map/ppermute | solution.py:238
  80.3 5.8 %collective-permute-start.28 = (bf16[1,128,256]{2,1,0:T(8,128)(2,1)S(1)}, bf16[1,128,256]{2,1,0:T(8,128)(2,1)S(1)}, u32[]{:S(2)}, u32[]{:S(2)}) collective-permute-start(bf16[1,128,256]{2,1,0:T(8,128)(2,1)S(1)} %add_convert_fusion.4), channel_id=1, source_target_pairs={{0,128},{8,136},{16,144},{24,152},{32,160},{40,168},{48,176},{56,1... | collective-permute-start | bytes 196616 | tf_op jit(solution)/shard_map/ppermute | solution.py:230
  80.5 5.7 %collective-permute-start.29 = (bf16[128,256]{1,0:T(8,128)(2,1)S(1)}, bf16[128,256]{1,0:T(8,128)(2,1)S(1)}, u32[]{:S(2)}, u32[]{:S(2)}) collective-permute-start(bf16[128,256]{1,0:T(8,128)(2,1)S(1)} %fusion.6), channel_id=1, source_target_pairs={{0,192},{8,200},{16,208},{24,216},{32,224},{40,232},{48,240},{56,2... | collective-permute-start | bytes 196616 | tf_op jit(solution)/shard_map/ppermute | solution.py:230
  (10 other events, 51.9 us)

commit v4 on v3

--- a/solution.py
+++ b/solution.py
@@ -28,11 +28,11 @@
 HBM = pl.BlockSpec(memory_space=pltpu.HBM)
 NT = (((1,), (1,)), ((), ()))
 
-PLACE = {0: (0, 0), 4: (0, 1), 8: (1, 0), 1: (2, 0), 5: (2, 1), 2: (3, 0), 6: (3, 1), 3: (4, 0), 7: (4, 1)}
-HELD = (2, 1, 2, 2, 2)
+PLACE = {0: (0, 0), 4: (0, 1), 8: (0, 2), 1: (1, 0), 5: (1, 1), 2: (1, 2), 6: (1, 3), 3: (1, 4), 7: (1, 5)}
+HELD = (3, 6)
 PART_ORDER = (2, 5, 6, 3, 1, 4, 7, 0)
-FORWARD_MIB = 40
-BACKWARD_MIB = 36
+FORWARD_MIB = 34
+BACKWARD_MIB = 12
 
 
 def dot_nt(a, b):
@@ -56,11 +56,8 @@
 
 
 def packed(keys, values, ids):
-    count = jnp.sum(ids[None, :] < jnp.arange(DOCS, dtype=jnp.int32)[:, None], axis=1).astype(jnp.bfloat16)
-    counts = jnp.broadcast_to(count[:, None], (DOCS, TOK))
-    numbers = jnp.broadcast_to(ids.astype(jnp.bfloat16)[None, :], (DOCS, TOK))
-    rows = jnp.concatenate([keys, values], 1)
-    return jnp.concatenate([rows, jnp.concatenate([counts, numbers], 1)], 0)[None]
+    numbers = jnp.broadcast_to(jnp.tile(ids, 2).astype(jnp.bfloat16)[None, :], (DOCS, 2 * TOK))
+    return jnp.concatenate([jnp.concatenate([keys, values], 1), numbers], 0)[None]
 
 
 def fetch_weight(aheads, z, w_ref, held_ref, sems):
@@ -88,14 +85,15 @@
 
 
 def forward_kernel(info_ref, w_ref, rows_ref, *refs):
-    own, sib, refs = refs[:5], refs[5:10], refs[10:]
-    att_t_ref, log_ref, first_ref, key_ref, value_ref, held_ref = refs[:6]
-    sends, keeps, refs = refs[6:8], refs[8:12], refs[12:]
-    score_ref, acc_ref, max_ref, sum_ref, att_ref, sems = refs
+    own, sib, refs = refs[:2], refs[2:4], refs[4:]
+    att_t_ref, inverse_ref, first_ref, key_ref, value_ref, weight_ref, held_ref = refs[:7]
+    sends, keeps, refs = refs[7:9], refs[9:13], refs[13:]
+    score_ref, acc_ref, max_ref, sum_ref, att_ref, peak_ref, sems = refs
     query_pair, core = info_ref[0], info_ref[1]
     w_copies = fetch_weight(PART_ORDER, info_ref[2], w_ref, held_ref, sems)
     at_own = pl.multiple_of(core * TOK, TOK)
     at_sib = pl.multiple_of((1 - core) * TOK, TOK)
+    number = lax.broadcasted_iota(jnp.int32, (DOCS, TOK), 0).astype(jnp.float32)
     below = jnp.zeros((DOCS, TOK), jnp.float32)
     for j in range(SLOTS):
         array, place = PLACE[j]
@@ -104,10 +102,11 @@
             ref = held[array]
             key_ref[pl.ds(j * PAIR + at, TOK), :] = ref[place, 0:TOK, 0:HEAD_SIZE]
             value_ref[pl.ds(j * PAIR + at, TOK), :] = ref[place, 0:TOK, HEAD_SIZE : 2 * HEAD_SIZE]
-            below = below + valid * ref[place, TOK:ROWS, 0:TOK].astype(jnp.float32)
-    number = lax.broadcasted_iota(jnp.int32, (DOCS, TOK), 0)
-    numbers = own[0][0, TOK:ROWS, TOK : 2 * TOK].astype(jnp.float32).astype(jnp.int32)
-    before = jnp.sum(jnp.where(numbers == number, below, 0.0), axis=0, keepdims=True)
+            ids = ref[place, TOK:ROWS, 0:TOK].astype(jnp.float32)
+            below = below + jnp.where(ids < number, valid, 0.0)
+    below = jnp.sum(below, axis=1, keepdims=True)
+    mine = own[0][0, TOK:ROWS, 0:TOK].astype(jnp.float32)
+    before = jnp.sum(jnp.where(mine == number, below, 0.0), axis=0, keepdims=True)
     first_row = before.astype(jnp.int32) + PAIR * jnp.maximum(query_pair - (SLOTS - 1), 0)
     first_ref[...] = first_row
     live = query_pair - jnp.min(first_row) // PAIR + 1
@@ -130,9 +129,11 @@
         value_t = value_ref[rows, :].T
         for n in range(QROWS // CHUNK):
             cols = slice(n * CHUNK, (n + 1) * CHUNK)
-            weight = jnp.exp2(score_ref[rows, cols] - log_ref[:, cols])
+            weight = jnp.exp2(score_ref[rows, cols] - peak_ref[:, cols])
             sum_ref[:, cols] = sum_ref[:, cols] + jnp.sum(eights(weight), axis=0)
-            acc_ref[:, cols] = acc_ref[:, cols] + dot(value_t, weight.astype(jnp.bfloat16))
+            weight = weight.astype(jnp.bfloat16)
+            weight_ref[rows, cols] = weight
+            acc_ref[:, cols] = acc_ref[:, cols] + dot(value_t, weight)
 
     def score_step(s, unused):
         score_rows(pl.multiple_of(PAIR + s * STEP, PAIR), STEP, (query_pair - 1 - 2 * s) * PAIR)
@@ -144,12 +145,11 @@
 
     score_rows(0, PAIR, query_pair * PAIR)
     lax.fori_loop(0, live // 2, score_step, 0)
-    log_ref[...] = jnp.max(max_ref[...], axis=0, keepdims=True)
+    peak_ref[...] = jnp.max(max_ref[...], axis=0, keepdims=True)
     mix_rows(0, PAIR)
     lax.fori_loop(0, live // 2, mix_step, 0)
-    total = jnp.sum(sum_ref[...], axis=0, keepdims=True)
-    log_ref[...] = log_ref[...] + jnp.log2(total)
-    inverse = 1.0 / total
+    inverse = 1.0 / jnp.sum(sum_ref[...], axis=0, keepdims=True)
+    inverse_ref[...] = inverse
     for h in range(HEADS):
         cols = slice(h * TOK, (h + 1) * TOK)
         mixed = acc_ref[:, cols] * inverse[:, cols]
@@ -167,14 +167,13 @@
 
 def backward_kernel(info_ref, held_ref, *refs):
     pieces, refs = refs[:6], refs[6:]
-    rows_ref, key_ref, value_ref, att_t_ref, log_ref, first_ref = refs[:6]
-    dq_ref, own, sib, refs = refs[6], refs[7:12], refs[12:17], refs[17:]
+    rows_ref, key_ref, value_ref, weight_ref, att_t_ref, inverse_ref, first_ref = refs[:7]
+    dq_ref, own, sib, refs = refs[7], refs[8:10], refs[10:12], refs[12:]
     cot_ref, grad_ref, grad_t_ref, grows_ref, acc_ref, delta_ref, out_ref = refs
     query_pair, core = info_ref[0], info_ref[1]
     at_own = pl.multiple_of(core * TOK, TOK)
     at_sib = pl.multiple_of((1 - core) * TOK, TOK)
-    first_row = first_ref[...]
-    live = query_pair - jnp.min(first_row) // PAIR + 1
+    live = query_pair - jnp.min(first_ref[...]) // PAIR + 1
     n = 0
     for ref in pieces:
         for j in range(ref.shape[0] // TOK):
@@ -183,39 +182,36 @@
     grad_ref[...] = dot_nt(held_ref[...], cot_ref[...])
     for h in range(HEADS):
         part = slice(h * TOK, (h + 1) * TOK)
-        grad_t = grad_ref[part, :].astype(jnp.bfloat16)
+        grad_t = grad_ref[part, :] * inverse_ref[:, part]
+        delta_ref[:, part] = jnp.sum(grad_t * att_t_ref[:, part].astype(jnp.float32), axis=0, keepdims=True)
+        grad_t = grad_t.astype(jnp.bfloat16)
         grad_t_ref[:, part] = grad_t
         grows_ref[part, :] = grad_t.T
-        product = grad_t.astype(jnp.float32) * att_t_ref[:, part].astype(jnp.float32)
-        delta_ref[:, part] = jnp.sum(product, axis=0, keepdims=True)
     acc_ref[...] = jnp.zeros(acc_ref.shape, jnp.float32)
     out_ref[...] = jnp.zeros(out_ref.shape, jnp.bfloat16)
 
-    def grad_rows(start, count, base):
+    def grad_rows(start, count):
         rows = pl.ds(start, count)
-        key = key_ref[rows, :]
+        key_t = key_ref[rows, :].T
         value = value_ref[rows, :]
-        key_t = key.T
-        bias = bias_of(base, count, core, query_pair, first_row)
         dkey = jnp.zeros((count, HEAD_SIZE), jnp.float32)
         dvalue = jnp.zeros((count, HEAD_SIZE), jnp.float32)
         for n in range(QROWS // CHUNK):
             cols = slice(n * CHUNK, (n + 1) * CHUNK)
-            score = dot_nt(key, rows_ref[cols, :]) * SCALE_LOG2 + bias
-            prob = jnp.exp2(score - log_ref[:, cols])
+            weight = weight_ref[rows, cols]
             gprob = dot(value, grad_t_ref[:, cols])
-            gscore = (prob * (gprob - delta_ref[:, cols])).astype(jnp.bfloat16)
-            dvalue = dvalue + dot(prob.astype(jnp.bfloat16), grows_ref[cols, :])
+            gscore = (weight.astype(jnp.float32) * (gprob - delta_ref[:, cols])).astype(jnp.bfloat16)
+            dvalue = dvalue + dot(weight, grows_ref[cols, :])
             dkey = dkey + dot(gscore, rows_ref[cols, :])
             acc_ref[:, cols] = acc_ref[:, cols] + dot(key_t, gscore)
         out_ref[rows, 0:HEAD_SIZE] = (dkey * SCALE).astype(jnp.bfloat16)
         out_ref[rows, HEAD_SIZE : 2 * HEAD_SIZE] = dvalue.astype(jnp.bfloat16)
 
     def grad_step(s, unused):
-        grad_rows(pl.multiple_of(PAIR + s * STEP, PAIR), STEP, (query_pair - 1 - 2 * s) * PAIR)
+        grad_rows(pl.multiple_of(PAIR + s * STEP, PAIR), STEP)
         return unused
 
-    grad_rows(0, PAIR, query_pair * PAIR)
+    grad_rows(0, PAIR)
     lax.fori_loop(0, live // 2, grad_step, 0)
     for j in range(SLOTS):
         array, place = PLACE[j]
@@ -249,14 +245,15 @@
 def forward(info, weight, rows, own, sib):
     outs = pl.pallas_call(
         forward_kernel,
-        in_specs=[SMEM, HBM] + [VMEM] * 11,
-        out_specs=[VMEM] * 12,
+        in_specs=[SMEM, HBM] + [VMEM] * 5,
+        out_specs=[VMEM] * 13,
         out_shape=[
             shaped(HEAD_SIZE, QROWS),
             shaped(1, QROWS, dtype=jnp.float32),
             shaped(1, TOK, dtype=jnp.int32),
             shaped(KEYS, HEAD_SIZE),
             shaped(KEYS, HEAD_SIZE),
+            shaped(KEYS, QROWS),
             shaped(QROWS, 8 * FEATURES),
         ]
         + [shaped(2, TOK, FEATURES)] * 2
@@ -267,21 +264,22 @@
             pltpu.VMEM((8, QROWS), jnp.float32),
             pltpu.VMEM((8, QROWS), jnp.float32),
             pltpu.VMEM((TOK, QROWS), jnp.bfloat16),
+            pltpu.VMEM((1, QROWS), jnp.float32),
             pltpu.SemaphoreType.DMA((8,)),
         ],
         compiler_params=params(FORWARD_MIB),
         cost_estimate=cost(9_000_000_000, 1 << 20),
     )(info, weight, rows, *own, *sib)
-    return outs[:6], outs[6:8], outs[8:]
+    return outs[:7], outs[7:9], outs[9:]
 
 
 def backward(info, pieces, rows, saved):
-    att_t, log_total, first_row, key, value, held = saved
+    att_t, inverse, first_row, key, value, weight, held = saved
     blocks = [shaped(n, TOK, 2 * HEAD_SIZE) for n in HELD]
     outs = pl.pallas_call(
         backward_kernel,
-        in_specs=[SMEM] + [VMEM] * 13,
-        out_specs=[VMEM] * 11,
+        in_specs=[SMEM] + [VMEM] * 14,
+        out_specs=[VMEM] * 5,
         out_shape=[shaped(TOK, QROWS)] + blocks + blocks,
         scratch_shapes=[
             pltpu.VMEM((TOK, 8 * FEATURES), jnp.bfloat16),
@@ -294,8 +292,8 @@
         ],
         compiler_params=params(BACKWARD_MIB),
         cost_estimate=cost(14_000_000_000, 1 << 20),
-    )(info, held, *pieces, rows, key, value, att_t, log_total, first_row)
-    return outs[0], outs[1:6], outs[6:11]
+    )(info, held, *pieces, rows, key, value, weight, att_t, inverse, first_row)
+    return outs[0], outs[1:3], outs[3:5]
 
 
 def per_device(rotated_queries, rotated_keys, value_heads_packed, out_weight, out_cotangent, doc_ids):
@@ -310,7 +308,10 @@
     z_up, z_down, z_four = along_z(out_cotangent, -1), along_z(out_cotangent, 1), along_z(out_cotangent, 4)
     near = jnp.concatenate([block, block_4], 0)
     near, rows, z_up, z_down, z_four = lax.optimization_barrier((near, rows, z_up, z_down, z_four))
-    own = [near, block_8] + [chips_on(near, by) for by in (1, 2, 3)]
+    own = [
+        jnp.concatenate([near, block_8], 0),
+        jnp.concatenate([chips_on(near, by) for by in (1, 2, 3)], 0),
+    ]
     sib = [across(piece) for piece in own]
     z_far_up = along_z(jnp.concatenate([z_up, z_four], 0), -1)
     z_far_down = along_z(jnp.concatenate([z_down, z_four], 0), 1)
@@ -331,10 +332,10 @@
     projected = low(kept + wide(sum_up) + wide(sum_four) + wide(sum_down))
 
     both = [wide(mine) + wide(across(theirs)) for mine, theirs in zip(grad_own, grad_sib)]
-    back = [wide(chips_on(low(both[2 + n]), -(n + 1))) for n in range(3)]
-    back_8 = wide(chips_on(low(both[1]), -8))
-    near_sum = both[0] + back[0] + back[1] + back[2]
-    total = near_sum[0] + back_8[0] + wide(chips_on(low(near_sum[1]), -4))
+    back = [wide(chips_on(low(both[1][2 * n : 2 * n + 2]), -(n + 1))) for n in range(3)]
+    back_8 = wide(chips_on(low(both[0][2]), -8))
+    near_sum = both[0][0:2] + back[0] + back[1] + back[2]
+    total = near_sum[0] + back_8 + wide(chips_on(low(near_sum[1]), -4))
     total = low(total)
     return projected, query_grad, total[:, :HEAD_SIZE], total[:, HEAD_SIZE:]
 

time: 87.6 us -> 81.6 us (0.932)
  the two profiles are of different devices: /device:TPU:8 before, /device:TPU:22 now
where the time goes in v4:
time: 81.6 us; the launch traced here: 80.5 us
  starting transfers between devices  33.9 us (42%)
  waiting for transfers between devices  24.7 us (30%)
  Pallas kernels  17.6 us (22%)
  other arithmetic  2.65 us (3%)
  between operations  0.87 us (1%)
    ppermute x10, starting transfers between devices, along_z(): return lax.ppermute(value, 'tensor', [(i, (i + by) % 8) for i in range(8)])  25.3 us
    ppermute x10, waiting for transfers between devices, chips_on(): lax.ppermute(value, 'dp', [(i, (i + 2 * by) % 32) for i in range(32)])  23.3 us
    pallas_call x1, Pallas kernels, backward(): pl.pallas_call(backward_kernel, in_specs=[SMEM] + [VMEM] * 14, out_specs=...  10.7 us
    ppermute x10, starting transfers between devices, chips_on(): lax.ppermute(value, 'dp', [(i, (i + 2 * by) % 32) for i in range(32)])  7.43 us
    pallas_call x1, Pallas kernels, forward(): pl.pallas_call(forward_kernel, in_specs=[SMEM, HBM] + [VMEM] * 5, out_spe...  6.91 us
  transfers between devices with their start and end apart: 24, of which 8 were waited for; matrix products, arithmetic and copies ran while one was open for 3% of the time, Pallas kernels for 22%

profile of v4, /device:TPU:22, one launch (start us, length us, event | category | flops | bytes accessed | tf_op | source)
XLA Modules:
  0.0 80.5 jit_solution(5405079585786474468)
XLA Ops:
  0.6 2.0 %collective-permute-start.2 = (bf16[128,512]{1,0:T(8,128)(2,1)}, bf16[128,512]{1,0:T(8,128)(2,1)S(1)}, u32[]{:S(2)}, u32[]{:S(2)}) collective-permute-start(bf16[128,512]{1,0:T(8,128)(2,1)} %refs_5_.1), channel_id=1, source_target_pairs={{0,1},{1,2},{2,3},{3,4},{4,5},{5,6},{6,7},{7,0},{8,9},{9,10},{10,1... | collective-permute-start | bytes 393224 | tf_op jit(solution)/shard_map/ppermute | solution.py:234
  2.6 4.0 %collective-permute-start.1 = (bf16[128,512]{1,0:T(8,128)(2,1)}, bf16[128,512]{1,0:T(8,128)(2,1)S(1)}, u32[]{:S(2)}, u32[]{:S(2)}) collective-permute-start(bf16[128,512]{1,0:T(8,128)(2,1)} %refs_5_.1), channel_id=1, source_target_pairs={{0,7},{1,0},{2,1},{3,2},{4,3},{5,4},{6,5},{7,6},{8,15},{9,8},{10,9... | collective-permute-start | bytes 393224 | tf_op jit(solution)/shard_map/ppermute | solution.py:234
  6.7 4.5 %collective-permute-start.3 = (bf16[128,512]{1,0:T(8,128)(2,1)}, bf16[128,512]{1,0:T(8,128)(2,1)S(1)}, u32[]{:S(2)}, u32[]{:S(2)}) collective-permute-start(bf16[128,512]{1,0:T(8,128)(2,1)} %refs_5_.1), channel_id=1, source_target_pairs={{0,4},{1,5},{2,6},{3,7},{4,0},{5,1},{6,2},{7,3},{8,12},{9,13},{10,... | collective-permute-start | bytes 393224 | tf_op jit(solution)/shard_map/ppermute | solution.py:234
  11.1 0.7 convert_element_type.97
  11.8 0.8 maximum_bitcast_fusion
  13.2 3.8 %collective-permute-done = bf16[1,144,256]{2,1,0:T(8,128)(2,1)S(1)} collective-permute-done((bf16[1,144,256]{2,1,0:T(8,128)(2,1)S(1)}, bf16[1,144,256]{2,1,0:T(8,128)(2,1)S(1)}, u32[]{:S(2)}, u32[]{:S(2)}) %collective-permute-start) | collective-permute-done | bytes 73760 | tf_op jit(solution)/shard_map/ppermute | solution.py:226
  17.1 1.4 %collective-permute-done.3.refs_3_ = bf16[128,512]{1,0:T(8,128)(2,1)S(1)} collective-permute-done((bf16[128,512]{1,0:T(8,128)(2,1)}, bf16[128,512]{1,0:T(8,128)(2,1)S(1)}, u32[]{:S(2)}, u32[]{:S(2)}) %collective-permute-start.3) | collective-permute-done | bytes 131104 | tf_op jit(solution)/shard_map/ppermute | solution.py:234
  18.5 1.3 %collective-permute-start.5 = (bf16[2,144,256]{2,1,0:T(8,128)(2,1)S(1)}, bf16[2,144,256]{2,1,0:T(8,128)(2,1)S(1)}, u32[]{:S(2)}, u32[]{:S(2)}) collective-permute-start(bf16[2,144,256]{2,1,0:T(8,128)(2,1)S(1)} %pad_maximum_fusion.2), channel_id=1, source_target_pairs={{0,16},{8,24},{16,32},{24,40},{32,48},{40,56},{48,64},{56,72},{64,... | collective-permute-start | bytes 442376 | tf_op jit(solution)/shard_map/ppermute | solution.py:226
  20.3 2.4 %collective-permute-start.4 = (bf16[1,144,256]{2,1,0:T(8,128)(2,1)S(1)}, bf16[1,144,256]{2,1,0:T(8,128)(2,1)S(1)}, u32[]{:S(2)}, u32[]{:S(2)}) collective-permute-start(bf16[1,144,256]{2,1,0:T(8,128)(2,1)S(1)} %maximum_bitcast_fusion), channel_id=1, source_target_pairs={{0,128},{8,136},{16,144},{24,152},{32,160},{40,168},{48,176},{56,1... | collective-permute-start | bytes 221192 | tf_op jit(solution)/shard_map/ppermute | solution.py:226
  22.7 2.3 %collective-permute-start.7 = (bf16[2,144,256]{2,1,0:T(8,128)(2,1)S(1)}, bf16[2,144,256]{2,1,0:T(8,128)(2,1)S(1)}, u32[]{:S(2)}, u32[]{:S(2)}) collective-permute-start(bf16[2,144,256]{2,1,0:T(8,128)(2,1)S(1)} %pad_maximum_fusion.2), channel_id=1, source_target_pairs={{0,48},{8,56},{16,64},{24,72},{32,80},{40,88},{48,96},{56,104},{64... | collective-permute-start | bytes 442376 | tf_op jit(solution)/shard_map/ppermute | solution.py:226
  25.0 1.4 %collective-permute-done.6 = bf16[2,144,256]{2,1,0:T(8,128)(2,1)S(1)} collective-permute-done((bf16[2,144,256]{2,1,0:T(8,128)(2,1)S(1)}, bf16[2,144,256]{2,1,0:T(8,128)(2,1)S(1)}, u32[]{:S(2)}, u32[]{:S(2)}) %collective-permute-start.6) | collective-permute-done | bytes 147488 | tf_op jit(solution)/shard_map/ppermute | solution.py:226
  26.4 3.7 %collective-permute-done.7 = bf16[2,144,256]{2,1,0:T(8,128)(2,1)S(1)} collective-permute-done((bf16[2,144,256]{2,1,0:T(8,128)(2,1)S(1)}, bf16[2,144,256]{2,1,0:T(8,128)(2,1)S(1)}, u32[]{:S(2)}, u32[]{:S(2)}) %collective-permute-start.7) | collective-permute-done | bytes 147488 | tf_op jit(solution)/shard_map/ppermute | solution.py:226
  30.9 1.5 %collective-permute-start.11 = (bf16[256,512]{1,0:T(8,128)(2,1)S(1)}, bf16[256,512]{1,0:T(8,128)(2,1)S(1)}, u32[]{:S(2)}, u32[]{:S(2)}) collective-permute-start(bf16[256,512]{1,0:T(8,128)(2,1)S(1)} %get-tuple-element.64), channel_id=1, source_target_pairs={{0,1},{1,2},{2,3},{3,4},{4,5},{5,6},{6,7},{7,0},{8,9},{9,10},{10,1... | collective-permute-start | bytes 786440 | tf_op jit(solution)/shard_map/ppermute | solution.py:234
  32.4 1.8 %collective-permute-start.10 = (bf16[256,512]{1,0:T(8,128)(2,1)S(1)}, bf16[256,512]{1,0:T(8,128)(2,1)S(1)}, u32[]{:S(2)}, u32[]{:S(2)}) collective-permute-start(bf16[256,512]{1,0:T(8,128)(2,1)S(1)} %get-tuple-element.65), channel_id=1, source_target_pairs={{0,7},{1,0},{2,1},{3,2},{4,3},{5,4},{6,5},{7,6},{8,15},{9,8},{10,9... | collective-permute-start | bytes 786440 | tf_op jit(solution)/shard_map/ppermute | solution.py:234
  34.2 6.9 %shard_map.93 = (bf16[128,1024]{1,0:T(8,128)(2,1)S(1)}, f32[1,1024]{1,0:T(1,128)S(1)}, s32[1,128]{1,0:T(1,128)S(1)}, bf16[2304,128]{1,0:T(8,128)(2,1)S(1)}, bf16...) custom-call(s32[3]{0:T(128)S(1)} %pad_add_fusion.info_ref, ...), custom_call_target="tpu_custom_call" | custom-call | flops 8999999488 | bytes 1048576 | tf_op jit(solution)/shard_map/pallas_call | solution.py:246
  41.6 3.0 %collective-permute-start.13 = (bf16[2,128,512]{2,1,0:T(8,128)(2,1)S(1)}, bf16[2,128,512]{2,1,0:T(8,128)(2,1)S(1)}, u32[]{:S(2)}, u32[]{:S(2)}) collective-permute-start(bf16[2,128,512]{2,1,0:T(8,128)(2,1)S(1)} %get-tuple-element.48), channel_id=1, source_target_pairs={{0,7},{1,0},{2,1},{3,2},{4,3},{5,4},{6,5},{7,6},{8,15},{9,8},{10,9... | collective-permute-start | bytes 786440 | tf_op jit(solution)/shard_map/ppermute | solution.py:234
  44.7 10.7 %shard_map.94 = (bf16[128,1024]{1,0:T(8,128)(2,1)}, bf16[3,128,256]{2,1,0:T(8,128)(2,1)S(1)}, bf16[6,128,256]{2,1,0:T(8,128)(2,1)S(1)}, bf16[3,128,256]{2,1,0:T(8,128)(2,1)S(1)}, bf16[6,128,256]{2,1,0:T(8,128)(2,1)S(1)}) custom-call(s32[3]{0:T(128)S(1)} %pad_add_fusion.info_ref, bf16[1024,4096]{1,0:T(8,128)(2,1)S(1)} %get-tuple-element.35.held_ref, ...), custom_call_target="tpu_custom_call" | custom-call | flops 14000000000 | bytes 1048576 | tf_op jit(solution)/shard_map/pallas_call | solution.py:279
  56.1 4.8 %collective-permute-start.15 = (bf16[128,512]{1,0:T(8,128)(2,1)S(1)}, bf16[128,512]{1,0:T(8,128)(2,1)S(1)}, u32[]{:S(2)}, u32[]{:S(2)}) collective-permute-start(bf16[128,512]{1,0:T(8,128)(2,1)S(1)} %get-tuple-element.62), channel_id=1, source_target_pairs={{0,4},{1,5},{2,6},{3,7},{4,0},{5,1},{6,2},{7,3},{8,12},{9,13},{10,... | collective-permute-start | bytes 393224 | tf_op jit(solution)/shard_map/ppermute | solution.py:234
  61.4 6.2 %collective-permute-done.19 = bf16[2,128,256]{2,1,0:T(8,128)(2,1)S(1)} collective-permute-done((bf16[2,128,256]{2,1,0:T(8,128)(2,1)S(1)}, bf16[2,128,256]{2,1,0:T(8,128)(2,1)S(1)}, u32[]{:S(2)}, u32[]{:S(2)}) %collective-permute-start.19) | collective-permute-done | bytes 131104 | tf_op jit(solution)/shard_map/ppermute | solution.py:226
  67.6 3.1 %collective-permute-start.16 = (bf16[128,512]{1,0:T(8,128)(2,1)S(1)}, bf16[128,512]{1,0:T(8,128)(2,1)S(1)}, u32[]{:S(2)}, u32[]{:S(2)}) collective-permute-start(bf16[128,512]{1,0:T(8,128)(2,1)S(1)} %get-tuple-element.63), channel_id=1, source_target_pairs={{0,7},{1,0},{2,1},{3,2},{4,3},{5,4},{6,5},{7,6},{8,15},{9,8},{10,9... | collective-permute-start | bytes 393224 | tf_op jit(solution)/shard_map/ppermute | solution.py:234
  70.7 3.5 %collective-permute-done.20 = bf16[2,128,256]{2,1,0:T(8,128)(2,1)S(1)} collective-permute-done((bf16[2,128,256]{2,1,0:T(8,128)(2,1)S(1)}, bf16[2,128,256]{2,1,0:T(8,128)(2,1)S(1)}, u32[]{:S(2)}, u32[]{:S(2)}) %collective-permute-start.20) | collective-permute-done | bytes 131104 | tf_op jit(solution)/shard_map/ppermute | solution.py:226
  74.4 0.7 add_convert_fusion.1
  75.1 1.3 %collective-permute-done.22 = bf16[128,256]{1,0:T(8,128)(2,1)S(1)} collective-permute-done((bf16[128,256]{1,0:T(8,128)(2,1)S(1)}, bf16[128,256]{1,0:T(8,128)(2,1)S(1)}, u32[]{:S(2)}, u32[]{:S(2)}) %collective-permute-start.22) | collective-permute-done | bytes 65568 | tf_op jit(solution)/shard_map/ppermute | solution.py:226
  76.4 3.4 %collective-permute-done.23 = bf16[128,256]{1,0:T(8,128)(2,1)S(1)} collective-permute-done((bf16[128,256]{1,0:T(8,128)(2,1)S(1)}, bf16[128,256]{1,0:T(8,128)(2,1)S(1)}, u32[]{:S(2)}, u32[]{:S(2)}) %collective-permute-start.23) | collective-permute-done | bytes 65568 | tf_op jit(solution)/shard_map/ppermute | solution.py:226
  (53 shorter events, 4.5 us)
Async XLA Ops:
  0.6 16.4 %collective-permute-start.2 = (bf16[128,512]{1,0:T(8,128)(2,1)}, bf16[128,512]{1,0:T(8,128)(2,1)S(1)}, u32[]{:S(2)}, u32[]{:S(2)}) collective-permute-start(bf16[128,512]{1,0:T(8,128)(2,1)} %refs_5_.1), channel_id=1, source_target_pairs={{0,1},{1,2},{2,3},{3,4},{4,5},{5,6},{6,7},{7,0},{8,9},{9,10},{10,1... | collective-permute-start | bytes 393224 | tf_op jit(solution)/shard_map/ppermute | solution.py:234
  2.6 14.4 %collective-permute-start.1 = (bf16[128,512]{1,0:T(8,128)(2,1)}, bf16[128,512]{1,0:T(8,128)(2,1)S(1)}, u32[]{:S(2)}, u32[]{:S(2)}) collective-permute-start(bf16[128,512]{1,0:T(8,128)(2,1)} %refs_5_.1), channel_id=1, source_target_pairs={{0,7},{1,0},{2,1},{3,2},{4,3},{5,4},{6,5},{7,6},{8,15},{9,8},{10,9... | collective-permute-start | bytes 393224 | tf_op jit(solution)/shard_map/ppermute | solution.py:234
  6.7 11.8 %collective-permute-start.3 = (bf16[128,512]{1,0:T(8,128)(2,1)}, bf16[128,512]{1,0:T(8,128)(2,1)S(1)}, u32[]{:S(2)}, u32[]{:S(2)}) collective-permute-start(bf16[128,512]{1,0:T(8,128)(2,1)} %refs_5_.1), channel_id=1, source_target_pairs={{0,4},{1,5},{2,6},{3,7},{4,0},{5,1},{6,2},{7,3},{8,12},{9,13},{10,... | collective-permute-start | bytes 393224 | tf_op jit(solution)/shard_map/ppermute | solution.py:234
  12.6 4.4 %collective-permute-start = (bf16[1,144,256]{2,1,0:T(8,128)(2,1)S(1)}, bf16[1,144,256]{2,1,0:T(8,128)(2,1)S(1)}, u32[]{:S(2)}, u32[]{:S(2)}) collective-permute-start(bf16[1,144,256]{2,1,0:T(8,128)(2,1)S(1)} %maximum_bitcast_fusion), channel_id=1, source_target_pairs={{0,64},{8,72},{16,80},{24,88},{32,96},{40,104},{48,112},{56,120},{... | collective-permute-start | bytes 221192 | tf_op jit(solution)/shard_map/ppermute | solution.py:226
  18.5 6.5 %collective-permute-start.5 = (bf16[2,144,256]{2,1,0:T(8,128)(2,1)S(1)}, bf16[2,144,256]{2,1,0:T(8,128)(2,1)S(1)}, u32[]{:S(2)}, u32[]{:S(2)}) collective-permute-start(bf16[2,144,256]{2,1,0:T(8,128)(2,1)S(1)} %pad_maximum_fusion.2), channel_id=1, source_target_pairs={{0,16},{8,24},{16,32},{24,40},{32,48},{40,56},{48,64},{56,72},{64,... | collective-permute-start | bytes 442376 | tf_op jit(solution)/shard_map/ppermute | solution.py:226
  19.7 6.6 %collective-permute-start.6 = (bf16[2,144,256]{2,1,0:T(8,128)(2,1)S(1)}, bf16[2,144,256]{2,1,0:T(8,128)(2,1)S(1)}, u32[]{:S(2)}, u32[]{:S(2)}) collective-permute-start(bf16[2,144,256]{2,1,0:T(8,128)(2,1)S(1)} %pad_maximum_fusion.2), channel_id=1, source_target_pairs={{0,32},{8,40},{16,48},{24,56},{32,64},{40,72},{48,80},{56,88},{64,... | collective-permute-start | bytes 442376 | tf_op jit(solution)/shard_map/ppermute | solution.py:226
  20.3 9.9 %collective-permute-start.4 = (bf16[1,144,256]{2,1,0:T(8,128)(2,1)S(1)}, bf16[1,144,256]{2,1,0:T(8,128)(2,1)S(1)}, u32[]{:S(2)}, u32[]{:S(2)}) collective-permute-start(bf16[1,144,256]{2,1,0:T(8,128)(2,1)S(1)} %maximum_bitcast_fusion), channel_id=1, source_target_pairs={{0,128},{8,136},{16,144},{24,152},{32,160},{40,168},{48,176},{56,1... | collective-permute-start | bytes 221192 | tf_op jit(solution)/shard_map/ppermute | solution.py:226
  22.7 7.4 %collective-permute-start.7 = (bf16[2,144,256]{2,1,0:T(8,128)(2,1)S(1)}, bf16[2,144,256]{2,1,0:T(8,128)(2,1)S(1)}, u32[]{:S(2)}, u32[]{:S(2)}) collective-permute-start(bf16[2,144,256]{2,1,0:T(8,128)(2,1)S(1)} %pad_maximum_fusion.2), channel_id=1, source_target_pairs={{0,48},{8,56},{16,64},{24,72},{32,80},{40,88},{48,96},{56,104},{64... | collective-permute-start | bytes 442376 | tf_op jit(solution)/shard_map/ppermute | solution.py:226
  30.1 4.2 %collective-permute-start.9 = (bf16[6,144,256]{2,1,0:T(8,128)(2,1)S(1)}, bf16[6,144,256]{2,1,0:T(8,128)(2,1)S(1)}, u32[]{:S(2)}, u32[]{:S(2)}) collective-permute-start(bf16[6,144,256]{2,1,0:T(8,128)(2,1)S(1)} %constant_dynamic-update-slice_fusion.2.refs_1_), channel_id=1, source_target_pairs={{0,8},{8,0},{16,24},{24,16},{32,40},{40,32},{48,56},{56,48},{64,72... | collective-permute-start | bytes 1327112 | tf_op jit(solution)/shard_map/ppermute | solution.py:230
  30.2 4.0 %collective-permute-start.8 = (bf16[3,144,256]{2,1,0:T(8,128)(2,1)S(1)}, bf16[3,144,256]{2,1,0:T(8,128)(2,1)S(1)}, u32[]{:S(2)}, u32[]{:S(2)}) collective-permute-start(bf16[3,144,256]{2,1,0:T(8,128)(2,1)S(1)} %constant_dynamic-update-slice_fusion.refs_0_), channel_id=1, source_target_pairs={{0,8},{8,0},{16,24},{24,16},{32,40},{40,32},{48,56},{56,48},{64,72... | collective-permute-start | bytes 663560 | tf_op jit(solution)/shard_map/ppermute | solution.py:230
  30.9 13.7 %collective-permute-start.11 = (bf16[256,512]{1,0:T(8,128)(2,1)S(1)}, bf16[256,512]{1,0:T(8,128)(2,1)S(1)}, u32[]{:S(2)}, u32[]{:S(2)}) collective-permute-start(bf16[256,512]{1,0:T(8,128)(2,1)S(1)} %get-tuple-element.64), channel_id=1, source_target_pairs={{0,1},{1,2},{2,3},{3,4},{4,5},{5,6},{6,7},{7,0},{8,9},{9,10},{10,1... | collective-permute-start | bytes 786440 | tf_op jit(solution)/shard_map/ppermute | solution.py:234
  32.4 12.2 %collective-permute-start.10 = (bf16[256,512]{1,0:T(8,128)(2,1)S(1)}, bf16[256,512]{1,0:T(8,128)(2,1)S(1)}, u32[]{:S(2)}, u32[]{:S(2)}) collective-permute-start(bf16[256,512]{1,0:T(8,128)(2,1)S(1)} %get-tuple-element.65), channel_id=1, source_target_pairs={{0,7},{1,0},{2,1},{3,2},{4,3},{5,4},{6,5},{7,6},{8,15},{9,8},{10,9... | collective-permute-start | bytes 786440 | tf_op jit(solution)/shard_map/ppermute | solution.py:234
  41.2 14.2 %collective-permute-start.12 = (bf16[2,128,512]{2,1,0:T(8,128)(2,1)S(1)}, bf16[2,128,512]{2,1,0:T(8,128)(2,1)S(1)}, u32[]{:S(2)}, u32[]{:S(2)}) collective-permute-start(bf16[2,128,512]{2,1,0:T(8,128)(2,1)S(1)} %get-tuple-element.47), channel_id=1, source_target_pairs={{0,1},{1,2},{2,3},{3,4},{4,5},{5,6},{6,7},{7,0},{8,9},{9,10},{10,1... | collective-permute-start | bytes 786440 | tf_op jit(solution)/shard_map/ppermute | solution.py:234
  41.6 13.8 %collective-permute-start.13 = (bf16[2,128,512]{2,1,0:T(8,128)(2,1)S(1)}, bf16[2,128,512]{2,1,0:T(8,128)(2,1)S(1)}, u32[]{:S(2)}, u32[]{:S(2)}) collective-permute-start(bf16[2,128,512]{2,1,0:T(8,128)(2,1)S(1)} %get-tuple-element.48), channel_id=1, source_target_pairs={{0,7},{1,0},{2,1},{3,2},{4,3},{5,4},{6,5},{7,6},{8,15},{9,8},{10,9... | collective-permute-start | bytes 786440 | tf_op jit(solution)/shard_map/ppermute | solution.py:234
  55.4 5.5 %collective-permute-start.17 = (bf16[3,128,256]{2,1,0:T(8,128)(2,1)S(1)}, bf16[3,128,256]{2,1,0:T(8,128)(2,1)S(1)}, u32[]{:S(2)}, u32[]{:S(2)}) collective-permute-start(bf16[3,128,256]{2,1,0:T(8,128)(2,1)S(1)} %get-tuple-element.55), channel_id=1, source_target_pairs={{0,8},{8,0},{16,24},{24,16},{32,40},{40,32},{48,56},{56,48},{64,72... | collective-permute-start | bytes 589832 | tf_op jit(solution)/shard_map/ppermute | solution.py:230
  55.4 5.6 %collective-permute-start.18 = (bf16[6,128,256]{2,1,0:T(8,128)(2,1)S(1)}, bf16[6,128,256]{2,1,0:T(8,128)(2,1)S(1)}, u32[]{:S(2)}, u32[]{:S(2)}) collective-permute-start(bf16[6,128,256]{2,1,0:T(8,128)(2,1)S(1)} %get-tuple-element.57), channel_id=1, source_target_pairs={{0,8},{8,0},{16,24},{24,16},{32,40},{40,32},{48,56},{56,48},{64,72... | collective-permute-start | bytes 1179656 | tf_op jit(solution)/shard_map/ppermute | solution.py:230
  56.0 18.3 %collective-permute-start.14 = (bf16[128,512]{1,0:T(8,128)(2,1)S(1)}, bf16[128,512]{1,0:T(8,128)(2,1)S(1)}, u32[]{:S(2)}, u32[]{:S(2)}) collective-permute-start(bf16[128,512]{1,0:T(8,128)(2,1)S(1)} %get-tuple-element.61), channel_id=1, source_target_pairs={{0,1},{1,2},{2,3},{3,4},{4,5},{5,6},{6,7},{7,0},{8,9},{9,10},{10,1... | collective-permute-start | bytes 393224 | tf_op jit(solution)/shard_map/ppermute | solution.py:234
  56.1 18.3 %collective-permute-start.15 = (bf16[128,512]{1,0:T(8,128)(2,1)S(1)}, bf16[128,512]{1,0:T(8,128)(2,1)S(1)}, u32[]{:S(2)}, u32[]{:S(2)}) collective-permute-start(bf16[128,512]{1,0:T(8,128)(2,1)S(1)} %get-tuple-element.62), channel_id=1, source_target_pairs={{0,4},{1,5},{2,6},{3,7},{4,0},{5,1},{6,2},{7,3},{8,12},{9,13},{10,... | collective-permute-start | bytes 393224 | tf_op jit(solution)/shard_map/ppermute | solution.py:234
  61.1 6.5 %collective-permute-start.19 = (bf16[2,128,256]{2,1,0:T(8,128)(2,1)S(1)}, bf16[2,128,256]{2,1,0:T(8,128)(2,1)S(1)}, u32[]{:S(2)}, u32[]{:S(2)}) collective-permute-start(bf16[2,128,256]{2,1,0:T(8,128)(2,1)S(1)} %get-tuple-element.58), channel_id=1, source_target_pairs={{0,240},{8,248},{16,0},{24,8},{32,16},{40,24},{48,32},{56,40},{64,... | collective-permute-start | bytes 393224 | tf_op jit(solution)/shard_map/ppermute | solution.py:226
  61.2 9.5 %collective-permute-start.21 = (bf16[2,128,256]{2,1,0:T(8,128)(2,1)S(1)}, bf16[2,128,256]{2,1,0:T(8,128)(2,1)S(1)}, u32[]{:S(2)}, u32[]{:S(2)}) collective-permute-start(bf16[2,128,256]{2,1,0:T(8,128)(2,1)S(1)} %get-tuple-element.59), channel_id=1, source_target_pairs={{0,208},{8,216},{16,224},{24,232},{32,240},{40,248},{48,0},{56,8},... | collective-permute-start | bytes 393224 | tf_op jit(solution)/shard_map/ppermute | solution.py:226
  61.3 12.9 %collective-permute-start.20 = (bf16[2,128,256]{2,1,0:T(8,128)(2,1)S(1)}, bf16[2,128,256]{2,1,0:T(8,128)(2,1)S(1)}, u32[]{:S(2)}, u32[]{:S(2)}) collective-permute-start(bf16[2,128,256]{2,1,0:T(8,128)(2,1)S(1)} %get-tuple-element.60), channel_id=1, source_target_pairs={{0,224},{8,232},{16,240},{24,248},{32,0},{40,8},{48,16},{56,24},{6... | collective-permute-start | bytes 393224 | tf_op jit(solution)/shard_map/ppermute | solution.py:226
  67.6 6.8 %collective-permute-start.16 = (bf16[128,512]{1,0:T(8,128)(2,1)S(1)}, bf16[128,512]{1,0:T(8,128)(2,1)S(1)}, u32[]{:S(2)}, u32[]{:S(2)}) collective-permute-start(bf16[128,512]{1,0:T(8,128)(2,1)S(1)} %get-tuple-element.63), channel_id=1, source_target_pairs={{0,7},{1,0},{2,1},{3,2},{4,3},{5,4},{6,5},{7,6},{8,15},{9,8},{10,9... | collective-permute-start | bytes 393224 | tf_op jit(solution)/shard_map/ppermute | solution.py:234
  70.7 5.8 %collective-permute-start.22 = (bf16[128,256]{1,0:T(8,128)(2,1)S(1)}, bf16[128,256]{1,0:T(8,128)(2,1)S(1)}, u32[]{:S(2)}, u32[]{:S(2)}) collective-permute-start(bf16[128,256]{1,0:T(8,128)(2,1)S(1)} %fusion.8), channel_id=1, source_target_pairs={{0,128},{8,136},{16,144},{24,152},{32,160},{40,168},{48,176},{56,1... | collective-permute-start | bytes 196616 | tf_op jit(solution)/shard_map/ppermute | solution.py:226
  74.3 5.6 %collective-permute-start.23 = (bf16[128,256]{1,0:T(8,128)(2,1)S(1)}, bf16[128,256]{1,0:T(8,128)(2,1)S(1)}, u32[]{:S(2)}, u32[]{:S(2)}) collective-permute-start(bf16[128,256]{1,0:T(8,128)(2,1)S(1)} %fusion.9), channel_id=1, source_target_pairs={{0,192},{8,200},{16,208},{24,216},{32,224},{40,232},{48,240},{56,2... | collective-permute-start | bytes 196616 | tf_op jit(solution)/shard_map/ppermute | solution.py:226
  (2 other events, 24.8 us)

commit v5 on v4

--- a/solution.py
+++ b/solution.py
@@ -307,7 +307,7 @@
     block_8 = chips_on(block, 8)
     z_up, z_down, z_four = along_z(out_cotangent, -1), along_z(out_cotangent, 1), along_z(out_cotangent, 4)
     near = jnp.concatenate([block, block_4], 0)
-    near, rows, z_up, z_down, z_four = lax.optimization_barrier((near, rows, z_up, z_down, z_four))
+    near, rows = lax.optimization_barrier((near, rows))
     own = [
         jnp.concatenate([near, block_8], 0),
         jnp.concatenate([chips_on(near, by) for by in (1, 2, 3)], 0),

time: 81.6 us -> 77.3 us (0.947)
  the two profiles are of different devices: /device:TPU:22 before, /device:TPU:8 now
where the time goes in v5:
time: 77.3 us; the launch traced here: 76 us
  starting transfers between devices  43.9 us (57%)
  waiting for transfers between devices  15.4 us (20%)
  Pallas kernels  12.4 us (16%)
  other arithmetic  2.69 us (3%)
  between operations  0.83 us (1%)
  local copies, waits for them, and re-layouts  0.8 us (1%)
    ppermute x10, starting transfers between devices, along_z(): return lax.ppermute(value, 'tensor', [(i, (i + by) % 8) for i in range(8)])  21.6 us
    ppermute x10, starting transfers between devices, chips_on(): lax.ppermute(value, 'dp', [(i, (i + 2 * by) % 32) for i in range(32)])  21.1 us
    ppermute x10, waiting for transfers between devices, chips_on(): lax.ppermute(value, 'dp', [(i, (i + 2 * by) % 32) for i in range(32)])  12.3 us
    pallas_call x1, Pallas kernels, backward(): pl.pallas_call(backward_kernel, in_specs=[SMEM] + [VMEM] * 14, out_specs=...  6.67 us
    pallas_call x1, Pallas kernels, forward(): pl.pallas_call(forward_kernel, in_specs=[SMEM, HBM] + [VMEM] * 5, out_spe...  5.72 us
    ppermute x10, waiting for transfers between devices, along_z(): return lax.ppermute(value, 'tensor', [(i, (i + by) % 8) for i in range(8)])  3.14 us
  transfers between devices with their start and end apart: 24, of which 6 were waited for; matrix products, arithmetic and copies ran while one was open for 2% of the time, Pallas kernels for 16%

profile of v5, /device:TPU:8, one launch (start us, length us, event | category | flops | bytes accessed | tf_op | source)
XLA Modules:
  0.0 76.0 jit_solution(17046382531813755126)
XLA Ops:
  1.4 0.8 %maximum_bitcast_fusion = bf16[1,144,256]{2,1,0:T(8,128)(2,1)S(1)} fusion(bf16[16,256]{1,0:T(8,128)(2,1)S(1)} %broadcast_in_dim.4, bf16[128,128]{1,0:T(8,128)(2,1)} %param.8, bf16[128,128]{1,0:T(8,128)(2,1)} %param.7), kind=kLoop, calls=%fused_computation.23 | loop fusion | flops 221184 | bytes 147456 | tf_op jit(solution)/shard_map/broadcast_in_dim | solution.py:60
  2.1 1.6 %collective-permute-start = (bf16[1,144,256]{2,1,0:T(8,128)(2,1)S(1)}, bf16[1,144,256]{2,1,0:T(8,128)(2,1)S(1)}, u32[]{:S(2)}, u32[]{:S(2)}) collective-permute-start(bf16[1,144,256]{2,1,0:T(8,128)(2,1)S(1)} %maximum_bitcast_fusion), channel_id=1, source_target_pairs={{0,64},{8,72},{16,80},{24,88},{32,96},{40,104},{48,112},{56,120},{... | collective-permute-start | bytes 221192 | tf_op jit(solution)/shard_map/ppermute | solution.py:226
  3.8 4.0 %collective-permute-done = bf16[1,144,256]{2,1,0:T(8,128)(2,1)S(1)} collective-permute-done((bf16[1,144,256]{2,1,0:T(8,128)(2,1)S(1)}, bf16[1,144,256]{2,1,0:T(8,128)(2,1)S(1)}, u32[]{:S(2)}, u32[]{:S(2)}) %collective-permute-start) | collective-permute-done | bytes 73760 | tf_op jit(solution)/shard_map/ppermute | solution.py:226
  7.8 1.7 %collective-permute-start.2 = (bf16[2,144,256]{2,1,0:T(8,128)(2,1)S(1)}, bf16[2,144,256]{2,1,0:T(8,128)(2,1)S(1)}, u32[]{:S(2)}, u32[]{:S(2)}) collective-permute-start(bf16[2,144,256]{2,1,0:T(8,128)(2,1)S(1)} %pad_maximum_fusion.2), channel_id=1, source_target_pairs={{0,16},{8,24},{16,32},{24,40},{32,48},{40,56},{48,64},{56,72},{64,... | collective-permute-start | bytes 442376 | tf_op jit(solution)/shard_map/ppermute | solution.py:226
  9.5 0.9 %collective-permute-start.3 = (bf16[2,144,256]{2,1,0:T(8,128)(2,1)S(1)}, bf16[2,144,256]{2,1,0:T(8,128)(2,1)S(1)}, u32[]{:S(2)}, u32[]{:S(2)}) collective-permute-start(bf16[2,144,256]{2,1,0:T(8,128)(2,1)S(1)} %pad_maximum_fusion.2), channel_id=1, source_target_pairs={{0,32},{8,40},{16,48},{24,56},{32,64},{40,72},{48,80},{56,88},{64,... | collective-permute-start | bytes 442376 | tf_op jit(solution)/shard_map/ppermute | solution.py:226
  10.4 2.5 %collective-permute-start.1 = (bf16[1,144,256]{2,1,0:T(8,128)(2,1)S(1)}, bf16[1,144,256]{2,1,0:T(8,128)(2,1)S(1)}, u32[]{:S(2)}, u32[]{:S(2)}) collective-permute-start(bf16[1,144,256]{2,1,0:T(8,128)(2,1)S(1)} %maximum_bitcast_fusion), channel_id=1, source_target_pairs={{0,128},{8,136},{16,144},{24,152},{32,160},{40,168},{48,176},{56,1... | collective-permute-start | bytes 221192 | tf_op jit(solution)/shard_map/ppermute | solution.py:226
  12.9 7.2 %collective-permute-start.8 = (bf16[128,512]{1,0:T(8,128)(2,1)}, bf16[128,512]{1,0:T(8,128)(2,1)S(1)}, u32[]{:S(2)}, u32[]{:S(2)}) collective-permute-start(bf16[128,512]{1,0:T(8,128)(2,1)} %refs_5_.1), channel_id=1, source_target_pairs={{0,4},{1,5},{2,6},{3,7},{4,0},{5,1},{6,2},{7,3},{8,12},{9,13},{10,... | collective-permute-start | bytes 393224 | tf_op jit(solution)/shard_map/ppermute | solution.py:234
  20.2 1.8 %collective-permute-start.4 = (bf16[2,144,256]{2,1,0:T(8,128)(2,1)S(1)}, bf16[2,144,256]{2,1,0:T(8,128)(2,1)S(1)}, u32[]{:S(2)}, u32[]{:S(2)}) collective-permute-start(bf16[2,144,256]{2,1,0:T(8,128)(2,1)S(1)} %pad_maximum_fusion.2), channel_id=1, source_target_pairs={{0,48},{8,56},{16,64},{24,72},{32,80},{40,88},{48,96},{56,104},{64... | collective-permute-start | bytes 442376 | tf_op jit(solution)/shard_map/ppermute | solution.py:226
  22.0 2.0 %collective-permute-start.10 = (bf16[128,512]{1,0:T(8,128)(2,1)}, bf16[128,512]{1,0:T(8,128)(2,1)S(1)}, u32[]{:S(2)}, u32[]{:S(2)}) collective-permute-start(bf16[128,512]{1,0:T(8,128)(2,1)} %refs_5_.1), channel_id=1, source_target_pairs={{0,1},{1,2},{2,3},{3,4},{4,5},{5,6},{6,7},{7,0},{8,9},{9,10},{10,1... | collective-permute-start | bytes 393224 | tf_op jit(solution)/shard_map/ppermute | solution.py:234
  24.0 3.4 %collective-permute-done.4 = bf16[2,144,256]{2,1,0:T(8,128)(2,1)S(1)} collective-permute-done((bf16[2,144,256]{2,1,0:T(8,128)(2,1)S(1)}, bf16[2,144,256]{2,1,0:T(8,128)(2,1)S(1)}, u32[]{:S(2)}, u32[]{:S(2)}) %collective-permute-start.4) | collective-permute-done | bytes 147488 | tf_op jit(solution)/shard_map/ppermute | solution.py:226
  28.2 3.1 %collective-permute-done.10.refs_4_ = bf16[128,512]{1,0:T(8,128)(2,1)S(1)} collective-permute-done((bf16[128,512]{1,0:T(8,128)(2,1)}, bf16[128,512]{1,0:T(8,128)(2,1)S(1)}, u32[]{:S(2)}, u32[]{:S(2)}) %collective-permute-start.10) | collective-permute-done | bytes 131104 | tf_op jit(solution)/shard_map/ppermute | solution.py:234
  31.5 3.2 %collective-permute-start.9 = (bf16[256,512]{1,0:T(8,128)(2,1)S(1)}, bf16[256,512]{1,0:T(8,128)(2,1)S(1)}, u32[]{:S(2)}, u32[]{:S(2)}) collective-permute-start(bf16[256,512]{1,0:T(8,128)(2,1)S(1)} %get-tuple-element.59), channel_id=1, source_target_pairs={{0,7},{1,0},{2,1},{3,2},{4,3},{5,4},{6,5},{7,6},{8,15},{9,8},{10,9... | collective-permute-start | bytes 786440 | tf_op jit(solution)/shard_map/ppermute | solution.py:234
  34.7 5.7 %shard_map.93 = (bf16[128,1024]{1,0:T(8,128)(2,1)S(1)}, f32[1,1024]{1,0:T(1,128)S(1)}, s32[1,128]{1,0:T(1,128)S(1)}, bf16[2304,128]{1,0:T(8,128)(2,1)S(1)}, bf16...) custom-call(s32[3]{0:T(128)S(1)} %pad_add_fusion.info_ref, ...), custom_call_target="tpu_custom_call" | custom-call | flops 8999999488 | bytes 1048576 | tf_op jit(solution)/shard_map/pallas_call | solution.py:246
  40.7 3.2 %collective-permute-start.13 = (bf16[2,128,512]{2,1,0:T(8,128)(2,1)S(1)}, bf16[2,128,512]{2,1,0:T(8,128)(2,1)S(1)}, u32[]{:S(2)}, u32[]{:S(2)}) collective-permute-start(bf16[2,128,512]{2,1,0:T(8,128)(2,1)S(1)} %get-tuple-element.42), channel_id=1, source_target_pairs={{0,7},{1,0},{2,1},{3,2},{4,3},{5,4},{6,5},{7,6},{8,15},{9,8},{10,9... | collective-permute-start | bytes 786440 | tf_op jit(solution)/shard_map/ppermute | solution.py:234
  43.9 6.7 %shard_map.94 = (bf16[128,1024]{1,0:T(8,128)(2,1)}, bf16[3,128,256]{2,1,0:T(8,128)(2,1)S(1)}, bf16[6,128,256]{2,1,0:T(8,128)(2,1)S(1)}, bf16[3,128,256]{2,1,0:T(8,128)(2,1)S(1)}, bf16[6,128,256]{2,1,0:T(8,128)(2,1)S(1)}) custom-call(s32[3]{0:T(128)S(1)} %pad_add_fusion.info_ref, bf16[1024,4096]{1,0:T(8,128)(2,1)S(1)} %get-tuple-element.32.held_ref, ...), custom_call_target="tpu_custom_call" | custom-call | flops 14000000000 | bytes 1048576 | tf_op jit(solution)/shard_map/pallas_call | solution.py:279
  51.4 2.5 %collective-permute-start.15 = (bf16[128,512]{1,0:T(8,128)(2,1)S(1)}, bf16[128,512]{1,0:T(8,128)(2,1)S(1)}, u32[]{:S(2)}, u32[]{:S(2)}) collective-permute-start(bf16[128,512]{1,0:T(8,128)(2,1)S(1)} %get-tuple-element.56), channel_id=1, source_target_pairs={{0,4},{1,5},{2,6},{3,7},{4,0},{5,1},{6,2},{7,3},{8,12},{9,13},{10,... | collective-permute-start | bytes 393224 | tf_op jit(solution)/shard_map/ppermute | solution.py:234
  54.2 3.2 %collective-permute-start.21 = (bf16[2,128,256]{2,1,0:T(8,128)(2,1)S(1)}, bf16[2,128,256]{2,1,0:T(8,128)(2,1)S(1)}, u32[]{:S(2)}, u32[]{:S(2)}) collective-permute-start(bf16[2,128,256]{2,1,0:T(8,128)(2,1)S(1)} %get-tuple-element.53), channel_id=1, source_target_pairs={{0,208},{8,216},{16,224},{24,232},{32,240},{40,248},{48,0},{56,8},... | collective-permute-start | bytes 393224 | tf_op jit(solution)/shard_map/ppermute | solution.py:226
  57.4 1.6 %collective-permute-start.20 = (bf16[2,128,256]{2,1,0:T(8,128)(2,1)S(1)}, bf16[2,128,256]{2,1,0:T(8,128)(2,1)S(1)}, u32[]{:S(2)}, u32[]{:S(2)}) collective-permute-start(bf16[2,128,256]{2,1,0:T(8,128)(2,1)S(1)} %get-tuple-element.54), channel_id=1, source_target_pairs={{0,224},{8,232},{16,240},{24,248},{32,0},{40,8},{48,16},{56,24},{6... | collective-permute-start | bytes 393224 | tf_op jit(solution)/shard_map/ppermute | solution.py:226
  59.4 2.9 %collective-permute-start.16 = (bf16[128,512]{1,0:T(8,128)(2,1)S(1)}, bf16[128,512]{1,0:T(8,128)(2,1)S(1)}, u32[]{:S(2)}, u32[]{:S(2)}) collective-permute-start(bf16[128,512]{1,0:T(8,128)(2,1)S(1)} %get-tuple-element.57), channel_id=1, source_target_pairs={{0,7},{1,0},{2,1},{3,2},{4,3},{5,4},{6,5},{7,6},{8,15},{9,8},{10,9... | collective-permute-start | bytes 393224 | tf_op jit(solution)/shard_map/ppermute | solution.py:234
  62.3 3.4 %collective-permute-done.21 = bf16[2,128,256]{2,1,0:T(8,128)(2,1)S(1)} collective-permute-done((bf16[2,128,256]{2,1,0:T(8,128)(2,1)S(1)}, bf16[2,128,256]{2,1,0:T(8,128)(2,1)S(1)}, u32[]{:S(2)}, u32[]{:S(2)}) %collective-permute-start.21) | collective-permute-done | bytes 131104 | tf_op jit(solution)/shard_map/ppermute | solution.py:226
  65.7 2.5 %collective-permute-start.22 = (bf16[128,256]{1,0:T(8,128)(2,1)S(1)}, bf16[128,256]{1,0:T(8,128)(2,1)S(1)}, u32[]{:S(2)}, u32[]{:S(2)}) collective-permute-start(bf16[128,256]{1,0:T(8,128)(2,1)S(1)} %fusion.8), channel_id=1, source_target_pairs={{0,128},{8,136},{16,144},{24,152},{32,160},{40,168},{48,176},{56,1... | collective-permute-start | bytes 196616 | tf_op jit(solution)/shard_map/ppermute | solution.py:226
  68.3 5.2 %collective-permute-start.23 = (bf16[128,256]{1,0:T(8,128)(2,1)S(1)}, bf16[128,256]{1,0:T(8,128)(2,1)S(1)}, u32[]{:S(2)}, u32[]{:S(2)}) collective-permute-start(bf16[128,256]{1,0:T(8,128)(2,1)S(1)} %fusion.9), channel_id=1, source_target_pairs={{0,192},{8,200},{16,208},{24,216},{32,224},{40,232},{48,240},{56,2... | collective-permute-start | bytes 196616 | tf_op jit(solution)/shard_map/ppermute | solution.py:226
  73.5 0.7 add_convert_fusion.1
  74.2 1.2 %collective-permute-done.23 = bf16[128,256]{1,0:T(8,128)(2,1)S(1)} collective-permute-done((bf16[128,256]{1,0:T(8,128)(2,1)S(1)}, bf16[128,256]{1,0:T(8,128)(2,1)S(1)}, u32[]{:S(2)}, u32[]{:S(2)}) %collective-permute-start.23) | collective-permute-done | bytes 65568 | tf_op jit(solution)/shard_map/ppermute | solution.py:226
  (53 shorter events, 4.1 us)
Async XLA Ops:
  2.1 5.6 %collective-permute-start = (bf16[1,144,256]{2,1,0:T(8,128)(2,1)S(1)}, bf16[1,144,256]{2,1,0:T(8,128)(2,1)S(1)}, u32[]{:S(2)}, u32[]{:S(2)}) collective-permute-start(bf16[1,144,256]{2,1,0:T(8,128)(2,1)S(1)} %maximum_bitcast_fusion), channel_id=1, source_target_pairs={{0,64},{8,72},{16,80},{24,88},{32,96},{40,104},{48,112},{56,120},{... | collective-permute-start | bytes 221192 | tf_op jit(solution)/shard_map/ppermute | solution.py:226
  7.8 12.3 %collective-permute-start.2 = (bf16[2,144,256]{2,1,0:T(8,128)(2,1)S(1)}, bf16[2,144,256]{2,1,0:T(8,128)(2,1)S(1)}, u32[]{:S(2)}, u32[]{:S(2)}) collective-permute-start(bf16[2,144,256]{2,1,0:T(8,128)(2,1)S(1)} %pad_maximum_fusion.2), channel_id=1, source_target_pairs={{0,16},{8,24},{16,32},{24,40},{32,48},{40,56},{48,64},{56,72},{64,... | collective-permute-start | bytes 442376 | tf_op jit(solution)/shard_map/ppermute | solution.py:226
  9.5 12.5 %collective-permute-start.3 = (bf16[2,144,256]{2,1,0:T(8,128)(2,1)S(1)}, bf16[2,144,256]{2,1,0:T(8,128)(2,1)S(1)}, u32[]{:S(2)}, u32[]{:S(2)}) collective-permute-start(bf16[2,144,256]{2,1,0:T(8,128)(2,1)S(1)} %pad_maximum_fusion.2), channel_id=1, source_target_pairs={{0,32},{8,40},{16,48},{24,56},{32,64},{40,72},{48,80},{56,88},{64,... | collective-permute-start | bytes 442376 | tf_op jit(solution)/shard_map/ppermute | solution.py:226
  10.4 17.2 %collective-permute-start.1 = (bf16[1,144,256]{2,1,0:T(8,128)(2,1)S(1)}, bf16[1,144,256]{2,1,0:T(8,128)(2,1)S(1)}, u32[]{:S(2)}, u32[]{:S(2)}) collective-permute-start(bf16[1,144,256]{2,1,0:T(8,128)(2,1)S(1)} %maximum_bitcast_fusion), channel_id=1, source_target_pairs={{0,128},{8,136},{16,144},{24,152},{32,160},{40,168},{48,176},{56,1... | collective-permute-start | bytes 221192 | tf_op jit(solution)/shard_map/ppermute | solution.py:226
  12.9 15.4 %collective-permute-start.8 = (bf16[128,512]{1,0:T(8,128)(2,1)}, bf16[128,512]{1,0:T(8,128)(2,1)S(1)}, u32[]{:S(2)}, u32[]{:S(2)}) collective-permute-start(bf16[128,512]{1,0:T(8,128)(2,1)} %refs_5_.1), channel_id=1, source_target_pairs={{0,4},{1,5},{2,6},{3,7},{4,0},{5,1},{6,2},{7,3},{8,12},{9,13},{10,... | collective-permute-start | bytes 393224 | tf_op jit(solution)/shard_map/ppermute | solution.py:234
  20.0 8.2 %collective-permute-start.7 = (bf16[128,512]{1,0:T(8,128)(2,1)}, bf16[128,512]{1,0:T(8,128)(2,1)S(1)}, u32[]{:S(2)}, u32[]{:S(2)}) collective-permute-start(bf16[128,512]{1,0:T(8,128)(2,1)} %refs_5_.1), channel_id=1, source_target_pairs={{0,7},{1,0},{2,1},{3,2},{4,3},{5,4},{6,5},{7,6},{8,15},{9,8},{10,9... | collective-permute-start | bytes 393224 | tf_op jit(solution)/shard_map/ppermute | solution.py:234
  20.2 7.3 %collective-permute-start.4 = (bf16[2,144,256]{2,1,0:T(8,128)(2,1)S(1)}, bf16[2,144,256]{2,1,0:T(8,128)(2,1)S(1)}, u32[]{:S(2)}, u32[]{:S(2)}) collective-permute-start(bf16[2,144,256]{2,1,0:T(8,128)(2,1)S(1)} %pad_maximum_fusion.2), channel_id=1, source_target_pairs={{0,48},{8,56},{16,64},{24,72},{32,80},{40,88},{48,96},{56,104},{64... | collective-permute-start | bytes 442376 | tf_op jit(solution)/shard_map/ppermute | solution.py:226
  22.0 9.4 %collective-permute-start.10 = (bf16[128,512]{1,0:T(8,128)(2,1)}, bf16[128,512]{1,0:T(8,128)(2,1)S(1)}, u32[]{:S(2)}, u32[]{:S(2)}) collective-permute-start(bf16[128,512]{1,0:T(8,128)(2,1)} %refs_5_.1), channel_id=1, source_target_pairs={{0,1},{1,2},{2,3},{3,4},{4,5},{5,6},{6,7},{7,0},{8,9},{9,10},{10,1... | collective-permute-start | bytes 393224 | tf_op jit(solution)/shard_map/ppermute | solution.py:234
  27.4 7.3 %collective-permute-start.6 = (bf16[6,144,256]{2,1,0:T(8,128)(2,1)S(1)}, bf16[6,144,256]{2,1,0:T(8,128)(2,1)S(1)}, u32[]{:S(2)}, u32[]{:S(2)}) collective-permute-start(bf16[6,144,256]{2,1,0:T(8,128)(2,1)S(1)} %constant_dynamic-update-slice_fusion.2.refs_1_), channel_id=1, source_target_pairs={{0,8},{8,0},{16,24},{24,16},{32,40},{40,32},{48,56},{56,48},{64,72... | collective-permute-start | bytes 1327112 | tf_op jit(solution)/shard_map/ppermute | solution.py:230
  27.6 7.1 %collective-permute-start.5 = (bf16[3,144,256]{2,1,0:T(8,128)(2,1)S(1)}, bf16[3,144,256]{2,1,0:T(8,128)(2,1)S(1)}, u32[]{:S(2)}, u32[]{:S(2)}) collective-permute-start(bf16[3,144,256]{2,1,0:T(8,128)(2,1)S(1)} %constant_dynamic-update-slice_fusion.refs_0_), channel_id=1, source_target_pairs={{0,8},{8,0},{16,24},{24,16},{32,40},{40,32},{48,56},{56,48},{64,72... | collective-permute-start | bytes 663560 | tf_op jit(solution)/shard_map/ppermute | solution.py:230
  31.4 12.5 %collective-permute-start.11 = (bf16[256,512]{1,0:T(8,128)(2,1)S(1)}, bf16[256,512]{1,0:T(8,128)(2,1)S(1)}, u32[]{:S(2)}, u32[]{:S(2)}) collective-permute-start(bf16[256,512]{1,0:T(8,128)(2,1)S(1)} %get-tuple-element.58), channel_id=1, source_target_pairs={{0,1},{1,2},{2,3},{3,4},{4,5},{5,6},{6,7},{7,0},{8,9},{9,10},{10,1... | collective-permute-start | bytes 786440 | tf_op jit(solution)/shard_map/ppermute | solution.py:234
  31.5 12.4 %collective-permute-start.9 = (bf16[256,512]{1,0:T(8,128)(2,1)S(1)}, bf16[256,512]{1,0:T(8,128)(2,1)S(1)}, u32[]{:S(2)}, u32[]{:S(2)}) collective-permute-start(bf16[256,512]{1,0:T(8,128)(2,1)S(1)} %get-tuple-element.59), channel_id=1, source_target_pairs={{0,7},{1,0},{2,1},{3,2},{4,3},{5,4},{6,5},{7,6},{8,15},{9,8},{10,9... | collective-permute-start | bytes 786440 | tf_op jit(solution)/shard_map/ppermute | solution.py:234
  40.4 10.2 %collective-permute-start.12 = (bf16[2,128,512]{2,1,0:T(8,128)(2,1)S(1)}, bf16[2,128,512]{2,1,0:T(8,128)(2,1)S(1)}, u32[]{:S(2)}, u32[]{:S(2)}) collective-permute-start(bf16[2,128,512]{2,1,0:T(8,128)(2,1)S(1)} %get-tuple-element.41), channel_id=1, source_target_pairs={{0,1},{1,2},{2,3},{3,4},{4,5},{5,6},{6,7},{7,0},{8,9},{9,10},{10,1... | collective-permute-start | bytes 786440 | tf_op jit(solution)/shard_map/ppermute | solution.py:234
  40.7 9.9 %collective-permute-start.13 = (bf16[2,128,512]{2,1,0:T(8,128)(2,1)S(1)}, bf16[2,128,512]{2,1,0:T(8,128)(2,1)S(1)}, u32[]{:S(2)}, u32[]{:S(2)}) collective-permute-start(bf16[2,128,512]{2,1,0:T(8,128)(2,1)S(1)} %get-tuple-element.42), channel_id=1, source_target_pairs={{0,7},{1,0},{2,1},{3,2},{4,3},{5,4},{6,5},{7,6},{8,15},{9,8},{10,9... | collective-permute-start | bytes 786440 | tf_op jit(solution)/shard_map/ppermute | solution.py:234
  50.6 3.3 %collective-permute-start.17 = (bf16[3,128,256]{2,1,0:T(8,128)(2,1)S(1)}, bf16[3,128,256]{2,1,0:T(8,128)(2,1)S(1)}, u32[]{:S(2)}, u32[]{:S(2)}) collective-permute-start(bf16[3,128,256]{2,1,0:T(8,128)(2,1)S(1)} %get-tuple-element.49), channel_id=1, source_target_pairs={{0,8},{8,0},{16,24},{24,16},{32,40},{40,32},{48,56},{56,48},{64,72... | collective-permute-start | bytes 589832 | tf_op jit(solution)/shard_map/ppermute | solution.py:230
  50.6 3.3 %collective-permute-start.18 = (bf16[6,128,256]{2,1,0:T(8,128)(2,1)S(1)}, bf16[6,128,256]{2,1,0:T(8,128)(2,1)S(1)}, u32[]{:S(2)}, u32[]{:S(2)}) collective-permute-start(bf16[6,128,256]{2,1,0:T(8,128)(2,1)S(1)} %get-tuple-element.51), channel_id=1, source_target_pairs={{0,8},{8,0},{16,24},{24,16},{32,40},{40,32},{48,56},{56,48},{64,72... | collective-permute-start | bytes 1179656 | tf_op jit(solution)/shard_map/ppermute | solution.py:230
  51.3 22.2 %collective-permute-start.14 = (bf16[128,512]{1,0:T(8,128)(2,1)S(1)}, bf16[128,512]{1,0:T(8,128)(2,1)S(1)}, u32[]{:S(2)}, u32[]{:S(2)}) collective-permute-start(bf16[128,512]{1,0:T(8,128)(2,1)S(1)} %get-tuple-element.55), channel_id=1, source_target_pairs={{0,1},{1,2},{2,3},{3,4},{4,5},{5,6},{6,7},{7,0},{8,9},{9,10},{10,1... | collective-permute-start | bytes 393224 | tf_op jit(solution)/shard_map/ppermute | solution.py:234
  51.4 22.1 %collective-permute-start.15 = (bf16[128,512]{1,0:T(8,128)(2,1)S(1)}, bf16[128,512]{1,0:T(8,128)(2,1)S(1)}, u32[]{:S(2)}, u32[]{:S(2)}) collective-permute-start(bf16[128,512]{1,0:T(8,128)(2,1)S(1)} %get-tuple-element.56), channel_id=1, source_target_pairs={{0,4},{1,5},{2,6},{3,7},{4,0},{5,1},{6,2},{7,3},{8,12},{9,13},{10,... | collective-permute-start | bytes 393224 | tf_op jit(solution)/shard_map/ppermute | solution.py:234
  54.1 5.3 %collective-permute-start.19 = (bf16[2,128,256]{2,1,0:T(8,128)(2,1)S(1)}, bf16[2,128,256]{2,1,0:T(8,128)(2,1)S(1)}, u32[]{:S(2)}, u32[]{:S(2)}) collective-permute-start(bf16[2,128,256]{2,1,0:T(8,128)(2,1)S(1)} %get-tuple-element.52), channel_id=1, source_target_pairs={{0,240},{8,248},{16,0},{24,8},{32,16},{40,24},{48,32},{56,40},{64,... | collective-permute-start | bytes 393224 | tf_op jit(solution)/shard_map/ppermute | solution.py:226
  54.2 11.5 %collective-permute-start.21 = (bf16[2,128,256]{2,1,0:T(8,128)(2,1)S(1)}, bf16[2,128,256]{2,1,0:T(8,128)(2,1)S(1)}, u32[]{:S(2)}, u32[]{:S(2)}) collective-permute-start(bf16[2,128,256]{2,1,0:T(8,128)(2,1)S(1)} %get-tuple-element.53), channel_id=1, source_target_pairs={{0,208},{8,216},{16,224},{24,232},{32,240},{40,248},{48,0},{56,8},... | collective-permute-start | bytes 393224 | tf_op jit(solution)/shard_map/ppermute | solution.py:226
  57.4 10.8 %collective-permute-start.20 = (bf16[2,128,256]{2,1,0:T(8,128)(2,1)S(1)}, bf16[2,128,256]{2,1,0:T(8,128)(2,1)S(1)}, u32[]{:S(2)}, u32[]{:S(2)}) collective-permute-start(bf16[2,128,256]{2,1,0:T(8,128)(2,1)S(1)} %get-tuple-element.54), channel_id=1, source_target_pairs={{0,224},{8,232},{16,240},{24,248},{32,0},{40,8},{48,16},{56,24},{6... | collective-permute-start | bytes 393224 | tf_op jit(solution)/shard_map/ppermute | solution.py:226
  59.4 14.1 %collective-permute-start.16 = (bf16[128,512]{1,0:T(8,128)(2,1)S(1)}, bf16[128,512]{1,0:T(8,128)(2,1)S(1)}, u32[]{:S(2)}, u32[]{:S(2)}) collective-permute-start(bf16[128,512]{1,0:T(8,128)(2,1)S(1)} %get-tuple-element.57), channel_id=1, source_target_pairs={{0,7},{1,0},{2,1},{3,2},{4,3},{5,4},{6,5},{7,6},{8,15},{9,8},{10,9... | collective-permute-start | bytes 393224 | tf_op jit(solution)/shard_map/ppermute | solution.py:234
  65.7 8.5 %collective-permute-start.22 = (bf16[128,256]{1,0:T(8,128)(2,1)S(1)}, bf16[128,256]{1,0:T(8,128)(2,1)S(1)}, u32[]{:S(2)}, u32[]{:S(2)}) collective-permute-start(bf16[128,256]{1,0:T(8,128)(2,1)S(1)} %fusion.8), channel_id=1, source_target_pairs={{0,128},{8,136},{16,144},{24,152},{32,160},{40,168},{48,176},{56,1... | collective-permute-start | bytes 196616 | tf_op jit(solution)/shard_map/ppermute | solution.py:226
  68.3 7.1 %collective-permute-start.23 = (bf16[128,256]{1,0:T(8,128)(2,1)S(1)}, bf16[128,256]{1,0:T(8,128)(2,1)S(1)}, u32[]{:S(2)}, u32[]{:S(2)}) collective-permute-start(bf16[128,256]{1,0:T(8,128)(2,1)S(1)} %fusion.9), channel_id=1, source_target_pairs={{0,192},{8,200},{16,208},{24,216},{32,224},{40,232},{48,240},{56,2... | collective-permute-start | bytes 196616 | tf_op jit(solution)/shard_map/ppermute | solution.py:226
  (2 other events, 15.6 us)

commit v6 on v5

--- a/solution.py
+++ b/solution.py
@@ -16,7 +16,8 @@
 SLOTS = 9
 KEYS = SLOTS * PAIR
 STEP = 2 * PAIR
-CHUNK = 256
+CHUNK = 512
+GRAD_CHUNK = 1024
 QROWS = HEADS * TOK
 FEATURES = 512
 MASKED = -1e30
@@ -179,10 +180,10 @@
         for j in range(ref.shape[0] // TOK):
             cot_ref[:, n * FEATURES : (n + 1) * FEATURES] = ref[j * TOK : (j + 1) * TOK, :]
             n = n + 1
-    grad_ref[...] = dot_nt(held_ref[...], cot_ref[...])
+    grad_ref[...] = dot_nt(cot_ref[...], held_ref[...])
     for h in range(HEADS):
         part = slice(h * TOK, (h + 1) * TOK)
-        grad_t = grad_ref[part, :] * inverse_ref[:, part]
+        grad_t = grad_ref[:, part].T * inverse_ref[:, part]
         delta_ref[:, part] = jnp.sum(grad_t * att_t_ref[:, part].astype(jnp.float32), axis=0, keepdims=True)
         grad_t = grad_t.astype(jnp.bfloat16)
         grad_t_ref[:, part] = grad_t
@@ -196,8 +197,8 @@
         value = value_ref[rows, :]
         dkey = jnp.zeros((count, HEAD_SIZE), jnp.float32)
         dvalue = jnp.zeros((count, HEAD_SIZE), jnp.float32)
-        for n in range(QROWS // CHUNK):
-            cols = slice(n * CHUNK, (n + 1) * CHUNK)
+        for n in range(QROWS // GRAD_CHUNK):
+            cols = slice(n * GRAD_CHUNK, (n + 1) * GRAD_CHUNK)
             weight = weight_ref[rows, cols]
             gprob = dot(value, grad_t_ref[:, cols])
             gscore = (weight.astype(jnp.float32) * (gprob - delta_ref[:, cols])).astype(jnp.bfloat16)
@@ -283,7 +284,7 @@
         out_shape=[shaped(TOK, QROWS)] + blocks + blocks,
         scratch_shapes=[
             pltpu.VMEM((TOK, 8 * FEATURES), jnp.bfloat16),
-            pltpu.VMEM((QROWS, TOK), jnp.float32),
+            pltpu.VMEM((TOK, QROWS), jnp.float32),
             pltpu.VMEM((HEAD_SIZE, QROWS), jnp.bfloat16),
             pltpu.VMEM((QROWS, HEAD_SIZE), jnp.bfloat16),
             pltpu.VMEM((HEAD_SIZE, QROWS), jnp.float32),

time: 77.3 us -> 75.4 us (0.975); the launches traced: 76 us -> 75.5 us
  starting transfers between devices: 43.9 us -> 42.8 us
  waiting for transfers between devices: 15.4 us -> 16.4 us
    ppermute x10, starting transfers between devices: 21.1 us -> 20 us  [chips_on(): lax.ppermute(value, 'dp', [(i, (i + 2 * by) % 32) for i in range(32)])]
    ppermute x10, waiting for transfers between devices: 12.3 us -> 13.2 us  [chips_on(): lax.ppermute(value, 'dp', [(i, (i + 2 * by) % 32) for i in range(32)])]
  transfers between devices with their start and end apart: 24 -> 24, of which waited for: 6 -> 7; matrix products, arithmetic and copies ran while one was open for 2% -> 2% of each run, Pallas kernels for 16% -> 16%
where the time goes in v6:
time: 75.4 us; the launch traced here: 75.5 us
  starting transfers between devices  42.8 us (57%)
  waiting for transfers between devices  16.4 us (22%)
  Pallas kernels  11.9 us (16%)
  other arithmetic  2.69 us (4%)
  between operations  0.85 us (1%)
  local copies, waits for them, and re-layouts  0.8 us (1%)
    ppermute x10, starting transfers between devices, along_z(): return lax.ppermute(value, 'tensor', [(i, (i + by) % 8) for i in range(8)])  21.6 us
    ppermute x10, starting transfers between devices, chips_on(): lax.ppermute(value, 'dp', [(i, (i + 2 * by) % 32) for i in range(32)])  20 us
    ppermute x10, waiting for transfers between devices, chips_on(): lax.ppermute(value, 'dp', [(i, (i + 2 * by) % 32) for i in range(32)])  13.2 us
    pallas_call x1, Pallas kernels, backward(): pl.pallas_call(backward_kernel, in_specs=[SMEM] + [VMEM] * 14, out_specs=...  6.22 us
    pallas_call x1, Pallas kernels, forward(): pl.pallas_call(forward_kernel, in_specs=[SMEM, HBM] + [VMEM] * 5, out_spe...  5.72 us
    ppermute x10, waiting for transfers between devices, along_z(): return lax.ppermute(value, 'tensor', [(i, (i + by) % 8) for i in range(8)])  3.14 us
  transfers between devices with their start and end apart: 24, of which 7 were waited for; matrix products, arithmetic and copies ran while one was open for 2% of the time, Pallas kernels for 16%

profile of v6, /device:TPU:8, one launch (start us, length us, event | category | flops | bytes accessed | tf_op | source)
XLA Modules:
  0.0 75.5 jit_solution(6512856292705702424)
XLA Ops:
  1.4 0.8 %maximum_bitcast_fusion = bf16[1,144,256]{2,1,0:T(8,128)(2,1)S(1)} fusion(bf16[16,256]{1,0:T(8,128)(2,1)S(1)} %broadcast_in_dim.4, bf16[128,128]{1,0:T(8,128)(2,1)} %param.8, bf16[128,128]{1,0:T(8,128)(2,1)} %param.7), kind=kLoop, calls=%fused_computation.23 | loop fusion | flops 221184 | bytes 147456 | tf_op jit(solution)/shard_map/broadcast_in_dim | solution.py:61
  2.1 1.6 %collective-permute-start = (bf16[1,144,256]{2,1,0:T(8,128)(2,1)S(1)}, bf16[1,144,256]{2,1,0:T(8,128)(2,1)S(1)}, u32[]{:S(2)}, u32[]{:S(2)}) collective-permute-start(bf16[1,144,256]{2,1,0:T(8,128)(2,1)S(1)} %maximum_bitcast_fusion), channel_id=1, source_target_pairs={{0,64},{8,72},{16,80},{24,88},{32,96},{40,104},{48,112},{56,120},{... | collective-permute-start | bytes 221192 | tf_op jit(solution)/shard_map/ppermute | solution.py:227
  3.8 4.0 %collective-permute-done = bf16[1,144,256]{2,1,0:T(8,128)(2,1)S(1)} collective-permute-done((bf16[1,144,256]{2,1,0:T(8,128)(2,1)S(1)}, bf16[1,144,256]{2,1,0:T(8,128)(2,1)S(1)}, u32[]{:S(2)}, u32[]{:S(2)}) %collective-permute-start) | collective-permute-done | bytes 73760 | tf_op jit(solution)/shard_map/ppermute | solution.py:227
  7.8 1.7 %collective-permute-start.2 = (bf16[2,144,256]{2,1,0:T(8,128)(2,1)S(1)}, bf16[2,144,256]{2,1,0:T(8,128)(2,1)S(1)}, u32[]{:S(2)}, u32[]{:S(2)}) collective-permute-start(bf16[2,144,256]{2,1,0:T(8,128)(2,1)S(1)} %pad_maximum_fusion.2), channel_id=1, source_target_pairs={{0,16},{8,24},{16,32},{24,40},{32,48},{40,56},{48,64},{56,72},{64,... | collective-permute-start | bytes 442376 | tf_op jit(solution)/shard_map/ppermute | solution.py:227
  9.5 0.9 %collective-permute-start.3 = (bf16[2,144,256]{2,1,0:T(8,128)(2,1)S(1)}, bf16[2,144,256]{2,1,0:T(8,128)(2,1)S(1)}, u32[]{:S(2)}, u32[]{:S(2)}) collective-permute-start(bf16[2,144,256]{2,1,0:T(8,128)(2,1)S(1)} %pad_maximum_fusion.2), channel_id=1, source_target_pairs={{0,32},{8,40},{16,48},{24,56},{32,64},{40,72},{48,80},{56,88},{64,... | collective-permute-start | bytes 442376 | tf_op jit(solution)/shard_map/ppermute | solution.py:227
  10.4 2.5 %collective-permute-start.1 = (bf16[1,144,256]{2,1,0:T(8,128)(2,1)S(1)}, bf16[1,144,256]{2,1,0:T(8,128)(2,1)S(1)}, u32[]{:S(2)}, u32[]{:S(2)}) collective-permute-start(bf16[1,144,256]{2,1,0:T(8,128)(2,1)S(1)} %maximum_bitcast_fusion), channel_id=1, source_target_pairs={{0,128},{8,136},{16,144},{24,152},{32,160},{40,168},{48,176},{56,1... | collective-permute-start | bytes 221192 | tf_op jit(solution)/shard_map/ppermute | solution.py:227
  12.9 7.2 %collective-permute-start.8 = (bf16[128,512]{1,0:T(8,128)(2,1)}, bf16[128,512]{1,0:T(8,128)(2,1)S(1)}, u32[]{:S(2)}, u32[]{:S(2)}) collective-permute-start(bf16[128,512]{1,0:T(8,128)(2,1)} %refs_5_.1), channel_id=1, source_target_pairs={{0,4},{1,5},{2,6},{3,7},{4,0},{5,1},{6,2},{7,3},{8,12},{9,13},{10,... | collective-permute-start | bytes 393224 | tf_op jit(solution)/shard_map/ppermute | solution.py:235
  20.2 1.8 %collective-permute-start.4 = (bf16[2,144,256]{2,1,0:T(8,128)(2,1)S(1)}, bf16[2,144,256]{2,1,0:T(8,128)(2,1)S(1)}, u32[]{:S(2)}, u32[]{:S(2)}) collective-permute-start(bf16[2,144,256]{2,1,0:T(8,128)(2,1)S(1)} %pad_maximum_fusion.2), channel_id=1, source_target_pairs={{0,48},{8,56},{16,64},{24,72},{32,80},{40,88},{48,96},{56,104},{64... | collective-permute-start | bytes 442376 | tf_op jit(solution)/shard_map/ppermute | solution.py:227
  22.0 2.0 %collective-permute-start.10 = (bf16[128,512]{1,0:T(8,128)(2,1)}, bf16[128,512]{1,0:T(8,128)(2,1)S(1)}, u32[]{:S(2)}, u32[]{:S(2)}) collective-permute-start(bf16[128,512]{1,0:T(8,128)(2,1)} %refs_5_.1), channel_id=1, source_target_pairs={{0,1},{1,2},{2,3},{3,4},{4,5},{5,6},{6,7},{7,0},{8,9},{9,10},{10,1... | collective-permute-start | bytes 393224 | tf_op jit(solution)/shard_map/ppermute | solution.py:235
  24.0 3.4 %collective-permute-done.4 = bf16[2,144,256]{2,1,0:T(8,128)(2,1)S(1)} collective-permute-done((bf16[2,144,256]{2,1,0:T(8,128)(2,1)S(1)}, bf16[2,144,256]{2,1,0:T(8,128)(2,1)S(1)}, u32[]{:S(2)}, u32[]{:S(2)}) %collective-permute-start.4) | collective-permute-done | bytes 147488 | tf_op jit(solution)/shard_map/ppermute | solution.py:227
  28.2 3.1 %collective-permute-done.10.refs_4_ = bf16[128,512]{1,0:T(8,128)(2,1)S(1)} collective-permute-done((bf16[128,512]{1,0:T(8,128)(2,1)}, bf16[128,512]{1,0:T(8,128)(2,1)S(1)}, u32[]{:S(2)}, u32[]{:S(2)}) %collective-permute-start.10) | collective-permute-done | bytes 131104 | tf_op jit(solution)/shard_map/ppermute | solution.py:235
  31.5 3.2 %collective-permute-start.9 = (bf16[256,512]{1,0:T(8,128)(2,1)S(1)}, bf16[256,512]{1,0:T(8,128)(2,1)S(1)}, u32[]{:S(2)}, u32[]{:S(2)}) collective-permute-start(bf16[256,512]{1,0:T(8,128)(2,1)S(1)} %get-tuple-element.59), channel_id=1, source_target_pairs={{0,7},{1,0},{2,1},{3,2},{4,3},{5,4},{6,5},{7,6},{8,15},{9,8},{10,9... | collective-permute-start | bytes 786440 | tf_op jit(solution)/shard_map/ppermute | solution.py:235
  34.7 5.7 %shard_map.93 = (bf16[128,1024]{1,0:T(8,128)(2,1)S(1)}, f32[1,1024]{1,0:T(1,128)S(1)}, s32[1,128]{1,0:T(1,128)S(1)}, bf16[2304,128]{1,0:T(8,128)(2,1)S(1)}, bf16...) custom-call(s32[3]{0:T(128)S(1)} %pad_add_fusion.info_ref, ...), custom_call_target="tpu_custom_call" | custom-call | flops 8999999488 | bytes 1048576 | tf_op jit(solution)/shard_map/pallas_call | solution.py:247
  40.7 3.2 %collective-permute-start.13 = (bf16[2,128,512]{2,1,0:T(8,128)(2,1)S(1)}, bf16[2,128,512]{2,1,0:T(8,128)(2,1)S(1)}, u32[]{:S(2)}, u32[]{:S(2)}) collective-permute-start(bf16[2,128,512]{2,1,0:T(8,128)(2,1)S(1)} %get-tuple-element.42), channel_id=1, source_target_pairs={{0,7},{1,0},{2,1},{3,2},{4,3},{5,4},{6,5},{7,6},{8,15},{9,8},{10,9... | collective-permute-start | bytes 786440 | tf_op jit(solution)/shard_map/ppermute | solution.py:235
  43.9 6.2 %shard_map.94 = (bf16[128,1024]{1,0:T(8,128)(2,1)}, bf16[3,128,256]{2,1,0:T(8,128)(2,1)S(1)}, bf16[6,128,256]{2,1,0:T(8,128)(2,1)S(1)}, bf16[3,128,256]{2,1,0:T(8,128)(2,1)S(1)}, bf16[6,128,256]{2,1,0:T(8,128)(2,1)S(1)}) custom-call(s32[3]{0:T(128)S(1)} %pad_add_fusion.info_ref, bf16[1024,4096]{1,0:T(8,128)(2,1)S(1)} %get-tuple-element.32.held_ref, ...), custom_call_target="tpu_custom_call" | custom-call | flops 14000000000 | bytes 1048576 | tf_op jit(solution)/shard_map/pallas_call | solution.py:280
  50.9 2.5 %collective-permute-start.15 = (bf16[128,512]{1,0:T(8,128)(2,1)S(1)}, bf16[128,512]{1,0:T(8,128)(2,1)S(1)}, u32[]{:S(2)}, u32[]{:S(2)}) collective-permute-start(bf16[128,512]{1,0:T(8,128)(2,1)S(1)} %get-tuple-element.56), channel_id=1, source_target_pairs={{0,4},{1,5},{2,6},{3,7},{4,0},{5,1},{6,2},{7,3},{8,12},{9,13},{10,... | collective-permute-start | bytes 393224 | tf_op jit(solution)/shard_map/ppermute | solution.py:235
  53.8 3.1 %collective-permute-start.21 = (bf16[2,128,256]{2,1,0:T(8,128)(2,1)S(1)}, bf16[2,128,256]{2,1,0:T(8,128)(2,1)S(1)}, u32[]{:S(2)}, u32[]{:S(2)}) collective-permute-start(bf16[2,128,256]{2,1,0:T(8,128)(2,1)S(1)} %get-tuple-element.53), channel_id=1, source_target_pairs={{0,208},{8,216},{16,224},{24,232},{32,240},{40,248},{48,0},{56,8},... | collective-permute-start | bytes 393224 | tf_op jit(solution)/shard_map/ppermute | solution.py:227
  57.0 1.7 %collective-permute-start.20 = (bf16[2,128,256]{2,1,0:T(8,128)(2,1)S(1)}, bf16[2,128,256]{2,1,0:T(8,128)(2,1)S(1)}, u32[]{:S(2)}, u32[]{:S(2)}) collective-permute-start(bf16[2,128,256]{2,1,0:T(8,128)(2,1)S(1)} %get-tuple-element.54), channel_id=1, source_target_pairs={{0,224},{8,232},{16,240},{24,248},{32,0},{40,8},{48,16},{56,24},{6... | collective-permute-start | bytes 393224 | tf_op jit(solution)/shard_map/ppermute | solution.py:227
  58.9 2.9 %collective-permute-start.16 = (bf16[128,512]{1,0:T(8,128)(2,1)S(1)}, bf16[128,512]{1,0:T(8,128)(2,1)S(1)}, u32[]{:S(2)}, u32[]{:S(2)}) collective-permute-start(bf16[128,512]{1,0:T(8,128)(2,1)S(1)} %get-tuple-element.57), channel_id=1, source_target_pairs={{0,7},{1,0},{2,1},{3,2},{4,3},{5,4},{6,5},{7,6},{8,15},{9,8},{10,9... | collective-permute-start | bytes 393224 | tf_op jit(solution)/shard_map/ppermute | solution.py:235
  61.9 2.0 %collective-permute-done.21 = bf16[2,128,256]{2,1,0:T(8,128)(2,1)S(1)} collective-permute-done((bf16[2,128,256]{2,1,0:T(8,128)(2,1)S(1)}, bf16[2,128,256]{2,1,0:T(8,128)(2,1)S(1)}, u32[]{:S(2)}, u32[]{:S(2)}) %collective-permute-start.21) | collective-permute-done | bytes 131104 | tf_op jit(solution)/shard_map/ppermute | solution.py:227
  63.9 6.5 %collective-permute-start.22 = (bf16[128,256]{1,0:T(8,128)(2,1)S(1)}, bf16[128,256]{1,0:T(8,128)(2,1)S(1)}, u32[]{:S(2)}, u32[]{:S(2)}) collective-permute-start(bf16[128,256]{1,0:T(8,128)(2,1)S(1)} %fusion.8), channel_id=1, source_target_pairs={{0,128},{8,136},{16,144},{24,152},{32,160},{40,168},{48,176},{56,1... | collective-permute-start | bytes 196616 | tf_op jit(solution)/shard_map/ppermute | solution.py:227
  70.6 0.7 add_convert_fusion.1
  71.3 1.3 %collective-permute-done.22 = bf16[128,256]{1,0:T(8,128)(2,1)S(1)} collective-permute-done((bf16[128,256]{1,0:T(8,128)(2,1)S(1)}, bf16[128,256]{1,0:T(8,128)(2,1)S(1)}, u32[]{:S(2)}, u32[]{:S(2)}) %collective-permute-start.22) | collective-permute-done | bytes 65568 | tf_op jit(solution)/shard_map/ppermute | solution.py:227
  72.6 2.2 %collective-permute-done.23 = bf16[128,256]{1,0:T(8,128)(2,1)S(1)} collective-permute-done((bf16[128,256]{1,0:T(8,128)(2,1)S(1)}, bf16[128,256]{1,0:T(8,128)(2,1)S(1)}, u32[]{:S(2)}, u32[]{:S(2)}) %collective-permute-start.23) | collective-permute-done | bytes 65568 | tf_op jit(solution)/shard_map/ppermute | solution.py:227
  (53 shorter events, 4.3 us)
Async XLA Ops:
  2.1 5.6 %collective-permute-start = (bf16[1,144,256]{2,1,0:T(8,128)(2,1)S(1)}, bf16[1,144,256]{2,1,0:T(8,128)(2,1)S(1)}, u32[]{:S(2)}, u32[]{:S(2)}) collective-permute-start(bf16[1,144,256]{2,1,0:T(8,128)(2,1)S(1)} %maximum_bitcast_fusion), channel_id=1, source_target_pairs={{0,64},{8,72},{16,80},{24,88},{32,96},{40,104},{48,112},{56,120},{... | collective-permute-start | bytes 221192 | tf_op jit(solution)/shard_map/ppermute | solution.py:227
  7.8 12.3 %collective-permute-start.2 = (bf16[2,144,256]{2,1,0:T(8,128)(2,1)S(1)}, bf16[2,144,256]{2,1,0:T(8,128)(2,1)S(1)}, u32[]{:S(2)}, u32[]{:S(2)}) collective-permute-start(bf16[2,144,256]{2,1,0:T(8,128)(2,1)S(1)} %pad_maximum_fusion.2), channel_id=1, source_target_pairs={{0,16},{8,24},{16,32},{24,40},{32,48},{40,56},{48,64},{56,72},{64,... | collective-permute-start | bytes 442376 | tf_op jit(solution)/shard_map/ppermute | solution.py:227
  9.5 12.5 %collective-permute-start.3 = (bf16[2,144,256]{2,1,0:T(8,128)(2,1)S(1)}, bf16[2,144,256]{2,1,0:T(8,128)(2,1)S(1)}, u32[]{:S(2)}, u32[]{:S(2)}) collective-permute-start(bf16[2,144,256]{2,1,0:T(8,128)(2,1)S(1)} %pad_maximum_fusion.2), channel_id=1, source_target_pairs={{0,32},{8,40},{16,48},{24,56},{32,64},{40,72},{48,80},{56,88},{64,... | collective-permute-start | bytes 442376 | tf_op jit(solution)/shard_map/ppermute | solution.py:227
  10.4 17.2 %collective-permute-start.1 = (bf16[1,144,256]{2,1,0:T(8,128)(2,1)S(1)}, bf16[1,144,256]{2,1,0:T(8,128)(2,1)S(1)}, u32[]{:S(2)}, u32[]{:S(2)}) collective-permute-start(bf16[1,144,256]{2,1,0:T(8,128)(2,1)S(1)} %maximum_bitcast_fusion), channel_id=1, source_target_pairs={{0,128},{8,136},{16,144},{24,152},{32,160},{40,168},{48,176},{56,1... | collective-permute-start | bytes 221192 | tf_op jit(solution)/shard_map/ppermute | solution.py:227
  12.9 15.4 %collective-permute-start.8 = (bf16[128,512]{1,0:T(8,128)(2,1)}, bf16[128,512]{1,0:T(8,128)(2,1)S(1)}, u32[]{:S(2)}, u32[]{:S(2)}) collective-permute-start(bf16[128,512]{1,0:T(8,128)(2,1)} %refs_5_.1), channel_id=1, source_target_pairs={{0,4},{1,5},{2,6},{3,7},{4,0},{5,1},{6,2},{7,3},{8,12},{9,13},{10,... | collective-permute-start | bytes 393224 | tf_op jit(solution)/shard_map/ppermute | solution.py:235
  20.0 8.2 %collective-permute-start.7 = (bf16[128,512]{1,0:T(8,128)(2,1)}, bf16[128,512]{1,0:T(8,128)(2,1)S(1)}, u32[]{:S(2)}, u32[]{:S(2)}) collective-permute-start(bf16[128,512]{1,0:T(8,128)(2,1)} %refs_5_.1), channel_id=1, source_target_pairs={{0,7},{1,0},{2,1},{3,2},{4,3},{5,4},{6,5},{7,6},{8,15},{9,8},{10,9... | collective-permute-start | bytes 393224 | tf_op jit(solution)/shard_map/ppermute | solution.py:235
  20.2 7.3 %collective-permute-start.4 = (bf16[2,144,256]{2,1,0:T(8,128)(2,1)S(1)}, bf16[2,144,256]{2,1,0:T(8,128)(2,1)S(1)}, u32[]{:S(2)}, u32[]{:S(2)}) collective-permute-start(bf16[2,144,256]{2,1,0:T(8,128)(2,1)S(1)} %pad_maximum_fusion.2), channel_id=1, source_target_pairs={{0,48},{8,56},{16,64},{24,72},{32,80},{40,88},{48,96},{56,104},{64... | collective-permute-start | bytes 442376 | tf_op jit(solution)/shard_map/ppermute | solution.py:227
  22.0 9.4 %collective-permute-start.10 = (bf16[128,512]{1,0:T(8,128)(2,1)}, bf16[128,512]{1,0:T(8,128)(2,1)S(1)}, u32[]{:S(2)}, u32[]{:S(2)}) collective-permute-start(bf16[128,512]{1,0:T(8,128)(2,1)} %refs_5_.1), channel_id=1, source_target_pairs={{0,1},{1,2},{2,3},{3,4},{4,5},{5,6},{6,7},{7,0},{8,9},{9,10},{10,1... | collective-permute-start | bytes 393224 | tf_op jit(solution)/shard_map/ppermute | solution.py:235
  27.4 7.3 %collective-permute-start.6 = (bf16[6,144,256]{2,1,0:T(8,128)(2,1)S(1)}, bf16[6,144,256]{2,1,0:T(8,128)(2,1)S(1)}, u32[]{:S(2)}, u32[]{:S(2)}) collective-permute-start(bf16[6,144,256]{2,1,0:T(8,128)(2,1)S(1)} %constant_dynamic-update-slice_fusion.2.refs_1_), channel_id=1, source_target_pairs={{0,8},{8,0},{16,24},{24,16},{32,40},{40,32},{48,56},{56,48},{64,72... | collective-permute-start | bytes 1327112 | tf_op jit(solution)/shard_map/ppermute | solution.py:231
  27.6 7.1 %collective-permute-start.5 = (bf16[3,144,256]{2,1,0:T(8,128)(2,1)S(1)}, bf16[3,144,256]{2,1,0:T(8,128)(2,1)S(1)}, u32[]{:S(2)}, u32[]{:S(2)}) collective-permute-start(bf16[3,144,256]{2,1,0:T(8,128)(2,1)S(1)} %constant_dynamic-update-slice_fusion.refs_0_), channel_id=1, source_target_pairs={{0,8},{8,0},{16,24},{24,16},{32,40},{40,32},{48,56},{56,48},{64,72... | collective-permute-start | bytes 663560 | tf_op jit(solution)/shard_map/ppermute | solution.py:231
  31.4 12.5 %collective-permute-start.11 = (bf16[256,512]{1,0:T(8,128)(2,1)S(1)}, bf16[256,512]{1,0:T(8,128)(2,1)S(1)}, u32[]{:S(2)}, u32[]{:S(2)}) collective-permute-start(bf16[256,512]{1,0:T(8,128)(2,1)S(1)} %get-tuple-element.58), channel_id=1, source_target_pairs={{0,1},{1,2},{2,3},{3,4},{4,5},{5,6},{6,7},{7,0},{8,9},{9,10},{10,1... | collective-permute-start | bytes 786440 | tf_op jit(solution)/shard_map/ppermute | solution.py:235
  31.5 12.4 %collective-permute-start.9 = (bf16[256,512]{1,0:T(8,128)(2,1)S(1)}, bf16[256,512]{1,0:T(8,128)(2,1)S(1)}, u32[]{:S(2)}, u32[]{:S(2)}) collective-permute-start(bf16[256,512]{1,0:T(8,128)(2,1)S(1)} %get-tuple-element.59), channel_id=1, source_target_pairs={{0,7},{1,0},{2,1},{3,2},{4,3},{5,4},{6,5},{7,6},{8,15},{9,8},{10,9... | collective-permute-start | bytes 786440 | tf_op jit(solution)/shard_map/ppermute | solution.py:235
  40.4 9.7 %collective-permute-start.12 = (bf16[2,128,512]{2,1,0:T(8,128)(2,1)S(1)}, bf16[2,128,512]{2,1,0:T(8,128)(2,1)S(1)}, u32[]{:S(2)}, u32[]{:S(2)}) collective-permute-start(bf16[2,128,512]{2,1,0:T(8,128)(2,1)S(1)} %get-tuple-element.41), channel_id=1, source_target_pairs={{0,1},{1,2},{2,3},{3,4},{4,5},{5,6},{6,7},{7,0},{8,9},{9,10},{10,1... | collective-permute-start | bytes 786440 | tf_op jit(solution)/shard_map/ppermute | solution.py:235
  40.7 9.5 %collective-permute-start.13 = (bf16[2,128,512]{2,1,0:T(8,128)(2,1)S(1)}, bf16[2,128,512]{2,1,0:T(8,128)(2,1)S(1)}, u32[]{:S(2)}, u32[]{:S(2)}) collective-permute-start(bf16[2,128,512]{2,1,0:T(8,128)(2,1)S(1)} %get-tuple-element.42), channel_id=1, source_target_pairs={{0,7},{1,0},{2,1},{3,2},{4,3},{5,4},{6,5},{7,6},{8,15},{9,8},{10,9... | collective-permute-start | bytes 786440 | tf_op jit(solution)/shard_map/ppermute | solution.py:235
  50.2 3.3 %collective-permute-start.17 = (bf16[3,128,256]{2,1,0:T(8,128)(2,1)S(1)}, bf16[3,128,256]{2,1,0:T(8,128)(2,1)S(1)}, u32[]{:S(2)}, u32[]{:S(2)}) collective-permute-start(bf16[3,128,256]{2,1,0:T(8,128)(2,1)S(1)} %get-tuple-element.49), channel_id=1, source_target_pairs={{0,8},{8,0},{16,24},{24,16},{32,40},{40,32},{48,56},{56,48},{64,72... | collective-permute-start | bytes 589832 | tf_op jit(solution)/shard_map/ppermute | solution.py:231
  50.2 3.3 %collective-permute-start.18 = (bf16[6,128,256]{2,1,0:T(8,128)(2,1)S(1)}, bf16[6,128,256]{2,1,0:T(8,128)(2,1)S(1)}, u32[]{:S(2)}, u32[]{:S(2)}) collective-permute-start(bf16[6,128,256]{2,1,0:T(8,128)(2,1)S(1)} %get-tuple-element.51), channel_id=1, source_target_pairs={{0,8},{8,0},{16,24},{24,16},{32,40},{40,32},{48,56},{56,48},{64,72... | collective-permute-start | bytes 1179656 | tf_op jit(solution)/shard_map/ppermute | solution.py:231
  50.8 19.7 %collective-permute-start.14 = (bf16[128,512]{1,0:T(8,128)(2,1)S(1)}, bf16[128,512]{1,0:T(8,128)(2,1)S(1)}, u32[]{:S(2)}, u32[]{:S(2)}) collective-permute-start(bf16[128,512]{1,0:T(8,128)(2,1)S(1)} %get-tuple-element.55), channel_id=1, source_target_pairs={{0,1},{1,2},{2,3},{3,4},{4,5},{5,6},{6,7},{7,0},{8,9},{9,10},{10,1... | collective-permute-start | bytes 393224 | tf_op jit(solution)/shard_map/ppermute | solution.py:235
  50.9 19.7 %collective-permute-start.15 = (bf16[128,512]{1,0:T(8,128)(2,1)S(1)}, bf16[128,512]{1,0:T(8,128)(2,1)S(1)}, u32[]{:S(2)}, u32[]{:S(2)}) collective-permute-start(bf16[128,512]{1,0:T(8,128)(2,1)S(1)} %get-tuple-element.56), channel_id=1, source_target_pairs={{0,4},{1,5},{2,6},{3,7},{4,0},{5,1},{6,2},{7,3},{8,12},{9,13},{10,... | collective-permute-start | bytes 393224 | tf_op jit(solution)/shard_map/ppermute | solution.py:235
  53.6 5.3 %collective-permute-start.19 = (bf16[2,128,256]{2,1,0:T(8,128)(2,1)S(1)}, bf16[2,128,256]{2,1,0:T(8,128)(2,1)S(1)}, u32[]{:S(2)}, u32[]{:S(2)}) collective-permute-start(bf16[2,128,256]{2,1,0:T(8,128)(2,1)S(1)} %get-tuple-element.52), channel_id=1, source_target_pairs={{0,240},{8,248},{16,0},{24,8},{32,16},{40,24},{48,32},{56,40},{64,... | collective-permute-start | bytes 393224 | tf_op jit(solution)/shard_map/ppermute | solution.py:227
  53.8 10.0 %collective-permute-start.21 = (bf16[2,128,256]{2,1,0:T(8,128)(2,1)S(1)}, bf16[2,128,256]{2,1,0:T(8,128)(2,1)S(1)}, u32[]{:S(2)}, u32[]{:S(2)}) collective-permute-start(bf16[2,128,256]{2,1,0:T(8,128)(2,1)S(1)} %get-tuple-element.53), channel_id=1, source_target_pairs={{0,208},{8,216},{16,224},{24,232},{32,240},{40,248},{48,0},{56,8},... | collective-permute-start | bytes 393224 | tf_op jit(solution)/shard_map/ppermute | solution.py:227
  57.0 13.4 %collective-permute-start.20 = (bf16[2,128,256]{2,1,0:T(8,128)(2,1)S(1)}, bf16[2,128,256]{2,1,0:T(8,128)(2,1)S(1)}, u32[]{:S(2)}, u32[]{:S(2)}) collective-permute-start(bf16[2,128,256]{2,1,0:T(8,128)(2,1)S(1)} %get-tuple-element.54), channel_id=1, source_target_pairs={{0,224},{8,232},{16,240},{24,248},{32,0},{40,8},{48,16},{56,24},{6... | collective-permute-start | bytes 393224 | tf_op jit(solution)/shard_map/ppermute | solution.py:227
  58.9 11.7 %collective-permute-start.16 = (bf16[128,512]{1,0:T(8,128)(2,1)S(1)}, bf16[128,512]{1,0:T(8,128)(2,1)S(1)}, u32[]{:S(2)}, u32[]{:S(2)}) collective-permute-start(bf16[128,512]{1,0:T(8,128)(2,1)S(1)} %get-tuple-element.57), channel_id=1, source_target_pairs={{0,7},{1,0},{2,1},{3,2},{4,3},{5,4},{6,5},{7,6},{8,15},{9,8},{10,9... | collective-permute-start | bytes 393224 | tf_op jit(solution)/shard_map/ppermute | solution.py:235
  63.9 8.8 %collective-permute-start.22 = (bf16[128,256]{1,0:T(8,128)(2,1)S(1)}, bf16[128,256]{1,0:T(8,128)(2,1)S(1)}, u32[]{:S(2)}, u32[]{:S(2)}) collective-permute-start(bf16[128,256]{1,0:T(8,128)(2,1)S(1)} %fusion.8), channel_id=1, source_target_pairs={{0,128},{8,136},{16,144},{24,152},{32,160},{40,168},{48,176},{56,1... | collective-permute-start | bytes 196616 | tf_op jit(solution)/shard_map/ppermute | solution.py:227
  70.5 4.3 %collective-permute-start.23 = (bf16[128,256]{1,0:T(8,128)(2,1)S(1)}, bf16[128,256]{1,0:T(8,128)(2,1)S(1)}, u32[]{:S(2)}, u32[]{:S(2)}) collective-permute-start(bf16[128,256]{1,0:T(8,128)(2,1)S(1)} %fusion.9), channel_id=1, source_target_pairs={{0,192},{8,200},{16,208},{24,216},{32,224},{40,232},{48,240},{56,2... | collective-permute-start | bytes 196616 | tf_op jit(solution)/shard_map/ppermute | solution.py:227
  (2 other events, 15.6 us)

commit v7 on v6

--- a/solution.py
+++ b/solution.py
@@ -330,14 +330,16 @@
     sum_up = along_z(low(near_up + wide(got_up[0])), 1)
     sum_four = along_z(low(near_four + wide(got_up[1]) + wide(got_down[1])), 4)
     sum_down = along_z(low(near_down + wide(got_down[0])), -1)
-    projected = low(kept + wide(sum_up) + wide(sum_four) + wide(sum_down))
 
     both = [wide(mine) + wide(across(theirs)) for mine, theirs in zip(grad_own, grad_sib)]
-    back = [wide(chips_on(low(both[1][2 * n : 2 * n + 2]), -(n + 1))) for n in range(3)]
+    back = [chips_on(low(both[1][2 * n : 2 * n + 2]), -(n + 1)) for n in range(3)]
+    back, sum_up, sum_down = lax.optimization_barrier((back, sum_up, sum_down))
+    back = [wide(value) for value in back]
     back_8 = wide(chips_on(low(both[0][2]), -8))
     near_sum = both[0][0:2] + back[0] + back[1] + back[2]
     total = near_sum[0] + back_8 + wide(chips_on(low(near_sum[1]), -4))
     total = low(total)
+    projected = low(kept + wide(sum_up) + wide(sum_four) + wide(sum_down))
     return projected, query_grad, total[:, :HEAD_SIZE], total[:, HEAD_SIZE:]
 
 

time: 75.4 us -> 73.9 us (0.980); the launches traced: 75.5 us -> 73.2 us
  waiting for transfers between devices: 16.4 us -> 13.4 us
    ppermute x10, waiting for transfers between devices: 13.2 us -> 10.3 us  [chips_on(): lax.ppermute(value, 'dp', [(i, (i + 2 * by) % 32) for i in range(32)])]
    ppermute x10, starting transfers between devices: 21.6 us -> 23.8 us  [along_z(): return lax.ppermute(value, 'tensor', [(i, (i + by) % 8) for i in range(8)])]
    ppermute x10, starting transfers between devices: 20 us -> 18.6 us  [chips_on(): lax.ppermute(value, 'dp', [(i, (i + 2 * by) % 32) for i in range(32)])]
  transfers between devices with their start and end apart: 24 -> 24, of which waited for: 7 -> 6; matrix products, arithmetic and copies ran while one was open for 2% -> 2% of each run, Pallas kernels for 16% -> 16%
where the time goes in v7:
time: 73.9 us; the launch traced here: 73.2 us
  starting transfers between devices  43.5 us (59%)
  waiting for transfers between devices  13.4 us (18%)
  Pallas kernels  11.9 us (16%)
  other arithmetic  2.69 us (4%)
  between operations  0.83 us (1%)
  local copies, waits for them, and re-layouts  0.8 us (1%)
    ppermute x10, starting transfers between devices, along_z(): return lax.ppermute(value, 'tensor', [(i, (i + by) % 8) for i in range(8)])  23.8 us
    ppermute x10, starting transfers between devices, chips_on(): lax.ppermute(value, 'dp', [(i, (i + 2 * by) % 32) for i in range(32)])  18.6 us
    ppermute x10, waiting for transfers between devices, chips_on(): lax.ppermute(value, 'dp', [(i, (i + 2 * by) % 32) for i in range(32)])  10.3 us
    pallas_call x1, Pallas kernels, backward(): pl.pallas_call(backward_kernel, in_specs=[SMEM] + [VMEM] * 14, out_specs=...  6.22 us
    pallas_call x1, Pallas kernels, forward(): pl.pallas_call(forward_kernel, in_specs=[SMEM, HBM] + [VMEM] * 5, out_spe...  5.72 us
    ppermute x10, waiting for transfers between devices, along_z(): return lax.ppermute(value, 'tensor', [(i, (i + by) % 8) for i in range(8)])  3.14 us
  transfers between devices with their start and end apart: 24, of which 6 were waited for; matrix products, arithmetic and copies ran while one was open for 2% of the time, Pallas kernels for 16%

profile of v7, /device:TPU:8, one launch (start us, length us, event | category | flops | bytes accessed | tf_op | source)
XLA Modules:
  0.0 73.2 jit_solution(8344664064640609879)
XLA Ops:
  0.6 0.7 convert_element_type.97
  1.4 0.8 %maximum_bitcast_fusion = bf16[1,144,256]{2,1,0:T(8,128)(2,1)S(1)} fusion(bf16[16,256]{1,0:T(8,128)(2,1)S(1)} %broadcast_in_dim.4, bf16[128,128]{1,0:T(8,128)(2,1)} %param.8, bf16[128,128]{1,0:T(8,128)(2,1)} %param.7), kind=kLoop, calls=%fused_computation.23 | loop fusion | flops 221184 | bytes 147456 | tf_op jit(solution)/shard_map/broadcast_in_dim | solution.py:61
  2.1 1.6 %collective-permute-start = (bf16[1,144,256]{2,1,0:T(8,128)(2,1)S(1)}, bf16[1,144,256]{2,1,0:T(8,128)(2,1)S(1)}, u32[]{:S(2)}, u32[]{:S(2)}) collective-permute-start(bf16[1,144,256]{2,1,0:T(8,128)(2,1)S(1)} %maximum_bitcast_fusion), channel_id=1, source_target_pairs={{0,64},{8,72},{16,80},{24,88},{32,96},{40,104},{48,112},{56,120},{... | collective-permute-start | bytes 221192 | tf_op jit(solution)/shard_map/ppermute | solution.py:227
  3.8 4.0 %collective-permute-done = bf16[1,144,256]{2,1,0:T(8,128)(2,1)S(1)} collective-permute-done((bf16[1,144,256]{2,1,0:T(8,128)(2,1)S(1)}, bf16[1,144,256]{2,1,0:T(8,128)(2,1)S(1)}, u32[]{:S(2)}, u32[]{:S(2)}) %collective-permute-start) | collective-permute-done | bytes 73760 | tf_op jit(solution)/shard_map/ppermute | solution.py:227
  7.8 1.7 %collective-permute-start.2 = (bf16[2,144,256]{2,1,0:T(8,128)(2,1)S(1)}, bf16[2,144,256]{2,1,0:T(8,128)(2,1)S(1)}, u32[]{:S(2)}, u32[]{:S(2)}) collective-permute-start(bf16[2,144,256]{2,1,0:T(8,128)(2,1)S(1)} %pad_maximum_fusion.2), channel_id=1, source_target_pairs={{0,16},{8,24},{16,32},{24,40},{32,48},{40,56},{48,64},{56,72},{64,... | collective-permute-start | bytes 442376 | tf_op jit(solution)/shard_map/ppermute | solution.py:227
  9.5 0.9 %collective-permute-start.3 = (bf16[2,144,256]{2,1,0:T(8,128)(2,1)S(1)}, bf16[2,144,256]{2,1,0:T(8,128)(2,1)S(1)}, u32[]{:S(2)}, u32[]{:S(2)}) collective-permute-start(bf16[2,144,256]{2,1,0:T(8,128)(2,1)S(1)} %pad_maximum_fusion.2), channel_id=1, source_target_pairs={{0,32},{8,40},{16,48},{24,56},{32,64},{40,72},{48,80},{56,88},{64,... | collective-permute-start | bytes 442376 | tf_op jit(solution)/shard_map/ppermute | solution.py:227
  10.4 2.5 %collective-permute-start.1 = (bf16[1,144,256]{2,1,0:T(8,128)(2,1)S(1)}, bf16[1,144,256]{2,1,0:T(8,128)(2,1)S(1)}, u32[]{:S(2)}, u32[]{:S(2)}) collective-permute-start(bf16[1,144,256]{2,1,0:T(8,128)(2,1)S(1)} %maximum_bitcast_fusion), channel_id=1, source_target_pairs={{0,128},{8,136},{16,144},{24,152},{32,160},{40,168},{48,176},{56,1... | collective-permute-start | bytes 221192 | tf_op jit(solution)/shard_map/ppermute | solution.py:227
  12.9 7.2 %collective-permute-start.8 = (bf16[128,512]{1,0:T(8,128)(2,1)}, bf16[128,512]{1,0:T(8,128)(2,1)S(1)}, u32[]{:S(2)}, u32[]{:S(2)}) collective-permute-start(bf16[128,512]{1,0:T(8,128)(2,1)} %refs_5_.1), channel_id=1, source_target_pairs={{0,4},{1,5},{2,6},{3,7},{4,0},{5,1},{6,2},{7,3},{8,12},{9,13},{10,... | collective-permute-start | bytes 393224 | tf_op jit(solution)/shard_map/ppermute | solution.py:235
  20.2 1.8 %collective-permute-start.4 = (bf16[2,144,256]{2,1,0:T(8,128)(2,1)S(1)}, bf16[2,144,256]{2,1,0:T(8,128)(2,1)S(1)}, u32[]{:S(2)}, u32[]{:S(2)}) collective-permute-start(bf16[2,144,256]{2,1,0:T(8,128)(2,1)S(1)} %pad_maximum_fusion.2), channel_id=1, source_target_pairs={{0,48},{8,56},{16,64},{24,72},{32,80},{40,88},{48,96},{56,104},{64... | collective-permute-start | bytes 442376 | tf_op jit(solution)/shard_map/ppermute | solution.py:227
  22.0 2.0 %collective-permute-start.10 = (bf16[128,512]{1,0:T(8,128)(2,1)}, bf16[128,512]{1,0:T(8,128)(2,1)S(1)}, u32[]{:S(2)}, u32[]{:S(2)}) collective-permute-start(bf16[128,512]{1,0:T(8,128)(2,1)} %refs_5_.1), channel_id=1, source_target_pairs={{0,1},{1,2},{2,3},{3,4},{4,5},{5,6},{6,7},{7,0},{8,9},{9,10},{10,1... | collective-permute-start | bytes 393224 | tf_op jit(solution)/shard_map/ppermute | solution.py:235
  24.0 3.4 %collective-permute-done.4 = bf16[2,144,256]{2,1,0:T(8,128)(2,1)S(1)} collective-permute-done((bf16[2,144,256]{2,1,0:T(8,128)(2,1)S(1)}, bf16[2,144,256]{2,1,0:T(8,128)(2,1)S(1)}, u32[]{:S(2)}, u32[]{:S(2)}) %collective-permute-start.4) | collective-permute-done | bytes 147488 | tf_op jit(solution)/shard_map/ppermute | solution.py:227
  28.2 3.1 %collective-permute-done.10.refs_4_ = bf16[128,512]{1,0:T(8,128)(2,1)S(1)} collective-permute-done((bf16[128,512]{1,0:T(8,128)(2,1)}, bf16[128,512]{1,0:T(8,128)(2,1)S(1)}, u32[]{:S(2)}, u32[]{:S(2)}) %collective-permute-start.10) | collective-permute-done | bytes 131104 | tf_op jit(solution)/shard_map/ppermute | solution.py:235
  31.5 3.2 %collective-permute-start.9 = (bf16[256,512]{1,0:T(8,128)(2,1)S(1)}, bf16[256,512]{1,0:T(8,128)(2,1)S(1)}, u32[]{:S(2)}, u32[]{:S(2)}) collective-permute-start(bf16[256,512]{1,0:T(8,128)(2,1)S(1)} %get-tuple-element.69), channel_id=1, source_target_pairs={{0,7},{1,0},{2,1},{3,2},{4,3},{5,4},{6,5},{7,6},{8,15},{9,8},{10,9... | collective-permute-start | bytes 786440 | tf_op jit(solution)/shard_map/ppermute | solution.py:235
  34.7 5.7 %shard_map.93 = (bf16[128,1024]{1,0:T(8,128)(2,1)S(1)}, f32[1,1024]{1,0:T(1,128)S(1)}, s32[1,128]{1,0:T(1,128)S(1)}, bf16[2304,128]{1,0:T(8,128)(2,1)S(1)}, bf16...) custom-call(s32[3]{0:T(128)S(1)} %pad_add_fusion.info_ref, ...), custom_call_target="tpu_custom_call" | custom-call | flops 8999999488 | bytes 1048576 | tf_op jit(solution)/shard_map/pallas_call | solution.py:247
  40.7 3.2 %collective-permute-start.13 = (bf16[2,128,512]{2,1,0:T(8,128)(2,1)S(1)}, bf16[2,128,512]{2,1,0:T(8,128)(2,1)S(1)}, u32[]{:S(2)}, u32[]{:S(2)}) collective-permute-start(bf16[2,128,512]{2,1,0:T(8,128)(2,1)S(1)} %get-tuple-element.47), channel_id=1, source_target_pairs={{0,7},{1,0},{2,1},{3,2},{4,3},{5,4},{6,5},{7,6},{8,15},{9,8},{10,9... | collective-permute-start | bytes 786440 | tf_op jit(solution)/shard_map/ppermute | solution.py:235
  43.9 6.2 %shard_map.94 = (bf16[128,1024]{1,0:T(8,128)(2,1)}, bf16[3,128,256]{2,1,0:T(8,128)(2,1)S(1)}, bf16[6,128,256]{2,1,0:T(8,128)(2,1)S(1)}, bf16[3,128,256]{2,1,0:T(8,128)(2,1)S(1)}, bf16[6,128,256]{2,1,0:T(8,128)(2,1)S(1)}) custom-call(s32[3]{0:T(128)S(1)} %pad_add_fusion.info_ref, bf16[1024,4096]{1,0:T(8,128)(2,1)S(1)} %get-tuple-element.36.held_ref, ...), custom_call_target="tpu_custom_call" | custom-call | flops 14000000000 | bytes 1048576 | tf_op jit(solution)/shard_map/pallas_call | solution.py:280
  50.9 3.2 %collective-permute-start.19 = (bf16[128,512]{1,0:T(8,128)(2,1)S(1)}, bf16[128,512]{1,0:T(8,128)(2,1)S(1)}, u32[]{:S(2)}, u32[]{:S(2)}) collective-permute-start(bf16[128,512]{1,0:T(8,128)(2,1)S(1)} %get-tuple-element.67), channel_id=1, source_target_pairs={{0,7},{1,0},{2,1},{3,2},{4,3},{5,4},{6,5},{7,6},{8,15},{9,8},{10,9... | collective-permute-start | bytes 393224 | tf_op jit(solution)/shard_map/ppermute | solution.py:235
  54.3 2.0 %collective-permute-start.17 = (bf16[2,128,256]{2,1,0:T(8,128)(2,1)S(1)}, bf16[2,128,256]{2,1,0:T(8,128)(2,1)S(1)}, u32[]{:S(2)}, u32[]{:S(2)}) collective-permute-start(bf16[2,128,256]{2,1,0:T(8,128)(2,1)S(1)} %get-tuple-element.62), channel_id=1, source_target_pairs={{0,208},{8,216},{16,224},{24,232},{32,240},{40,248},{48,0},{56,8},... | collective-permute-start | bytes 393224 | tf_op jit(solution)/shard_map/ppermute | solution.py:227
  56.3 3.0 %collective-permute-start.16 = (bf16[2,128,256]{2,1,0:T(8,128)(2,1)S(1)}, bf16[2,128,256]{2,1,0:T(8,128)(2,1)S(1)}, u32[]{:S(2)}, u32[]{:S(2)}) collective-permute-start(bf16[2,128,256]{2,1,0:T(8,128)(2,1)S(1)} %get-tuple-element.63), channel_id=1, source_target_pairs={{0,224},{8,232},{16,240},{24,248},{32,0},{40,8},{48,16},{56,24},{6... | collective-permute-start | bytes 393224 | tf_op jit(solution)/shard_map/ppermute | solution.py:227
  59.4 4.4 %collective-permute-start.20 = (bf16[128,512]{1,0:T(8,128)(2,1)S(1)}, bf16[128,512]{1,0:T(8,128)(2,1)S(1)}, u32[]{:S(2)}, u32[]{:S(2)}) collective-permute-start(bf16[128,512]{1,0:T(8,128)(2,1)S(1)} %get-tuple-element.65), channel_id=1, source_target_pairs={{0,4},{1,5},{2,6},{3,7},{4,0},{5,1},{6,2},{7,3},{8,12},{9,13},{10,... | collective-permute-start | bytes 393224 | tf_op jit(solution)/shard_map/ppermute | solution.py:235
  64.0 1.4 %collective-permute-done.15 = bf16[2,128,256]{2,1,0:T(8,128)(2,1)S(1)} collective-permute-done((bf16[2,128,256]{2,1,0:T(8,128)(2,1)S(1)}, bf16[2,128,256]{2,1,0:T(8,128)(2,1)S(1)}, u32[]{:S(2)}, u32[]{:S(2)}) %collective-permute-start.15) | collective-permute-done | bytes 131104 | tf_op jit(solution)/shard_map/ppermute | solution.py:227
  65.5 5.1 %collective-permute-start.23 = (bf16[128,256]{1,0:T(8,128)(2,1)S(1)}, bf16[128,256]{1,0:T(8,128)(2,1)S(1)}, u32[]{:S(2)}, u32[]{:S(2)}) collective-permute-start(bf16[128,256]{1,0:T(8,128)(2,1)S(1)} %fusion.9), channel_id=1, source_target_pairs={{0,192},{8,200},{16,208},{24,216},{32,224},{40,232},{48,240},{56,2... | collective-permute-start | bytes 196616 | tf_op jit(solution)/shard_map/ppermute | solution.py:227
  70.6 0.7 add_convert_fusion.1
  71.4 1.2 %collective-permute-done.23 = bf16[128,256]{1,0:T(8,128)(2,1)S(1)} collective-permute-done((bf16[128,256]{1,0:T(8,128)(2,1)S(1)}, bf16[128,256]{1,0:T(8,128)(2,1)S(1)}, u32[]{:S(2)}, u32[]{:S(2)}) %collective-permute-start.23) | collective-permute-done | bytes 65568 | tf_op jit(solution)/shard_map/ppermute | solution.py:227
  (53 shorter events, 3.3 us)
Async XLA Ops:
  2.1 5.6 %collective-permute-start = (bf16[1,144,256]{2,1,0:T(8,128)(2,1)S(1)}, bf16[1,144,256]{2,1,0:T(8,128)(2,1)S(1)}, u32[]{:S(2)}, u32[]{:S(2)}) collective-permute-start(bf16[1,144,256]{2,1,0:T(8,128)(2,1)S(1)} %maximum_bitcast_fusion), channel_id=1, source_target_pairs={{0,64},{8,72},{16,80},{24,88},{32,96},{40,104},{48,112},{56,120},{... | collective-permute-start | bytes 221192 | tf_op jit(solution)/shard_map/ppermute | solution.py:227
  7.8 12.3 %collective-permute-start.2 = (bf16[2,144,256]{2,1,0:T(8,128)(2,1)S(1)}, bf16[2,144,256]{2,1,0:T(8,128)(2,1)S(1)}, u32[]{:S(2)}, u32[]{:S(2)}) collective-permute-start(bf16[2,144,256]{2,1,0:T(8,128)(2,1)S(1)} %pad_maximum_fusion.2), channel_id=1, source_target_pairs={{0,16},{8,24},{16,32},{24,40},{32,48},{40,56},{48,64},{56,72},{64,... | collective-permute-start | bytes 442376 | tf_op jit(solution)/shard_map/ppermute | solution.py:227
  9.5 12.5 %collective-permute-start.3 = (bf16[2,144,256]{2,1,0:T(8,128)(2,1)S(1)}, bf16[2,144,256]{2,1,0:T(8,128)(2,1)S(1)}, u32[]{:S(2)}, u32[]{:S(2)}) collective-permute-start(bf16[2,144,256]{2,1,0:T(8,128)(2,1)S(1)} %pad_maximum_fusion.2), channel_id=1, source_target_pairs={{0,32},{8,40},{16,48},{24,56},{32,64},{40,72},{48,80},{56,88},{64,... | collective-permute-start | bytes 442376 | tf_op jit(solution)/shard_map/ppermute | solution.py:227
  10.4 17.2 %collective-permute-start.1 = (bf16[1,144,256]{2,1,0:T(8,128)(2,1)S(1)}, bf16[1,144,256]{2,1,0:T(8,128)(2,1)S(1)}, u32[]{:S(2)}, u32[]{:S(2)}) collective-permute-start(bf16[1,144,256]{2,1,0:T(8,128)(2,1)S(1)} %maximum_bitcast_fusion), channel_id=1, source_target_pairs={{0,128},{8,136},{16,144},{24,152},{32,160},{40,168},{48,176},{56,1... | collective-permute-start | bytes 221192 | tf_op jit(solution)/shard_map/ppermute | solution.py:227
  12.9 15.4 %collective-permute-start.8 = (bf16[128,512]{1,0:T(8,128)(2,1)}, bf16[128,512]{1,0:T(8,128)(2,1)S(1)}, u32[]{:S(2)}, u32[]{:S(2)}) collective-permute-start(bf16[128,512]{1,0:T(8,128)(2,1)} %refs_5_.1), channel_id=1, source_target_pairs={{0,4},{1,5},{2,6},{3,7},{4,0},{5,1},{6,2},{7,3},{8,12},{9,13},{10,... | collective-permute-start | bytes 393224 | tf_op jit(solution)/shard_map/ppermute | solution.py:235
  20.0 8.2 %collective-permute-start.7 = (bf16[128,512]{1,0:T(8,128)(2,1)}, bf16[128,512]{1,0:T(8,128)(2,1)S(1)}, u32[]{:S(2)}, u32[]{:S(2)}) collective-permute-start(bf16[128,512]{1,0:T(8,128)(2,1)} %refs_5_.1), channel_id=1, source_target_pairs={{0,7},{1,0},{2,1},{3,2},{4,3},{5,4},{6,5},{7,6},{8,15},{9,8},{10,9... | collective-permute-start | bytes 393224 | tf_op jit(solution)/shard_map/ppermute | solution.py:235
  20.2 7.3 %collective-permute-start.4 = (bf16[2,144,256]{2,1,0:T(8,128)(2,1)S(1)}, bf16[2,144,256]{2,1,0:T(8,128)(2,1)S(1)}, u32[]{:S(2)}, u32[]{:S(2)}) collective-permute-start(bf16[2,144,256]{2,1,0:T(8,128)(2,1)S(1)} %pad_maximum_fusion.2), channel_id=1, source_target_pairs={{0,48},{8,56},{16,64},{24,72},{32,80},{40,88},{48,96},{56,104},{64... | collective-permute-start | bytes 442376 | tf_op jit(solution)/shard_map/ppermute | solution.py:227
  22.0 9.4 %collective-permute-start.10 = (bf16[128,512]{1,0:T(8,128)(2,1)}, bf16[128,512]{1,0:T(8,128)(2,1)S(1)}, u32[]{:S(2)}, u32[]{:S(2)}) collective-permute-start(bf16[128,512]{1,0:T(8,128)(2,1)} %refs_5_.1), channel_id=1, source_target_pairs={{0,1},{1,2},{2,3},{3,4},{4,5},{5,6},{6,7},{7,0},{8,9},{9,10},{10,1... | collective-permute-start | bytes 393224 | tf_op jit(solution)/shard_map/ppermute | solution.py:235
  27.4 7.3 %collective-permute-start.6 = (bf16[6,144,256]{2,1,0:T(8,128)(2,1)S(1)}, bf16[6,144,256]{2,1,0:T(8,128)(2,1)S(1)}, u32[]{:S(2)}, u32[]{:S(2)}) collective-permute-start(bf16[6,144,256]{2,1,0:T(8,128)(2,1)S(1)} %constant_dynamic-update-slice_fusion.2.refs_1_), channel_id=1, source_target_pairs={{0,8},{8,0},{16,24},{24,16},{32,40},{40,32},{48,56},{56,48},{64,72... | collective-permute-start | bytes 1327112 | tf_op jit(solution)/shard_map/ppermute | solution.py:231
  27.6 7.1 %collective-permute-start.5 = (bf16[3,144,256]{2,1,0:T(8,128)(2,1)S(1)}, bf16[3,144,256]{2,1,0:T(8,128)(2,1)S(1)}, u32[]{:S(2)}, u32[]{:S(2)}) collective-permute-start(bf16[3,144,256]{2,1,0:T(8,128)(2,1)S(1)} %constant_dynamic-update-slice_fusion.refs_0_), channel_id=1, source_target_pairs={{0,8},{8,0},{16,24},{24,16},{32,40},{40,32},{48,56},{56,48},{64,72... | collective-permute-start | bytes 663560 | tf_op jit(solution)/shard_map/ppermute | solution.py:231
  31.4 12.5 %collective-permute-start.11 = (bf16[256,512]{1,0:T(8,128)(2,1)S(1)}, bf16[256,512]{1,0:T(8,128)(2,1)S(1)}, u32[]{:S(2)}, u32[]{:S(2)}) collective-permute-start(bf16[256,512]{1,0:T(8,128)(2,1)S(1)} %get-tuple-element.68), channel_id=1, source_target_pairs={{0,1},{1,2},{2,3},{3,4},{4,5},{5,6},{6,7},{7,0},{8,9},{9,10},{10,1... | collective-permute-start | bytes 786440 | tf_op jit(solution)/shard_map/ppermute | solution.py:235
  31.5 12.4 %collective-permute-start.9 = (bf16[256,512]{1,0:T(8,128)(2,1)S(1)}, bf16[256,512]{1,0:T(8,128)(2,1)S(1)}, u32[]{:S(2)}, u32[]{:S(2)}) collective-permute-start(bf16[256,512]{1,0:T(8,128)(2,1)S(1)} %get-tuple-element.69), channel_id=1, source_target_pairs={{0,7},{1,0},{2,1},{3,2},{4,3},{5,4},{6,5},{7,6},{8,15},{9,8},{10,9... | collective-permute-start | bytes 786440 | tf_op jit(solution)/shard_map/ppermute | solution.py:235
  40.4 9.7 %collective-permute-start.12 = (bf16[2,128,512]{2,1,0:T(8,128)(2,1)S(1)}, bf16[2,128,512]{2,1,0:T(8,128)(2,1)S(1)}, u32[]{:S(2)}, u32[]{:S(2)}) collective-permute-start(bf16[2,128,512]{2,1,0:T(8,128)(2,1)S(1)} %get-tuple-element.46), channel_id=1, source_target_pairs={{0,1},{1,2},{2,3},{3,4},{4,5},{5,6},{6,7},{7,0},{8,9},{9,10},{10,1... | collective-permute-start | bytes 786440 | tf_op jit(solution)/shard_map/ppermute | solution.py:235
  40.7 9.5 %collective-permute-start.13 = (bf16[2,128,512]{2,1,0:T(8,128)(2,1)S(1)}, bf16[2,128,512]{2,1,0:T(8,128)(2,1)S(1)}, u32[]{:S(2)}, u32[]{:S(2)}) collective-permute-start(bf16[2,128,512]{2,1,0:T(8,128)(2,1)S(1)} %get-tuple-element.47), channel_id=1, source_target_pairs={{0,7},{1,0},{2,1},{3,2},{4,3},{5,4},{6,5},{7,6},{8,15},{9,8},{10,9... | collective-permute-start | bytes 786440 | tf_op jit(solution)/shard_map/ppermute | solution.py:235
  50.2 4.0 %collective-permute-start.21 = (bf16[3,128,256]{2,1,0:T(8,128)(2,1)S(1)}, bf16[3,128,256]{2,1,0:T(8,128)(2,1)S(1)}, u32[]{:S(2)}, u32[]{:S(2)}) collective-permute-start(bf16[3,128,256]{2,1,0:T(8,128)(2,1)S(1)} %get-tuple-element.58), channel_id=1, source_target_pairs={{0,8},{8,0},{16,24},{24,16},{32,40},{40,32},{48,56},{56,48},{64,72... | collective-permute-start | bytes 589832 | tf_op jit(solution)/shard_map/ppermute | solution.py:231
  50.2 4.0 %collective-permute-start.14 = (bf16[6,128,256]{2,1,0:T(8,128)(2,1)S(1)}, bf16[6,128,256]{2,1,0:T(8,128)(2,1)S(1)}, u32[]{:S(2)}, u32[]{:S(2)}) collective-permute-start(bf16[6,128,256]{2,1,0:T(8,128)(2,1)S(1)} %get-tuple-element.48), channel_id=1, source_target_pairs={{0,8},{8,0},{16,24},{24,16},{32,40},{40,32},{48,56},{56,48},{64,72... | collective-permute-start | bytes 1179656 | tf_op jit(solution)/shard_map/ppermute | solution.py:231
  50.8 8.6 %collective-permute-start.18 = (bf16[128,512]{1,0:T(8,128)(2,1)S(1)}, bf16[128,512]{1,0:T(8,128)(2,1)S(1)}, u32[]{:S(2)}, u32[]{:S(2)}) collective-permute-start(bf16[128,512]{1,0:T(8,128)(2,1)S(1)} %get-tuple-element.66), channel_id=1, source_target_pairs={{0,1},{1,2},{2,3},{3,4},{4,5},{5,6},{6,7},{7,0},{8,9},{9,10},{10,1... | collective-permute-start | bytes 393224 | tf_op jit(solution)/shard_map/ppermute | solution.py:235
  50.9 12.9 %collective-permute-start.19 = (bf16[128,512]{1,0:T(8,128)(2,1)S(1)}, bf16[128,512]{1,0:T(8,128)(2,1)S(1)}, u32[]{:S(2)}, u32[]{:S(2)}) collective-permute-start(bf16[128,512]{1,0:T(8,128)(2,1)S(1)} %get-tuple-element.67), channel_id=1, source_target_pairs={{0,7},{1,0},{2,1},{3,2},{4,3},{5,4},{6,5},{7,6},{8,15},{9,8},{10,9... | collective-permute-start | bytes 393224 | tf_op jit(solution)/shard_map/ppermute | solution.py:235
  54.3 9.5 %collective-permute-start.17 = (bf16[2,128,256]{2,1,0:T(8,128)(2,1)S(1)}, bf16[2,128,256]{2,1,0:T(8,128)(2,1)S(1)}, u32[]{:S(2)}, u32[]{:S(2)}) collective-permute-start(bf16[2,128,256]{2,1,0:T(8,128)(2,1)S(1)} %get-tuple-element.62), channel_id=1, source_target_pairs={{0,208},{8,216},{16,224},{24,232},{32,240},{40,248},{48,0},{56,8},... | collective-permute-start | bytes 393224 | tf_op jit(solution)/shard_map/ppermute | solution.py:227
  56.3 7.7 %collective-permute-start.16 = (bf16[2,128,256]{2,1,0:T(8,128)(2,1)S(1)}, bf16[2,128,256]{2,1,0:T(8,128)(2,1)S(1)}, u32[]{:S(2)}, u32[]{:S(2)}) collective-permute-start(bf16[2,128,256]{2,1,0:T(8,128)(2,1)S(1)} %get-tuple-element.63), channel_id=1, source_target_pairs={{0,224},{8,232},{16,240},{24,248},{32,0},{40,8},{48,16},{56,24},{6... | collective-permute-start | bytes 393224 | tf_op jit(solution)/shard_map/ppermute | solution.py:227
  59.4 6.1 %collective-permute-start.15 = (bf16[2,128,256]{2,1,0:T(8,128)(2,1)S(1)}, bf16[2,128,256]{2,1,0:T(8,128)(2,1)S(1)}, u32[]{:S(2)}, u32[]{:S(2)}) collective-permute-start(bf16[2,128,256]{2,1,0:T(8,128)(2,1)S(1)} %get-tuple-element.64), channel_id=1, source_target_pairs={{0,240},{8,248},{16,0},{24,8},{32,16},{40,24},{48,32},{56,40},{64,... | collective-permute-start | bytes 393224 | tf_op jit(solution)/shard_map/ppermute | solution.py:227
  59.4 11.2 %collective-permute-start.20 = (bf16[128,512]{1,0:T(8,128)(2,1)S(1)}, bf16[128,512]{1,0:T(8,128)(2,1)S(1)}, u32[]{:S(2)}, u32[]{:S(2)}) collective-permute-start(bf16[128,512]{1,0:T(8,128)(2,1)S(1)} %get-tuple-element.65), channel_id=1, source_target_pairs={{0,4},{1,5},{2,6},{3,7},{4,0},{5,1},{6,2},{7,3},{8,12},{9,13},{10,... | collective-permute-start | bytes 393224 | tf_op jit(solution)/shard_map/ppermute | solution.py:235
  63.8 7.6 %collective-permute-start.22 = (bf16[128,256]{1,0:T(8,128)(2,1)S(1)}, bf16[128,256]{1,0:T(8,128)(2,1)S(1)}, u32[]{:S(2)}, u32[]{:S(2)}) collective-permute-start(bf16[128,256]{1,0:T(8,128)(2,1)S(1)} %fusion.8), channel_id=1, source_target_pairs={{0,128},{8,136},{16,144},{24,152},{32,160},{40,168},{48,176},{56,1... | collective-permute-start | bytes 196616 | tf_op jit(solution)/shard_map/ppermute | solution.py:227
  65.5 7.0 %collective-permute-start.23 = (bf16[128,256]{1,0:T(8,128)(2,1)S(1)}, bf16[128,256]{1,0:T(8,128)(2,1)S(1)}, u32[]{:S(2)}, u32[]{:S(2)}) collective-permute-start(bf16[128,256]{1,0:T(8,128)(2,1)S(1)} %fusion.9), channel_id=1, source_target_pairs={{0,192},{8,200},{16,208},{24,216},{32,224},{40,232},{48,240},{56,2... | collective-permute-start | bytes 196616 | tf_op jit(solution)/shard_map/ppermute | solution.py:227
  (2 other events, 15.6 us)

commit v8 on v7

--- a/solution.py
+++ b/solution.py
@@ -333,7 +333,7 @@
 
     both = [wide(mine) + wide(across(theirs)) for mine, theirs in zip(grad_own, grad_sib)]
     back = [chips_on(low(both[1][2 * n : 2 * n + 2]), -(n + 1)) for n in range(3)]
-    back, sum_up, sum_down = lax.optimization_barrier((back, sum_up, sum_down))
+    back, sum_down = lax.optimization_barrier((back, sum_down))
     back = [wide(value) for value in back]
     back_8 = wide(chips_on(low(both[0][2]), -8))
     near_sum = both[0][0:2] + back[0] + back[1] + back[2]

time: 73.9 us -> 74.2 us (level)
  the two profiles are of different devices: /device:TPU:8 before, /device:TPU:1 now
where the time goes in v8:
time: 74.2 us; the launch traced here: 74 us
  starting transfers between devices  49 us (66%)
  Pallas kernels  10.8 us (15%)
  waiting for transfers between devices  9.92 us (13%)
  other arithmetic  2.69 us (4%)
  between operations  0.81 us (1%)
  local copies, waits for them, and re-layouts  0.8 us (1%)
    ppermute x10, starting transfers between devices, along_z(): return lax.ppermute(value, 'tensor', [(i, (i + by) % 8) for i in range(8)])  21.5 us
    ppermute x10, starting transfers between devices, chips_on(): lax.ppermute(value, 'dp', [(i, (i + 2 * by) % 32) for i in range(32)])  21 us
    ppermute x4, starting transfers between devices, across(): return lax.ppermute(value, 'dp', [(i, i ^ 1) for i in range(32)])  6.54 us
    ppermute x10, waiting for transfers between devices, chips_on(): lax.ppermute(value, 'dp', [(i, (i + 2 * by) % 32) for i in range(32)])  5.8 us
    pallas_call x1, Pallas kernels, forward(): pl.pallas_call(forward_kernel, in_specs=[SMEM, HBM] + [VMEM] * 5, out_spe...  5.72 us
    pallas_call x1, Pallas kernels, backward(): pl.pallas_call(backward_kernel, in_specs=[SMEM] + [VMEM] * 14, out_specs=...  5.09 us
    ppermute x10, waiting for transfers between devices, along_z(): return lax.ppermute(value, 'tensor', [(i, (i + by) % 8) for i in range(8)])  4.11 us
  transfers between devices with their start and end apart: 24, of which 3 were waited for; matrix products, arithmetic and copies ran while one was open for 2% of the time, Pallas kernels for 15%

profile of v8, /device:TPU:1, one launch (start us, length us, event | category | flops | bytes accessed | tf_op | source)
XLA Modules:
  0.0 74.0 jit_solution(16235324364592046337)
XLA Ops:
  1.4 0.8 %maximum_bitcast_fusion = bf16[1,144,256]{2,1,0:T(8,128)(2,1)S(1)} fusion(bf16[16,256]{1,0:T(8,128)(2,1)S(1)} %broadcast_in_dim.4, bf16[128,128]{1,0:T(8,128)(2,1)} %param.8, bf16[128,128]{1,0:T(8,128)(2,1)} %param.7), kind=kLoop, calls=%fused_computation.23 | loop fusion | flops 221184 | bytes 147456 | tf_op jit(solution)/shard_map/broadcast_in_dim | solution.py:61
  2.1 2.1 %collective-permute-start = (bf16[1,144,256]{2,1,0:T(8,128)(2,1)S(1)}, bf16[1,144,256]{2,1,0:T(8,128)(2,1)S(1)}, u32[]{:S(2)}, u32[]{:S(2)}) collective-permute-start(bf16[1,144,256]{2,1,0:T(8,128)(2,1)S(1)} %maximum_bitcast_fusion), channel_id=1, source_target_pairs={{0,64},{8,72},{16,80},{24,88},{32,96},{40,104},{48,112},{56,120},{... | collective-permute-start | bytes 221192 | tf_op jit(solution)/shard_map/ppermute | solution.py:227
  4.3 3.0 %collective-permute-done = bf16[1,144,256]{2,1,0:T(8,128)(2,1)S(1)} collective-permute-done((bf16[1,144,256]{2,1,0:T(8,128)(2,1)S(1)}, bf16[1,144,256]{2,1,0:T(8,128)(2,1)S(1)}, u32[]{:S(2)}, u32[]{:S(2)}) %collective-permute-start) | collective-permute-done | bytes 73760 | tf_op jit(solution)/shard_map/ppermute | solution.py:227
  7.3 1.6 %collective-permute-start.2 = (bf16[2,144,256]{2,1,0:T(8,128)(2,1)S(1)}, bf16[2,144,256]{2,1,0:T(8,128)(2,1)S(1)}, u32[]{:S(2)}, u32[]{:S(2)}) collective-permute-start(bf16[2,144,256]{2,1,0:T(8,128)(2,1)S(1)} %pad_maximum_fusion.2), channel_id=1, source_target_pairs={{0,16},{8,24},{16,32},{24,40},{32,48},{40,56},{48,64},{56,72},{64,... | collective-permute-start | bytes 442376 | tf_op jit(solution)/shard_map/ppermute | solution.py:227
  8.9 2.6 %collective-permute-start.3 = (bf16[2,144,256]{2,1,0:T(8,128)(2,1)S(1)}, bf16[2,144,256]{2,1,0:T(8,128)(2,1)S(1)}, u32[]{:S(2)}, u32[]{:S(2)}) collective-permute-start(bf16[2,144,256]{2,1,0:T(8,128)(2,1)S(1)} %pad_maximum_fusion.2), channel_id=1, source_target_pairs={{0,32},{8,40},{16,48},{24,56},{32,64},{40,72},{48,80},{56,88},{64,... | collective-permute-start | bytes 442376 | tf_op jit(solution)/shard_map/ppermute | solution.py:227
  11.5 1.5 %collective-permute-start.1 = (bf16[1,144,256]{2,1,0:T(8,128)(2,1)S(1)}, bf16[1,144,256]{2,1,0:T(8,128)(2,1)S(1)}, u32[]{:S(2)}, u32[]{:S(2)}) collective-permute-start(bf16[1,144,256]{2,1,0:T(8,128)(2,1)S(1)} %maximum_bitcast_fusion), channel_id=1, source_target_pairs={{0,128},{8,136},{16,144},{24,152},{32,160},{40,168},{48,176},{56,1... | collective-permute-start | bytes 221192 | tf_op jit(solution)/shard_map/ppermute | solution.py:227
  13.0 6.9 %collective-permute-start.8 = (bf16[128,512]{1,0:T(8,128)(2,1)}, bf16[128,512]{1,0:T(8,128)(2,1)S(1)}, u32[]{:S(2)}, u32[]{:S(2)}) collective-permute-start(bf16[128,512]{1,0:T(8,128)(2,1)} %refs_5_.1), channel_id=1, source_target_pairs={{0,4},{1,5},{2,6},{3,7},{4,0},{5,1},{6,2},{7,3},{8,12},{9,13},{10,... | collective-permute-start | bytes 393224 | tf_op jit(solution)/shard_map/ppermute | solution.py:235
  19.9 1.7 %collective-permute-start.4 = (bf16[2,144,256]{2,1,0:T(8,128)(2,1)S(1)}, bf16[2,144,256]{2,1,0:T(8,128)(2,1)S(1)}, u32[]{:S(2)}, u32[]{:S(2)}) collective-permute-start(bf16[2,144,256]{2,1,0:T(8,128)(2,1)S(1)} %pad_maximum_fusion.2), channel_id=1, source_target_pairs={{0,48},{8,56},{16,64},{24,72},{32,80},{40,88},{48,96},{56,104},{64... | collective-permute-start | bytes 442376 | tf_op jit(solution)/shard_map/ppermute | solution.py:227
  21.7 1.5 %collective-permute-start.10 = (bf16[128,512]{1,0:T(8,128)(2,1)}, bf16[128,512]{1,0:T(8,128)(2,1)S(1)}, u32[]{:S(2)}, u32[]{:S(2)}) collective-permute-start(bf16[128,512]{1,0:T(8,128)(2,1)} %refs_5_.1), channel_id=1, source_target_pairs={{0,1},{1,2},{2,3},{3,4},{4,5},{5,6},{6,7},{7,0},{8,9},{9,10},{10,1... | collective-permute-start | bytes 393224 | tf_op jit(solution)/shard_map/ppermute | solution.py:235
  23.2 2.8 %collective-permute-done.4 = bf16[2,144,256]{2,1,0:T(8,128)(2,1)S(1)} collective-permute-done((bf16[2,144,256]{2,1,0:T(8,128)(2,1)S(1)}, bf16[2,144,256]{2,1,0:T(8,128)(2,1)S(1)}, u32[]{:S(2)}, u32[]{:S(2)}) %collective-permute-start.4) | collective-permute-done | bytes 147488 | tf_op jit(solution)/shard_map/ppermute | solution.py:227
  26.1 4.3 %collective-permute-start.6 = (bf16[6,144,256]{2,1,0:T(8,128)(2,1)S(1)}, bf16[6,144,256]{2,1,0:T(8,128)(2,1)S(1)}, u32[]{:S(2)}, u32[]{:S(2)}) collective-permute-start(bf16[6,144,256]{2,1,0:T(8,128)(2,1)S(1)} %constant_dynamic-update-slice_fusion.2.refs_1_), channel_id=1, source_target_pairs={{0,8},{8,0},{16,24},{24,16},{32,40},{40,32},{48,56},{56,48},{64,72... | collective-permute-start | bytes 1327112 | tf_op jit(solution)/shard_map/ppermute | solution.py:231
  30.6 1.7 %collective-permute-start.11 = (bf16[256,512]{1,0:T(8,128)(2,1)S(1)}, bf16[256,512]{1,0:T(8,128)(2,1)S(1)}, u32[]{:S(2)}, u32[]{:S(2)}) collective-permute-start(bf16[256,512]{1,0:T(8,128)(2,1)S(1)} %get-tuple-element.66), channel_id=1, source_target_pairs={{0,1},{1,2},{2,3},{3,4},{4,5},{5,6},{6,7},{7,0},{8,9},{9,10},{10,1... | collective-permute-start | bytes 786440 | tf_op jit(solution)/shard_map/ppermute | solution.py:235
  32.3 1.2 %collective-permute-start.9 = (bf16[256,512]{1,0:T(8,128)(2,1)S(1)}, bf16[256,512]{1,0:T(8,128)(2,1)S(1)}, u32[]{:S(2)}, u32[]{:S(2)}) collective-permute-start(bf16[256,512]{1,0:T(8,128)(2,1)S(1)} %get-tuple-element.67), channel_id=1, source_target_pairs={{0,7},{1,0},{2,1},{3,2},{4,3},{5,4},{6,5},{7,6},{8,15},{9,8},{10,9... | collective-permute-start | bytes 786440 | tf_op jit(solution)/shard_map/ppermute | solution.py:235
  33.6 5.7 %shard_map.93 = (bf16[128,1024]{1,0:T(8,128)(2,1)S(1)}, f32[1,1024]{1,0:T(1,128)S(1)}, s32[1,128]{1,0:T(1,128)S(1)}, bf16[2304,128]{1,0:T(8,128)(2,1)S(1)}, bf16...) custom-call(s32[3]{0:T(128)S(1)} %pad_add_fusion.info_ref, ...), custom_call_target="tpu_custom_call" | custom-call | flops 8999999488 | bytes 1048576 | tf_op jit(solution)/shard_map/pallas_call | solution.py:247
  39.8 2.4 %collective-permute-start.13 = (bf16[2,128,512]{2,1,0:T(8,128)(2,1)S(1)}, bf16[2,128,512]{2,1,0:T(8,128)(2,1)S(1)}, u32[]{:S(2)}, u32[]{:S(2)}) collective-permute-start(bf16[2,128,512]{2,1,0:T(8,128)(2,1)S(1)} %get-tuple-element.46), channel_id=1, source_target_pairs={{0,7},{1,0},{2,1},{3,2},{4,3},{5,4},{6,5},{7,6},{8,15},{9,8},{10,9... | collective-permute-start | bytes 786440 | tf_op jit(solution)/shard_map/ppermute | solution.py:235
  42.2 5.1 %shard_map.94 = (bf16[128,1024]{1,0:T(8,128)(2,1)}, bf16[3,128,256]{2,1,0:T(8,128)(2,1)S(1)}, bf16[6,128,256]{2,1,0:T(8,128)(2,1)S(1)}, bf16[3,128,256]{2,1,0:T(8,128)(2,1)S(1)}, bf16[6,128,256]{2,1,0:T(8,128)(2,1)S(1)}) custom-call(s32[3]{0:T(128)S(1)} %pad_add_fusion.info_ref, bf16[1024,4096]{1,0:T(8,128)(2,1)S(1)} %get-tuple-element.36.held_ref, ...), custom_call_target="tpu_custom_call" | custom-call | flops 14000000000 | bytes 1048576 | tf_op jit(solution)/shard_map/pallas_call | solution.py:280
  47.3 2.1 %collective-permute-start.21 = (bf16[3,128,256]{2,1,0:T(8,128)(2,1)S(1)}, bf16[3,128,256]{2,1,0:T(8,128)(2,1)S(1)}, u32[]{:S(2)}, u32[]{:S(2)}) collective-permute-start(bf16[3,128,256]{2,1,0:T(8,128)(2,1)S(1)} %get-tuple-element.56), channel_id=1, source_target_pairs={{0,8},{8,0},{16,24},{24,16},{32,40},{40,32},{48,56},{56,48},{64,72... | collective-permute-start | bytes 589832 | tf_op jit(solution)/shard_map/ppermute | solution.py:231
  49.7 2.7 %collective-permute-start.20 = (bf16[128,512]{1,0:T(8,128)(2,1)S(1)}, bf16[128,512]{1,0:T(8,128)(2,1)S(1)}, u32[]{:S(2)}, u32[]{:S(2)}) collective-permute-start(bf16[128,512]{1,0:T(8,128)(2,1)S(1)} %get-tuple-element.65), channel_id=1, source_target_pairs={{0,7},{1,0},{2,1},{3,2},{4,3},{5,4},{6,5},{7,6},{8,15},{9,8},{10,9... | collective-permute-start | bytes 393224 | tf_op jit(solution)/shard_map/ppermute | solution.py:235
  52.7 2.8 %collective-permute-start.19 = (bf16[2,128,256]{2,1,0:T(8,128)(2,1)S(1)}, bf16[2,128,256]{2,1,0:T(8,128)(2,1)S(1)}, u32[]{:S(2)}, u32[]{:S(2)}) collective-permute-start(bf16[2,128,256]{2,1,0:T(8,128)(2,1)S(1)} %get-tuple-element.60), channel_id=1, source_target_pairs={{0,208},{8,216},{16,224},{24,232},{32,240},{40,248},{48,0},{56,8},... | collective-permute-start | bytes 393224 | tf_op jit(solution)/shard_map/ppermute | solution.py:227
  55.4 0.8 %collective-permute-start.18 = (bf16[2,128,256]{2,1,0:T(8,128)(2,1)S(1)}, bf16[2,128,256]{2,1,0:T(8,128)(2,1)S(1)}, u32[]{:S(2)}, u32[]{:S(2)}) collective-permute-start(bf16[2,128,256]{2,1,0:T(8,128)(2,1)S(1)} %get-tuple-element.61), channel_id=1, source_target_pairs={{0,224},{8,232},{16,240},{24,248},{32,0},{40,8},{48,16},{56,24},{6... | collective-permute-start | bytes 393224 | tf_op jit(solution)/shard_map/ppermute | solution.py:227
  56.2 5.8 %collective-permute-start.17 = (bf16[2,128,256]{2,1,0:T(8,128)(2,1)S(1)}, bf16[2,128,256]{2,1,0:T(8,128)(2,1)S(1)}, u32[]{:S(2)}, u32[]{:S(2)}) collective-permute-start(bf16[2,128,256]{2,1,0:T(8,128)(2,1)S(1)} %get-tuple-element.62), channel_id=1, source_target_pairs={{0,240},{8,248},{16,0},{24,8},{32,16},{40,24},{48,32},{56,40},{64,... | collective-permute-start | bytes 393224 | tf_op jit(solution)/shard_map/ppermute | solution.py:227
  62.1 4.3 %collective-permute-start.15 = (bf16[128,512]{1,0:T(8,128)(2,1)S(1)}, bf16[128,512]{1,0:T(8,128)(2,1)S(1)}, u32[]{:S(2)}, u32[]{:S(2)}) collective-permute-start(bf16[128,512]{1,0:T(8,128)(2,1)S(1)} %get-tuple-element.64), channel_id=1, source_target_pairs={{0,4},{1,5},{2,6},{3,7},{4,0},{5,1},{6,2},{7,3},{8,12},{9,13},{10,... | collective-permute-start | bytes 393224 | tf_op jit(solution)/shard_map/ppermute | solution.py:235
  66.5 2.1 %collective-permute-start.23 = (bf16[128,256]{1,0:T(8,128)(2,1)S(1)}, bf16[128,256]{1,0:T(8,128)(2,1)S(1)}, u32[]{:S(2)}, u32[]{:S(2)}) collective-permute-start(bf16[128,256]{1,0:T(8,128)(2,1)S(1)} %fusion.9), channel_id=1, source_target_pairs={{0,192},{8,200},{16,208},{24,216},{32,224},{40,232},{48,240},{56,2... | collective-permute-start | bytes 196616 | tf_op jit(solution)/shard_map/ppermute | solution.py:227
  68.6 4.1 %collective-permute-done.15 = bf16[128,512]{1,0:T(8,128)(2,1)S(1)} collective-permute-done((bf16[128,512]{1,0:T(8,128)(2,1)S(1)}, bf16[128,512]{1,0:T(8,128)(2,1)S(1)}, u32[]{:S(2)}, u32[]{:S(2)}) %collective-permute-start.15) | collective-permute-done | bytes 131104 | tf_op jit(solution)/shard_map/ppermute | solution.py:235
  (53 shorter events, 3.5 us)
Async XLA Ops:
  2.1 5.1 %collective-permute-start = (bf16[1,144,256]{2,1,0:T(8,128)(2,1)S(1)}, bf16[1,144,256]{2,1,0:T(8,128)(2,1)S(1)}, u32[]{:S(2)}, u32[]{:S(2)}) collective-permute-start(bf16[1,144,256]{2,1,0:T(8,128)(2,1)S(1)} %maximum_bitcast_fusion), channel_id=1, source_target_pairs={{0,64},{8,72},{16,80},{24,88},{32,96},{40,104},{48,112},{56,120},{... | collective-permute-start | bytes 221192 | tf_op jit(solution)/shard_map/ppermute | solution.py:227
  7.3 12.6 %collective-permute-start.2 = (bf16[2,144,256]{2,1,0:T(8,128)(2,1)S(1)}, bf16[2,144,256]{2,1,0:T(8,128)(2,1)S(1)}, u32[]{:S(2)}, u32[]{:S(2)}) collective-permute-start(bf16[2,144,256]{2,1,0:T(8,128)(2,1)S(1)} %pad_maximum_fusion.2), channel_id=1, source_target_pairs={{0,16},{8,24},{16,32},{24,40},{32,48},{40,56},{48,64},{56,72},{64,... | collective-permute-start | bytes 442376 | tf_op jit(solution)/shard_map/ppermute | solution.py:227
  8.9 12.8 %collective-permute-start.3 = (bf16[2,144,256]{2,1,0:T(8,128)(2,1)S(1)}, bf16[2,144,256]{2,1,0:T(8,128)(2,1)S(1)}, u32[]{:S(2)}, u32[]{:S(2)}) collective-permute-start(bf16[2,144,256]{2,1,0:T(8,128)(2,1)S(1)} %pad_maximum_fusion.2), channel_id=1, source_target_pairs={{0,32},{8,40},{16,48},{24,56},{32,64},{40,72},{48,80},{56,88},{64,... | collective-permute-start | bytes 442376 | tf_op jit(solution)/shard_map/ppermute | solution.py:227
  11.5 18.9 %collective-permute-start.1 = (bf16[1,144,256]{2,1,0:T(8,128)(2,1)S(1)}, bf16[1,144,256]{2,1,0:T(8,128)(2,1)S(1)}, u32[]{:S(2)}, u32[]{:S(2)}) collective-permute-start(bf16[1,144,256]{2,1,0:T(8,128)(2,1)S(1)} %maximum_bitcast_fusion), channel_id=1, source_target_pairs={{0,128},{8,136},{16,144},{24,152},{32,160},{40,168},{48,176},{56,1... | collective-permute-start | bytes 221192 | tf_op jit(solution)/shard_map/ppermute | solution.py:227
  13.0 17.5 %collective-permute-start.8 = (bf16[128,512]{1,0:T(8,128)(2,1)}, bf16[128,512]{1,0:T(8,128)(2,1)S(1)}, u32[]{:S(2)}, u32[]{:S(2)}) collective-permute-start(bf16[128,512]{1,0:T(8,128)(2,1)} %refs_5_.1), channel_id=1, source_target_pairs={{0,4},{1,5},{2,6},{3,7},{4,0},{5,1},{6,2},{7,3},{8,12},{9,13},{10,... | collective-permute-start | bytes 393224 | tf_op jit(solution)/shard_map/ppermute | solution.py:235
  19.9 10.6 %collective-permute-start.7 = (bf16[128,512]{1,0:T(8,128)(2,1)}, bf16[128,512]{1,0:T(8,128)(2,1)S(1)}, u32[]{:S(2)}, u32[]{:S(2)}) collective-permute-start(bf16[128,512]{1,0:T(8,128)(2,1)} %refs_5_.1), channel_id=1, source_target_pairs={{0,7},{1,0},{2,1},{3,2},{4,3},{5,4},{6,5},{7,6},{8,15},{9,8},{10,9... | collective-permute-start | bytes 393224 | tf_op jit(solution)/shard_map/ppermute | solution.py:235
  19.9 6.1 %collective-permute-start.4 = (bf16[2,144,256]{2,1,0:T(8,128)(2,1)S(1)}, bf16[2,144,256]{2,1,0:T(8,128)(2,1)S(1)}, u32[]{:S(2)}, u32[]{:S(2)}) collective-permute-start(bf16[2,144,256]{2,1,0:T(8,128)(2,1)S(1)} %pad_maximum_fusion.2), channel_id=1, source_target_pairs={{0,48},{8,56},{16,64},{24,72},{32,80},{40,88},{48,96},{56,104},{64... | collective-permute-start | bytes 442376 | tf_op jit(solution)/shard_map/ppermute | solution.py:227
  21.7 8.9 %collective-permute-start.10 = (bf16[128,512]{1,0:T(8,128)(2,1)}, bf16[128,512]{1,0:T(8,128)(2,1)S(1)}, u32[]{:S(2)}, u32[]{:S(2)}) collective-permute-start(bf16[128,512]{1,0:T(8,128)(2,1)} %refs_5_.1), channel_id=1, source_target_pairs={{0,1},{1,2},{2,3},{3,4},{4,5},{5,6},{6,7},{7,0},{8,9},{9,10},{10,1... | collective-permute-start | bytes 393224 | tf_op jit(solution)/shard_map/ppermute | solution.py:235
  26.1 7.5 %collective-permute-start.6 = (bf16[6,144,256]{2,1,0:T(8,128)(2,1)S(1)}, bf16[6,144,256]{2,1,0:T(8,128)(2,1)S(1)}, u32[]{:S(2)}, u32[]{:S(2)}) collective-permute-start(bf16[6,144,256]{2,1,0:T(8,128)(2,1)S(1)} %constant_dynamic-update-slice_fusion.2.refs_1_), channel_id=1, source_target_pairs={{0,8},{8,0},{16,24},{24,16},{32,40},{40,32},{48,56},{56,48},{64,72... | collective-permute-start | bytes 1327112 | tf_op jit(solution)/shard_map/ppermute | solution.py:231
  30.4 3.2 %collective-permute-start.5 = (bf16[3,144,256]{2,1,0:T(8,128)(2,1)S(1)}, bf16[3,144,256]{2,1,0:T(8,128)(2,1)S(1)}, u32[]{:S(2)}, u32[]{:S(2)}) collective-permute-start(bf16[3,144,256]{2,1,0:T(8,128)(2,1)S(1)} %constant_dynamic-update-slice_fusion.refs_0_), channel_id=1, source_target_pairs={{0,8},{8,0},{16,24},{24,16},{32,40},{40,32},{48,56},{56,48},{64,72... | collective-permute-start | bytes 663560 | tf_op jit(solution)/shard_map/ppermute | solution.py:231
  30.6 11.6 %collective-permute-start.11 = (bf16[256,512]{1,0:T(8,128)(2,1)S(1)}, bf16[256,512]{1,0:T(8,128)(2,1)S(1)}, u32[]{:S(2)}, u32[]{:S(2)}) collective-permute-start(bf16[256,512]{1,0:T(8,128)(2,1)S(1)} %get-tuple-element.66), channel_id=1, source_target_pairs={{0,1},{1,2},{2,3},{3,4},{4,5},{5,6},{6,7},{7,0},{8,9},{9,10},{10,1... | collective-permute-start | bytes 786440 | tf_op jit(solution)/shard_map/ppermute | solution.py:235
  32.3 9.9 %collective-permute-start.9 = (bf16[256,512]{1,0:T(8,128)(2,1)S(1)}, bf16[256,512]{1,0:T(8,128)(2,1)S(1)}, u32[]{:S(2)}, u32[]{:S(2)}) collective-permute-start(bf16[256,512]{1,0:T(8,128)(2,1)S(1)} %get-tuple-element.67), channel_id=1, source_target_pairs={{0,7},{1,0},{2,1},{3,2},{4,3},{5,4},{6,5},{7,6},{8,15},{9,8},{10,9... | collective-permute-start | bytes 786440 | tf_op jit(solution)/shard_map/ppermute | solution.py:235
  39.3 8.0 %collective-permute-start.12 = (bf16[2,128,512]{2,1,0:T(8,128)(2,1)S(1)}, bf16[2,128,512]{2,1,0:T(8,128)(2,1)S(1)}, u32[]{:S(2)}, u32[]{:S(2)}) collective-permute-start(bf16[2,128,512]{2,1,0:T(8,128)(2,1)S(1)} %get-tuple-element.45), channel_id=1, source_target_pairs={{0,1},{1,2},{2,3},{3,4},{4,5},{5,6},{6,7},{7,0},{8,9},{9,10},{10,1... | collective-permute-start | bytes 786440 | tf_op jit(solution)/shard_map/ppermute | solution.py:235
  39.8 7.5 %collective-permute-start.13 = (bf16[2,128,512]{2,1,0:T(8,128)(2,1)S(1)}, bf16[2,128,512]{2,1,0:T(8,128)(2,1)S(1)}, u32[]{:S(2)}, u32[]{:S(2)}) collective-permute-start(bf16[2,128,512]{2,1,0:T(8,128)(2,1)S(1)} %get-tuple-element.46), channel_id=1, source_target_pairs={{0,7},{1,0},{2,1},{3,2},{4,3},{5,4},{6,5},{7,6},{8,15},{9,8},{10,9... | collective-permute-start | bytes 786440 | tf_op jit(solution)/shard_map/ppermute | solution.py:235
  47.3 5.1 %collective-permute-start.21 = (bf16[3,128,256]{2,1,0:T(8,128)(2,1)S(1)}, bf16[3,128,256]{2,1,0:T(8,128)(2,1)S(1)}, u32[]{:S(2)}, u32[]{:S(2)}) collective-permute-start(bf16[3,128,256]{2,1,0:T(8,128)(2,1)S(1)} %get-tuple-element.56), channel_id=1, source_target_pairs={{0,8},{8,0},{16,24},{24,16},{32,40},{40,32},{48,56},{56,48},{64,72... | collective-permute-start | bytes 589832 | tf_op jit(solution)/shard_map/ppermute | solution.py:231
  49.5 3.0 %collective-permute-start.16 = (bf16[6,128,256]{2,1,0:T(8,128)(2,1)S(1)}, bf16[6,128,256]{2,1,0:T(8,128)(2,1)S(1)}, u32[]{:S(2)}, u32[]{:S(2)}) collective-permute-start(bf16[6,128,256]{2,1,0:T(8,128)(2,1)S(1)} %get-tuple-element.51), channel_id=1, source_target_pairs={{0,8},{8,0},{16,24},{24,16},{32,40},{40,32},{48,56},{56,48},{64,72... | collective-permute-start | bytes 1179656 | tf_op jit(solution)/shard_map/ppermute | solution.py:231
  49.6 18.9 %collective-permute-start.14 = (bf16[128,512]{1,0:T(8,128)(2,1)S(1)}, bf16[128,512]{1,0:T(8,128)(2,1)S(1)}, u32[]{:S(2)}, u32[]{:S(2)}) collective-permute-start(bf16[128,512]{1,0:T(8,128)(2,1)S(1)} %get-tuple-element.63), channel_id=1, source_target_pairs={{0,1},{1,2},{2,3},{3,4},{4,5},{5,6},{6,7},{7,0},{8,9},{9,10},{10,1... | collective-permute-start | bytes 393224 | tf_op jit(solution)/shard_map/ppermute | solution.py:235
  49.7 12.3 %collective-permute-start.20 = (bf16[128,512]{1,0:T(8,128)(2,1)S(1)}, bf16[128,512]{1,0:T(8,128)(2,1)S(1)}, u32[]{:S(2)}, u32[]{:S(2)}) collective-permute-start(bf16[128,512]{1,0:T(8,128)(2,1)S(1)} %get-tuple-element.65), channel_id=1, source_target_pairs={{0,7},{1,0},{2,1},{3,2},{4,3},{5,4},{6,5},{7,6},{8,15},{9,8},{10,9... | collective-permute-start | bytes 393224 | tf_op jit(solution)/shard_map/ppermute | solution.py:235
  52.7 13.7 %collective-permute-start.19 = (bf16[2,128,256]{2,1,0:T(8,128)(2,1)S(1)}, bf16[2,128,256]{2,1,0:T(8,128)(2,1)S(1)}, u32[]{:S(2)}, u32[]{:S(2)}) collective-permute-start(bf16[2,128,256]{2,1,0:T(8,128)(2,1)S(1)} %get-tuple-element.60), channel_id=1, source_target_pairs={{0,208},{8,216},{16,224},{24,232},{32,240},{40,248},{48,0},{56,8},... | collective-permute-start | bytes 393224 | tf_op jit(solution)/shard_map/ppermute | solution.py:227
  55.4 10.9 %collective-permute-start.18 = (bf16[2,128,256]{2,1,0:T(8,128)(2,1)S(1)}, bf16[2,128,256]{2,1,0:T(8,128)(2,1)S(1)}, u32[]{:S(2)}, u32[]{:S(2)}) collective-permute-start(bf16[2,128,256]{2,1,0:T(8,128)(2,1)S(1)} %get-tuple-element.61), channel_id=1, source_target_pairs={{0,224},{8,232},{16,240},{24,248},{32,0},{40,8},{48,16},{56,24},{6... | collective-permute-start | bytes 393224 | tf_op jit(solution)/shard_map/ppermute | solution.py:227
  56.2 10.2 %collective-permute-start.17 = (bf16[2,128,256]{2,1,0:T(8,128)(2,1)S(1)}, bf16[2,128,256]{2,1,0:T(8,128)(2,1)S(1)}, u32[]{:S(2)}, u32[]{:S(2)}) collective-permute-start(bf16[2,128,256]{2,1,0:T(8,128)(2,1)S(1)} %get-tuple-element.62), channel_id=1, source_target_pairs={{0,240},{8,248},{16,0},{24,8},{32,16},{40,24},{48,32},{56,40},{64,... | collective-permute-start | bytes 393224 | tf_op jit(solution)/shard_map/ppermute | solution.py:227
  62.1 10.6 %collective-permute-start.15 = (bf16[128,512]{1,0:T(8,128)(2,1)S(1)}, bf16[128,512]{1,0:T(8,128)(2,1)S(1)}, u32[]{:S(2)}, u32[]{:S(2)}) collective-permute-start(bf16[128,512]{1,0:T(8,128)(2,1)S(1)} %get-tuple-element.64), channel_id=1, source_target_pairs={{0,4},{1,5},{2,6},{3,7},{4,0},{5,1},{6,2},{7,3},{8,12},{9,13},{10,... | collective-permute-start | bytes 393224 | tf_op jit(solution)/shard_map/ppermute | solution.py:235
  66.4 7.0 %collective-permute-start.22 = (bf16[128,256]{1,0:T(8,128)(2,1)S(1)}, bf16[128,256]{1,0:T(8,128)(2,1)S(1)}, u32[]{:S(2)}, u32[]{:S(2)}) collective-permute-start(bf16[128,256]{1,0:T(8,128)(2,1)S(1)} %fusion.8), channel_id=1, source_target_pairs={{0,128},{8,136},{16,144},{24,152},{32,160},{40,168},{48,176},{56,1... | collective-permute-start | bytes 196616 | tf_op jit(solution)/shard_map/ppermute | solution.py:227
  66.5 6.9 %collective-permute-start.23 = (bf16[128,256]{1,0:T(8,128)(2,1)S(1)}, bf16[128,256]{1,0:T(8,128)(2,1)S(1)}, u32[]{:S(2)}, u32[]{:S(2)}) collective-permute-start(bf16[128,256]{1,0:T(8,128)(2,1)S(1)} %fusion.9), channel_id=1, source_target_pairs={{0,192},{8,200},{16,208},{24,216},{32,224},{40,232},{48,240},{56,2... | collective-permute-start | bytes 196616 | tf_op jit(solution)/shard_map/ppermute | solution.py:227
  (2 other events, 13.5 us)
